TPU v7x, 128 devices: a whole 4x4x4 slice. The times are simulated.
128 devices in a mesh: grp: 4 (over z), tp: 32 (over y, x, core).
Axes of the slice: x: 4, y: 4, z: 4, core: 2. Of those that a mesh axis runs over, the one named last changes fastest.
Arguments:
- residual: bfloat16 [1024, 7168], P(('grp', 'tp')), may hold values from -64 to 64
- queries: bfloat16 [1024, 73728], P(('grp', 'tp')), may hold values from -64 to 64
- fresh_latents: bfloat16 [1024, 576], P(('grp', 'tp')), may hold values from -8 to 8
- cache_pages: bfloat16 [8192, 36864], P(('grp', 'tp')), may hold values from -6 to 6
- prefill_pages: bfloat16 [2048, 36864], P(('grp', 'tp')), may hold values from -6 to 6
- prefill_owner: int32 [2048], P(('grp', 'tp')), may hold values from 0 to 3, as said below
- prefill_slot: int32 [2048], P(('grp', 'tp')), may hold values from 0 to 15, as said below
- page_lists: int32 [512, 40], P(('grp', 'tp')), may hold values from 0 to 79, as said below
- context_len: int32 [512], P(('grp', 'tp')), may hold values from 1 to 2560, as said below
- value_up: bfloat16 [128, 512, 128], P('tp'), may hold values from -0.25 to 0.25
- out_proj: bfloat16 [16384, 7168], P('tp'), may hold values from -0.1875 to 0.1875
- norm_gain: bfloat16 [7168], replicated, may hold values from 0.5 to 1.5
- gate_weight: bfloat16 [7168, 9216], P(None, 'tp'), may hold values from -0.0625 to 0.0625
- up_weight: bfloat16 [7168, 9216], P(None, 'tp'), may hold values from -0.0625 to 0.0625
- down_weight: bfloat16 [9216, 7168], P('tp'), may hold values from -0.0625 to 0.0625
Outputs:
- layer_out: bfloat16 [1024, 7168], P(('grp', 'tp'))
Inputs may be any that keep to these rules, and one draw needn't show every extreme that they name: `prefill_owner`: within one tp index, every device receives exactly 16 prefilled pages in all, and one device sends at most 8 pages to one owner. `prefill_slot`: the received places of one owner's pages are all different. `page_lists`: entries below 64 name resident pages, 64 + s the received page s. The first ceil(context_len / 64) entries of a row are used, distinct over one device's requests; every received page is used; other entries are 0. `context_len`: every request has at least one cached position.
All inputs are finite; a program needn't handle non-finite values.
Results may differ from a plain program's by a relative error of at most 0.019.
Values may be sent and summed in bfloat16 or wider, within the bound.
No kernel may reach another device: no remote copies, remote signals or barrier semaphores. Data moves between devices by JAX's collectives and lax.ppermute only.
A program may use at most 128 MiB of HBM per device.

v0:
```python
import jax
import jax.numpy as jnp
from jax import lax
from jax.sharding import PartitionSpec as P

HEADS = 128
LAT = 512
ROPE = 64
HEADV = 128
PAGE = 64
KVW = 576
MOST = 8


def rms_norm(hidden, norm_gain):
    values = hidden.astype(jnp.float32)
    spread = jnp.mean(values * values, -1, keepdims=True)
    return (values * lax.rsqrt(spread + 1e-06) * norm_gain.astype(jnp.float32)).astype(jnp.bfloat16)


def shards(
    residual,
    queries,
    fresh_latents,
    cache_pages,
    prefill_pages,
    prefill_owner,
    prefill_slot,
    page_lists,
    context_len,
    value_up,
    out_proj,
    norm_gain,
    gate_weight,
    up_weight,
    down_weight,
):
    groups = lax.axis_size("grp")
    incoming_count = prefill_pages.shape[0]
    page_width = prefill_pages.shape[1]
    labels = jnp.arange(groups, dtype=jnp.int32)
    matches = (prefill_owner[:, None] == labels[None, :]).astype(jnp.int32)
    order_in = jnp.sum((jnp.cumsum(matches, 0) - matches) * matches, 1)
    targets = prefill_owner * MOST + order_in
    outbox = (
        jnp.zeros((groups * MOST, page_width), prefill_pages.dtype).at[targets].set(prefill_pages)
    )
    out_slots = jnp.full((groups * MOST,), incoming_count, jnp.int32).at[targets].set(prefill_slot)
    inbox, in_slots = (
        lax.all_to_all(
            outbox.reshape(groups, MOST, page_width), "grp", split_axis=0, concat_axis=0, tiled=True
        ),
        lax.all_to_all(
            out_slots.reshape(groups, MOST), "grp", split_axis=0, concat_axis=0, tiled=True
        ),
    )
    arrived = inbox.reshape(groups * MOST, page_width)
    arrived_slot = in_slots.reshape(groups * MOST)
    received = (
        jnp.zeros((incoming_count + 1, page_width), prefill_pages.dtype)
        .at[arrived_slot]
        .set(arrived)[:incoming_count]
    )
    pool = jnp.concatenate([cache_pages, received], 0).reshape(-1, PAGE, KVW)
    requests = page_lists.shape[0]
    query_rows = queries.reshape(requests, 2, HEADS, KVW)
    fresh_keys = fresh_latents.reshape(requests, 2, KVW)
    cache_keys = pool[page_lists].reshape(requests, -1, KVW)
    scale = (HEADV + ROPE) ** (-0.5)
    cached = (
        jnp.einsum("rjhc,rkc->rjhk", query_rows, cache_keys, preferred_element_type=jnp.float32)
        * scale
    )
    visible = jnp.arange(cache_keys.shape[1], dtype=jnp.int32)[None, :] < context_len[:, None]
    cached = jnp.where(visible[:, None, None, :], cached, -jnp.inf)
    recent = (
        jnp.einsum("rjhc,rkc->rjhk", query_rows, fresh_keys, preferred_element_type=jnp.float32)
        * scale
    )
    causal = jnp.arange(2)[:, None] >= jnp.arange(2)[None, :]
    recent = jnp.where(causal[None, :, None, :], recent, -jnp.inf)
    peak = jnp.maximum(jnp.max(cached, -1), jnp.max(recent, -1))[..., None]
    cached_exp = jnp.exp(cached - peak)
    recent_exp = jnp.exp(recent - peak)
    denominator = jnp.sum(cached_exp, -1, keepdims=True) + jnp.sum(recent_exp, -1, keepdims=True)
    cached_prob = (cached_exp / denominator).astype(jnp.bfloat16)
    recent_prob = (recent_exp / denominator).astype(jnp.bfloat16)
    attended = jnp.einsum(
        "rjhk,rkl->rjhl", cached_prob, cache_keys[..., :LAT], preferred_element_type=jnp.float32
    )
    attended = attended + jnp.einsum(
        "rjhk,rkl->rjhl", recent_prob, fresh_keys[..., :LAT], preferred_element_type=jnp.float32
    )
    tok_rows = requests * 2
    attended = attended.astype(jnp.bfloat16).reshape(tok_rows, HEADS * LAT)
    by_heads = lax.all_to_all(attended, "tp", split_axis=1, concat_axis=0, tiled=True)
    heads_dev = value_up.shape[0]
    values = jnp.einsum(
        "thl,hlv->thv",
        by_heads.reshape(-1, heads_dev, LAT),
        value_up,
        preferred_element_type=jnp.float32,
    )
    values = values.astype(jnp.bfloat16).reshape(-1, heads_dev * HEADV)
    attn_out = lax.psum_scatter(
        jnp.dot(values, out_proj, preferred_element_type=jnp.float32).astype(jnp.bfloat16),
        "tp",
        scatter_dimension=0,
        tiled=True,
    ).astype(jnp.float32)
    hidden = (residual.astype(jnp.float32) + attn_out).astype(jnp.bfloat16)
    normed = rms_norm(hidden, norm_gain)
    piece = lax.all_gather(normed, "tp", axis=0, tiled=True)
    gate = jnp.dot(piece, gate_weight, preferred_element_type=jnp.float32)
    up_part = jnp.dot(piece, up_weight, preferred_element_type=jnp.float32)
    act = (jax.nn.silu(gate) * up_part).astype(jnp.bfloat16)
    mlp = lax.psum_scatter(
        jnp.dot(act, down_weight, preferred_element_type=jnp.float32).astype(jnp.bfloat16),
        "tp",
        scatter_dimension=0,
        tiled=True,
    ).astype(jnp.float32)
    return (hidden.astype(jnp.float32) + mlp).astype(jnp.bfloat16)


def solution(mesh):
    placed = (
        P(("grp", "tp"), None),
        P(("grp", "tp"), None),
        P(("grp", "tp"), None),
        P(("grp", "tp"), None),
        P(("grp", "tp"), None),
        P(("grp", "tp")),
        P(("grp", "tp")),
        P(("grp", "tp"), None),
        P(("grp", "tp")),
        P("tp", None, None),
        P("tp", None),
        P(),
        P(None, "tp"),
        P(None, "tp"),
        P("tp", None),
    )
    return jax.shard_map(
        shards, mesh=mesh, in_specs=placed, out_specs=P(("grp", "tp"), None), check_vma=False
    )
```

profile of v0, /device:TPU:6, one launch (start us, length us, event | category | flops | bytes accessed | tf_op | source)
XLA Modules:
  0.0 380.4 jit_solution(16876258312700664778)
XLA Ops:
  10.3 5.3 %all-to-all-start = ((s32[4,1,8]{2,1,0:T(1,128)}), s32[4,1,8]{2,1,0:T(1,128)S(1)}, u32[]{:S(2)}, u32[]{:S(2)}) async-start(s32[4,1,8]{2,1,0:T(1,128)} %bitcast), calls=%async_computation | async-start | bytes 4096 | tf_op jit(solution)/shard_map/all_to_all | solution.py:53
  15.6 4.6 %scatter_custom_fusion.1 = bf16[32,36864]{1,0:T(8,128)(2,1)} fusion(s32[16]{0:T(128)S(1)} %compare_select_fusion.2, bf16[16,36864]{1,0:T(8,128)(2,1)} %param.19, bf16[]{:T(256)} %constant.13.clone.1), kind=kCustom, calls=%fused_computation.24 | custom fusion | bytes 2359808 | tf_op jit(solution)/shard_map/scatter | solution.py:46
  20.8 4.2 %all-to-all-start.1 = ((bf16[4,8,36864]{2,1,0:T(8,128)(2,1)}), bf16[4,8,36864]{2,1,0:T(8,128)(2,1)S(1)}, u32[]{:S(2)}, u32[]{:S(2)}) async-start(bf16[4,8,36864]{2,1,0:T(8,128)(2,1)} %bitcast.2), calls=%async_computation.1 | async-start | bytes 4718592 | tf_op jit(solution)/shard_map/all_to_all | solution.py:50
  25.1 2.8 reshape.182
  28.0 3.5 reshape.121
  31.5 1.8 fusion.38
  34.6 18.9 %all-to-all-done.1 = bf16[4,8,36864]{2,1,0:T(8,128)(2,1)S(1)} async-done(((bf16[4,8,36864]{2,1,0:T(8,128)(2,1)}), bf16[4,8,36864]{2,1,0:T(8,128)(2,1)S(1)}, u32[]{:S(2)}, u32[]{:S(2)}) %all-to-all-start.1) | async-done | bytes 2359328 | tf_op jit(solution)/shard_map/all_to_all | solution.py:50
  53.6 4.9 %scatter_custom_fusion.2 = bf16[17,36864]{1,0:T(8,128)(2,1)} fusion(s32[32]{0:T(128)S(1)} %fusion.32, bf16[4,8,36864]{2,1,0:T(8,128)(2,1)S(1)} %all-to-all-done.1, bf16[]{:T(256)} %constant.13.clone.1), kind=kCustom, calls=%fused_computation.20 | custom fusion | bytes 3612674 | tf_op jit(solution)/shard_map/scatter | solution.py:62
  58.5 1.3 slice.14
  59.8 5.2 %pad_maximum_fusion = bf16[80,36864]{1,0:T(8,128)(2,1)} fusion(bf16[16,36864]{1,0:T(8,128)(2,1)S(1)} %slice.14, bf16[64,36864]{1,0:T(8,128)(2,1)} %param.18), kind=kLoop, calls=%fused_computation.14 | loop fusion | flops 11796480 | bytes 11796480 | tf_op jit(solution)/shard_map/concatenate | solution.py:64
  65.1 12.0 %reshape.119 = bf16[80,64,576]{2,1,0:T(8,128)(2,1)} reshape(bf16[80,36864]{1,0:T(8,128)(2,1)} %pad_maximum_fusion) | data formatting | bytes 11796480 | tf_op jit(solution)/shard_map/reshape | solution.py:64
  77.1 11.4 %gather_fusion = bf16[160,64,576]{2,1,0:T(8,128)(2,1)} fusion(bf16[80,64,576]{2,1,0:T(8,128)(2,1)} %reshape.119, s32[1024]{0:T(1024)S(1)} %pad_clamp_fusion), kind=kCustom, calls=%fused_computation | custom fusion | bytes 23593600 | tf_op jit(solution)/shard_map/gather | solution.py:68
  88.5 13.2 %bitcast_reduce_fusion = (f32[4,2,128]{2,1,0:T(2,128)S(1)}, f32[4,2560,2,128]{3,1,2,0:T(8,128)}) fusion(pred[4,2560]{1,0:T(4,128)(4,1)S(1)} %iota_compare_fusion, bf16[4,2560,576,1]{2,1,3,0:T(8,128)(2,1)} %bitcast.58, bf16[4,2,128,576]{3,2,1,0:T(8,128)(2,1)S(1)} %copy-done.1), kind=kOutput, calls=%fused_computation.7 | convolution fusion | flops 3027762176 | bytes 23476224 | tf_op jit(solution)/shard_map/rjhc,rkc->rjhk/dot_general | solution.py:71
  101.7 6.9 %fusion.2 = f32[4,2,128]{2,1,0:T(2,128)S(1)} fusion(f32[4,2560,2,128]{3,1,2,0:T(8,128)} %get-tuple-element.6, f32[4,2,128]{2,1,0:T(2,128)S(1)} %max.7, pred[4,2560]{1,0:T(4,128)(4,1)S(1)} %iota_compare_fusion), kind=kLoop, calls=%fused_computation.13 | loop fusion | flops 10484736 | bytes 10504192 | tf_op jit(solution)/shard_map/reduce_sum | solution.py:85
  109.3 7.7 %add_convert_fusion = bf16[4,2,128,512]{3,2,1,0:T(8,128)(2,1)S(1)} fusion(f32[4,2,128,512]{3,2,1,0:T(8,128)S(1)} %fusion.27, bf16[4,2560,576]{2,1,0:T(8,128)(2,1)S(1)} %bitcast.61, f32[4,2560,2,128]{3,1,2,0:T(8,128)} %get-tuple-element.6, f32[4,2,128]{2,1,0:T(2,128)S(1)} %add.65, f32[4,2,128]{2,1,0:T(2,128)S(1)} %max.7, ...), kind=kOutput, calls=%fused_computation.22 | convolution fusion | flops 2698510336 | bytes 24135680 | tf_op jit(solution)/shard_map/rjhk,rkl->rjhl/dot_general | solution.py:88
  118.2 21.9 %all_to_all.30 = bf16[8,32,2048]{2,0,1:T(8,128)(2,1)S(1)} all-to-all(bf16[8,32,2048]{2,0,1:T(8,128)(2,1)S(1)} %copy.33), channel_id=1, replica_groups=mesh['grp'=4,'tp'=32] {'tp'}, dimensions={1} | all-to-all | bytes 2097152 | tf_op jit(solution)/shard_map/all_to_all | solution.py:96
  141.5 7.0 %convolution_convert_fusion.1 = bf16[256,7168]{1,0:T(8,128)(2,1)} fusion(bf16[256,512]{0,1:T(8,128)(2,1)S(1)} %bitcast.63, bf16[512,7168]{1,0:T(8,128)(2,1)} %param.25), kind=kOutput, calls=%fused_computation.12 | convolution fusion | flops 1880883200 | bytes 11272192 | tf_op jit(solution)/shard_map/dot_general | solution.py:106
  148.6 79.0 %reduce-scatter.3.cloned.1.call-done = bf16[8,7168]{1,0:T(8,128)(2,1)} async-done(((bf16[256,7168]{1,0:T(8,128)(2,1)}), bf16[8,7168]{1,0:T(8,128)(2,1)}) %reduce-scatter.3.cloned.1.call-update) | async-done | bytes 114704 | tf_op jit(solution)/shard_map/reduce_scatter | solution.py:105
  228.7 1.6 fusion.23
  230.6 44.6 %all-gather.2.cloned.1.call-done = bf16[256,7168]{1,0:T(8,128)(2,1)} async-done(((bf16[8,7168]{1,0:T(8,128)(2,1)}), bf16[256,7168]{1,0:T(8,128)(2,1)}) %all-gather.2.cloned.1.call-update) | async-done | bytes 3670032 | tf_op jit(solution)/shard_map/all_gather | solution.py:113
  275.2 4.6 %fusion.39 = f32[256,288]{0,1:T(8,128)S(1)} fusion(bf16[256,7168]{1,0:T(8,128)(2,1)} %all-gather.2.cloned.1.call-done, bf16[7168,288]{0,1:T(8,128)(2,1)} %param.27), kind=kOutput, calls=%fused_computation.71 | convolution fusion | flops 1056964608 | bytes 8093696 | tf_op jit(solution)/shard_map/dot_general | solution.py:114
  279.8 11.8 %convolution_convert_fusion = bf16[256,7168]{1,0:T(8,128)(2,1)} fusion(bf16[288,7168]{1,0:T(8,128)(2,1)} %param.29, bf16[256,7168]{1,0:T(8,128)(2,1)} %all-gather.2.cloned.1.call-done, bf16[7168,288]{0,1:T(8,128)(2,1)} %param.28, f32[256,288]{0,1:T(8,128)S(1)} %fusion.39), kind=kOutput, calls=%fused_computation.11 | convolution fusion | flops 2116206592 | bytes 15892480 | tf_op jit(solution)/shard_map/dot_general | solution.py:118
  291.6 80.7 %reduce-scatter.5.cloned.1.call-done = bf16[8,7168]{1,0:T(8,128)(2,1)} async-done(((bf16[256,7168]{1,0:T(8,128)(2,1)}), bf16[8,7168]{1,0:T(8,128)(2,1)}) %reduce-scatter.5.cloned.1.call-update) | async-done | bytes 114704 | tf_op jit(solution)/shard_map/reduce_scatter | solution.py:117
  372.3 1.6 fusion.24
  (60 shorter events, 10.3 us)
Async XLA Ops:
  6.5 134.4 %copy-start = (bf16[4,512,128]{2,1,0:T(8,128)(2,1)S(1)}, bf16[4,512,128]{2,1,0:T(8,128)(2,1)}, u32[]{:S(2)}) copy-start(bf16[4,512,128]{2,1,0:T(8,128)(2,1)} %param.24) | copy-start | bytes 1572868
  6.5 18.5 %copy-start.4 = (bf16[8,576]{1,0:T(8,128)(2,1)S(1)}, bf16[8,576]{1,0:T(8,128)(2,1)}, u32[]{:S(2)}) copy-start(bf16[8,576]{1,0:T(8,128)(2,1)} %param.17) | copy-start | bytes 27652
  6.5 18.5 %copy-start.6 = (s32[4,40]{1,0:T(4,128)S(1)}, s32[4,40]{1,0:T(4,128)}, u32[]{:S(2)}) copy-start(s32[4,40]{1,0:T(4,128)} %param.22) | copy-start | bytes 1924
  10.3 10.5 %all-to-all-start = ((s32[4,1,8]{2,1,0:T(1,128)}), s32[4,1,8]{2,1,0:T(1,128)S(1)}, u32[]{:S(2)}, u32[]{:S(2)}) async-start(s32[4,1,8]{2,1,0:T(1,128)} %bitcast), calls=%async_computation | async-start | bytes 4096 | tf_op jit(solution)/shard_map/all_to_all | solution.py:53
  20.8 32.8 %all-to-all-start.1 = ((bf16[4,8,36864]{2,1,0:T(8,128)(2,1)}), bf16[4,8,36864]{2,1,0:T(8,128)(2,1)S(1)}, u32[]{:S(2)}, u32[]{:S(2)}) async-start(bf16[4,8,36864]{2,1,0:T(8,128)(2,1)} %bitcast.2), calls=%async_computation.1 | async-start | bytes 4718592 | tf_op jit(solution)/shard_map/all_to_all | solution.py:50
  25.0 8.3 %copy-start.7 = (s32[4]{0:T(128)S(1)}, s32[4]{0:T(128)}, u32[]{:S(2)}) copy-start(s32[4]{0:T(128)} %param.23) | copy-start | bytes 52
  25.0 202.6 %reduce-scatter.3.cloned.1.call-start = ((), (), s32[]{:S(2)}) async-start(), calls=%async_computation.5 | async-start | bytes 3784704 | tf_op jit(solution)/shard_map/reduce_scatter | solution.py:105
  77.1 11.4 %copy-start.1 = (bf16[4,2,128,576]{3,2,1,0:T(8,128)(2,1)S(1)}, bf16[4,2,128,576]{3,2,1,0:T(8,128)(2,1)}, u32[]{:S(2)}) copy-start(bf16[4,2,128,576]{3,2,1,0:T(8,128)(2,1)} %reshape.121) | copy-start | bytes 3538948
  88.5 20.7 %slice-start = ((s8[13107200]{0:T(1024)(128)(4,1)}), s8[4194304]{0:T(1024)(128)(4,1)S(1)}, s32[]{:S(2)}) async-start(s8[13107200]{0:T(1024)(128)(4,1)} %bitcast.59), calls=%async_computation.8 | async-start | bytes 8388608
  88.5 20.7 %slice-start.1 = ((s8[13107200]{0:T(1024)(128)(4,1)}), s8[4194304]{0:T(1024)(128)(4,1)S(1)}, s32[]{:S(2)}) async-start(s8[13107200]{0:T(1024)(128)(4,1)} %bitcast.59), calls=%async_computation.9 | async-start | bytes 8388608
  88.5 20.7 %slice-start.2 = ((s8[13107200]{0:T(1024)(128)(4,1)}), s8[4194304]{0:T(1024)(128)(4,1)S(1)}, s32[]{:S(2)}) async-start(s8[13107200]{0:T(1024)(128)(4,1)} %bitcast.59), calls=%async_computation.10 | async-start | bytes 8388608
  101.7 7.5 %slice-start.3 = ((s8[13107200]{0:T(1024)(128)(4,1)}), s8[524288]{0:T(1024)(128)(4,1)S(1)}, s32[]{:S(2)}) async-start(s8[13107200]{0:T(1024)(128)(4,1)} %bitcast.59), calls=%async_computation.11 | async-start | bytes 1048576
  141.4 7.1 %copy-start.5 = (bf16[7168]{0:T(1024)(128)(2,1)S(1)}, bf16[7168]{0:T(1024)(128)(2,1)}, u32[]{:S(2)}) copy-start(bf16[7168]{0:T(1024)(128)(2,1)} %param.26) | copy-start | bytes 43012
  141.5 86.1 %copy-start.2 = (bf16[8,7168]{1,0:T(8,128)(2,1)S(1)}, bf16[8,7168]{1,0:T(8,128)(2,1)}, u32[]{:S(2)}) copy-start(bf16[8,7168]{1,0:T(8,128)(2,1)} %param.15) | copy-start | bytes 344068
  148.5 126.7 %all-gather.2.cloned.1.call-start = ((), (), s32[]{:S(2)}) async-start(), calls=%async_computation.6 | async-start | bytes 3784704 | tf_op jit(solution)/shard_map/all_gather | solution.py:113
  230.3 141.9 %reduce-scatter.5.cloned.1.call-start = ((), (), s32[]{:S(2)}) async-start(), calls=%async_computation.7 | async-start | bytes 3784704 | tf_op jit(solution)/shard_map/reduce_scatter | solution.py:117
  279.8 92.5 %copy-start.3 = (bf16[8,7168]{1,0:T(8,128)(2,1)S(1)}, bf16[8,7168]{1,0:T(8,128)(2,1)}, u32[]{:S(2)}) copy-start(bf16[8,7168]{1,0:T(8,128)(2,1)} %reduce-scatter.3.cloned.1.call-done) | copy-start | bytes 344068
Sparse Core Ops, SparseCore 0:
  148.6 78.9 reduce-scatter.2
  230.5 44.7 all-gather.1
  291.7 80.4 reduce-scatter.4
where the time goes:
time: 382 us; the launch traced here: 380 us
  waiting for transfers between devices  224 us (59%)
  matrix products  47 us (12%)
  local copies, waits for them, and re-layouts  44.8 us (12%)
  blocking collectives  21.9 us (6%)
  other arithmetic  19.6 us (5%)
  between operations  13.3 us (3%)
  starting transfers between devices  9.84 us (3%)
    reduce_scatter x1, waiting for transfers between devices, shards(): lax.psum_scatter(jnp.dot(act, down_weight, preferred_element_type=jnp.flo...  80.7 us
    reduce_scatter x1, waiting for transfers between devices, shards(): lax.psum_scatter(jnp.dot(values, out_proj, preferred_element_type=jnp.flo...  79 us
    all_gather x1, waiting for transfers between devices, shards(): piece = lax.all_gather(normed, 'tp', axis=0, tiled=True)  44.6 us
    all_to_all x1, blocking collectives, shards(): lax.all_to_all(attended, 'tp', split_axis=1, concat_axis=0, tiled=True)  21.9 us
    all_to_all x1, waiting for transfers between devices, shards(): lax.all_to_all(outbox.reshape(groups, MOST, page_width), 'grp', split_axi...  18.9 us
    dot_general x1, matrix products, shards(): jnp.einsum('rjhc,rkc->rjhk', query_rows, cache_keys, preferred_element_ty...  13.2 us
    reshape x1, local copies, waits for them, and re-layouts, shards(): pool = jnp.concatenate([cache_pages, received], 0).reshape(-1, PAGE, KVW)  12 us
    dot_general x1, matrix products, shards(): jnp.dot(act, down_weight, preferred_element_type=jnp.float32)  11.8 us
  transfers between devices with their start and end apart: 5, of which 5 were waited for; matrix products, arithmetic and copies ran while one was open for 4% of the time, Pallas kernels for 0%

commit v1 on v0

v1 whole, which is shorter than its diff:
```python
import math

import jax
import jax.numpy as jnp
from jax import lax
from jax.experimental import pallas as pl
from jax.experimental.pallas import tpu as pltpu
from jax.sharding import PartitionSpec as P

HEADS = 128
LAT = 512
ROPE = 64
HEADV = 128
PAGE = 64
KVW = 576
MOST = 8
PAGE_WIDTH = PAGE * KVW
PAIR = 2 * KVW
RES_BLOCKS = 11
UNROLL = 16
PRODUCT_WIDTH = 512
HIDDEN_WIDTH = 1792
REC_BLOCKS = 5
RES_SPARE = (RES_BLOCKS + 1) * 8
REC_SPARE = (REC_BLOCKS + 1) * 8
KEYS = 8 * PAGE
LOW = -1e30
EXPONENT = (HEADV + ROPE) ** (-0.5) * math.log2(math.e)
ROWS = 2 * HEADS
NT = (((1,), (1,)), ((), ()))
MIB = 1024 * 1024


def rms_norm(hidden, norm_gain):
    values = hidden.astype(jnp.float32)
    spread = jnp.mean(values * values, -1, keepdims=True)
    return (values * lax.rsqrt(spread + 1e-06) * norm_gain.astype(jnp.float32)).astype(jnp.bfloat16)


def chip_pairs(step0, step1):
    pairs = []
    for y in range(4):
        for x in range(4):
            for core, (dy, dx, flip) in enumerate((step0, step1)):
                there = (((y + dy) % 4) * 4 + (x + dx) % 4) * 2 + (core ^ flip)
                pairs.append(((y * 4 + x) * 2 + core, there))
    return pairs


def swap_cores(block):
    return lax.ppermute(block, "tp", chip_pairs((0, 0, 1), (0, 0, 1)))


def along_first(block, k):
    return lax.ppermute(block, "tp", chip_pairs((0, k, 0), (k, 0, 0)))


def along_second(block, k):
    return lax.ppermute(block, "tp", chip_pairs((k, 0, 0), (0, k, 0)))


def token_order():
    t = lax.axis_index("tp")
    y, x, core = t // 8, (t // 2) % 4, t % 2
    row = jnp.arange(256, dtype=jnp.int32)
    owner_core = jnp.where(row // 128 == 0, core, 1 - core)
    k1, k2, i = (row // 32) % 4, (row // 8) % 4, row % 8
    dy = jnp.where(owner_core == 0, k2, k1)
    dx = jnp.where(owner_core == 0, k1, k2)
    return ((((y + dy) % 4) * 4 + (x + dx) % 4) * 2 + owner_core) * 8 + i


def add_up(own, others):
    total = own.astype(jnp.float32)
    for other in others:
        total = total + other.astype(jnp.float32)
    return total


def reduce_rows(mine, theirs):
    got = {k: swap_cores(theirs[k]) for k in (1, 3, 2, 0)}
    chunks = {k: add_up(mine[k], [got[k]]) for k in (1, 3, 2, 0)}
    arrived = [along_first(chunks[k].astype(jnp.bfloat16), k) for k in (1, 3, 2)]
    chunks = add_up(chunks[0], arrived).reshape(4, 8, -1)
    arrived = [along_second(chunks[k].astype(jnp.bfloat16), k) for k in (1, 3, 2)]
    return add_up(chunks[0], arrived)


def gather_rows(block):
    arrived = {k: along_second(block, 4 - k) for k in (1, 3, 2)}
    rows = jnp.concatenate([block] + [arrived[k] for k in (1, 2, 3)], 0)
    arrived = {k: along_first(rows, 4 - k) for k in (1, 3, 2)}
    mine = [rows] + [arrived[k] for k in (1, 2, 3)]
    return mine + [swap_cores(part) for part in mine]


def iota(shape, dim):
    return lax.broadcasted_iota(jnp.int32, shape, dim)


def outbox_kernel(route, pages, out1, out2, out3):
    outs = (out1, out2, out3)
    rows, cols = iota((32, 128), 0), iota((32, 128), 1)
    pick = jnp.zeros((32, 128), jnp.float32)
    slots = jnp.full((32, 128), 64, jnp.int32)
    counts = [jnp.int32(0)] * 4
    for i in range(16):
        step = route[i] >> 4
        rank = jnp.int32(0)
        for k in range(1, 4):
            rank = jnp.where(step == k, counts[k], rank)
            counts[k] = counts[k] + jnp.where(step == k, 1, 0)
        target = jnp.where(step == 0, -1, (step - 1) * MOST + rank)
        pick = jnp.where((rows == target) & (cols == i), 1.0, pick)
        slots = jnp.where(rows == target, route[i] & 15, slots)
    pick = pick[:, :16].astype(jnp.bfloat16)
    slots = slots.astype(jnp.float32).astype(jnp.bfloat16)

    def chunk(n, _):
        for u in range(UNROLL):
            lanes = pl.ds(pl.multiple_of((n * UNROLL + u) * PAIR, 128), PAIR)
            got = jnp.dot(pick, pages[:, lanes], preferred_element_type=jnp.float32)
            for k in range(3):
                outs[k][:, lanes] = got[k * 8 : k * 8 + 8].astype(jnp.bfloat16)
        return 0

    lax.fori_loop(0, PAGE // 2 // UNROLL, chunk, 0)
    for k in range(3):
        outs[k][:, PAGE_WIDTH:] = slots[k * 8 : k * 8 + 8]


def outbox(route, pages):
    smem, vmem = pl.BlockSpec(memory_space=pltpu.SMEM), pl.BlockSpec(memory_space=pltpu.VMEM)
    return pl.pallas_call(
        outbox_kernel,
        out_shape=[jax.ShapeDtypeStruct((MOST, PAGE_WIDTH + 128), jnp.bfloat16)] * 3,
        in_specs=[smem, vmem],
        out_specs=[vmem] * 3,
        compiler_params=pltpu.CompilerParams(vmem_limit_bytes=16 * MIB),
        name="outbox",
    )(route, pages)


def lay_keys(pick, source, keys, blocks):
    def chunk(n, _):
        for u in range(UNROLL):
            at = n * UNROLL + u
            lanes = pl.ds(pl.multiple_of(at * PAIR, 128), PAIR)
            got = jnp.dot(pick, source(lanes), preferred_element_type=jnp.float32)
            even = got[: blocks * 8, :KVW].reshape(blocks, 8, KVW)
            odd = got[: blocks * 8, KVW:].reshape(blocks, 8, KVW)
            both = jnp.concatenate([even, odd], 1).astype(jnp.bfloat16)
            keys[:, pl.ds(pl.multiple_of(at * 16, 16), 16), :] = both
        return 0

    lax.fori_loop(0, PAGE // 2 // UNROLL, chunk, 0)


def key_limit(first, valid):
    at = iota((8, KEYS), 1)
    limit = jnp.zeros((8, KEYS), jnp.int32)
    for i in range(8):
        limit = jnp.where((at & 7) == i, valid[first + i], limit)
    return ((at >> 3) < limit)[:1]


def absorb(scores, live, value_rows, peak, total, acc, r):
    scores = jnp.where(live, scores * EXPONENT, LOW)
    before = peak[r]
    top = jnp.maximum(before, jnp.max(scores, -1, keepdims=True))
    weight = jnp.exp2(scores - top[:, :1])
    fade = jnp.exp2(before - top)
    peak[r] = top
    total[r] = total[r] * fade + jnp.sum(weight, -1, keepdims=True)
    acc[r] = acc[r] * fade[:, :1] + jnp.dot(
        weight.astype(jnp.bfloat16), value_rows, preferred_element_type=jnp.float32
    )


def absorb_blocks(blocks, first, valid, query_rows, keys, peak, total, acc, even, odd):
    def request_of(b):
        r = jnp.int32(0)
        for n in range(1, 4):
            r = r + jnp.where(b >= first[n], 1, 0)
        return r

    def scores_of(b):
        return lax.dot_general(
            query_rows[request_of(b)], keys[jnp.minimum(b, blocks - 1)], NT, preferred_element_type=jnp.float32
        )

    def take(b, scores):
        value_rows = keys[jnp.minimum(b, blocks - 1), :, :LAT]
        absorb(scores[...], key_limit(b * 8, valid), value_rows, peak, total, acc, request_of(b))

    even[...] = scores_of(0)

    def step(n, _):
        odd[...] = scores_of(2 * n + 1)
        take(2 * n, even)
        even[...] = scores_of(2 * n + 2)
        take(2 * n + 1, odd)
        return 0

    lax.fori_loop(0, (first[4] + 1) // 2, step, 0)


def resident_kernel(
    lists, lengths, queries, fresh, cache,
    query_rows, peak, total, acc, slot_row, rec_valid, rec_first,
    keys, even, odd, head_rows, res_page, res_valid, res_first,
):
    for i in range(RES_BLOCKS * 8):
        res_page[i] = 0
    for i in range(RES_SPARE):
        res_valid[i] = 0
    for i in range(REC_SPARE):
        rec_valid[i] = 0
    for i in range(17):
        slot_row[i] = 0
    res_at, rec_at = jnp.int32(0), jnp.int32(0)
    for r in range(4):
        res_first[r] = res_at // 8
        rec_first[r] = rec_at // 8
        length = lengths[r]

        def page(p, carry):
            res_at, rec_at = carry
            entry = lists[r, p]
            live = jnp.minimum(length - p * PAGE, PAGE)
            resident = entry < 64
            at = jnp.where(resident, res_at, RES_SPARE)
            res_page[at] = entry
            res_valid[at] = live
            at = jnp.where(resident, REC_SPARE, rec_at)
            rec_valid[at] = live
            slot_row[jnp.where(resident, 16, entry - 64)] = rec_at
            one = jnp.where(resident, 1, 0)
            return res_at + one, rec_at + 1 - one

        res_at, rec_at = lax.fori_loop(0, (length + PAGE - 1) // PAGE, page, (res_at, rec_at))
        res_at = (res_at + 7) // 8 * 8
        rec_at = (rec_at + 7) // 8 * 8
    res_first[4] = res_at // 8
    rec_first[4] = rec_at // 8

    to, of = iota((128, 128), 0), iota((128, 128), 1)
    wanted = ((to >> 1) & 15) * 8 + (to >> 5) * 2 + (to & 1)
    order = (wanted == of).astype(jnp.float32).astype(jnp.bfloat16)
    for g in range(HEADS // 16):
        for n in range(8):
            two = queries[:, (g * 8 + n) * PAIR : (g * 8 + n + 1) * PAIR].astype(jnp.float32)
            head_rows[pl.ds(n * 16, 16), :] = jnp.concatenate(
                [two[:, :KVW], two[:, KVW:]], 0
            ).astype(jnp.bfloat16)
        placed = jnp.dot(order, head_rows[...], preferred_element_type=jnp.float32).astype(jnp.bfloat16)
        for r in range(4):
            query_rows[r, g * 32 : g * 32 + 32, :] = placed[r * 32 : r * 32 + 32]

    new_keys = jnp.concatenate([fresh[...].astype(jnp.float32), jnp.zeros((120, KVW), jnp.float32)], 0).astype(jnp.bfloat16)
    for r in range(4):
        scores = lax.dot_general(query_rows[r], new_keys, NT, preferred_element_type=jnp.float32) * EXPONENT
        column, j = iota((ROWS, 128), 1), iota((ROWS, 128), 0) & 1
        seen = (column == 2 * r) | ((column == 2 * r + 1) & (j == 1))
        scores = jnp.where(seen, scores, LOW)
        top = jnp.max(scores, -1, keepdims=True)
        weight = jnp.exp2(scores - top)
        peak[r] = jnp.broadcast_to(top, (ROWS, 128))
        total[r] = jnp.broadcast_to(jnp.sum(weight, -1, keepdims=True), (ROWS, 128))
        acc[r] = jnp.dot(weight.astype(jnp.bfloat16), new_keys[:, :LAT], preferred_element_type=jnp.float32)

    pick = []
    sub, lane = iota((8, 64), 0), iota((8, 64), 1)
    for b in range(RES_BLOCKS):
        source = jnp.zeros((8, 64), jnp.int32)
        for i in range(8):
            source = jnp.where(sub == i, res_page[b * 8 + i], source)
        pick.append((source == lane).astype(jnp.float32))
    pick.append(jnp.zeros((8, 64), jnp.float32))
    pick = jnp.concatenate(pick, 0).astype(jnp.bfloat16)
    lay_keys(pick, lambda lanes: cache[:, lanes], keys, RES_BLOCKS)

    absorb_blocks(RES_BLOCKS, res_first, res_valid, query_rows, keys, peak, total, acc, even, odd)


def attend_resident(lists, lengths, queries, fresh, cache):
    smem, vmem = pl.BlockSpec(memory_space=pltpu.SMEM), pl.BlockSpec(memory_space=pltpu.VMEM)
    shapes = [
        jax.ShapeDtypeStruct((4, ROWS, KVW), jnp.bfloat16),
        jax.ShapeDtypeStruct((4, ROWS, 128), jnp.float32),
        jax.ShapeDtypeStruct((4, ROWS, 128), jnp.float32),
        jax.ShapeDtypeStruct((4, ROWS, LAT), jnp.float32),
        jax.ShapeDtypeStruct((24,), jnp.int32),
        jax.ShapeDtypeStruct((REC_SPARE + 8,), jnp.int32),
        jax.ShapeDtypeStruct((8,), jnp.int32),
    ]
    return pl.pallas_call(
        resident_kernel,
        out_shape=shapes,
        in_specs=[smem, smem, vmem, vmem, vmem],
        out_specs=[vmem] * 4 + [smem] * 3,
        scratch_shapes=[
            pltpu.VMEM((RES_BLOCKS, KEYS, KVW), jnp.bfloat16),
            pltpu.VMEM((ROWS, KEYS), jnp.float32),
            pltpu.VMEM((ROWS, KEYS), jnp.float32),
            pltpu.VMEM((128, KVW), jnp.bfloat16),
            pltpu.SMEM((RES_SPARE + 8,), jnp.int32),
            pltpu.SMEM((RES_SPARE + 8,), jnp.int32),
            pltpu.SMEM((8,), jnp.int32),
        ],
        compiler_params=pltpu.CompilerParams(vmem_limit_bytes=20 * MIB),
        cost_estimate=pl.CostEstimate(flops=8_000_000_000, bytes_accessed=12_000_000, transcendentals=2_000_000),
        name="attend_resident",
    )(lists, lengths, queries, fresh, cache)


def received_kernel(
    route, slot_row, rec_valid, rec_first,
    box1, box2, box3, own, query_rows, peak_in, total_in, acc_in,
    out, keys, even, odd, peak, total, acc,
):
    peak[...] = peak_in[...]
    total[...] = total_in[...]
    acc[...] = acc_in[...]
    boxes = (box1, box2, box3)
    cols = iota((24, 128), 1)
    slots = jnp.concatenate([box[:, PAGE_WIDTH:].astype(jnp.float32) for box in boxes], 0)
    arrived = jnp.zeros((24, 128), jnp.float32)
    for n in range(16):
        arrived = jnp.where((slots == float(n)) & (cols == slot_row[n]), 1.0, arrived)
    rows, cols = iota((16, 128), 0), iota((16, 128), 1)
    kept = jnp.zeros((16, 128), jnp.float32)
    for i in range(16):
        target = jnp.where(route[i] >> 4 == 0, slot_row[route[i] & 15], -1)
        kept = jnp.where((rows == i) & (cols == target), 1.0, kept)
    place_of = jnp.concatenate([arrived, kept, jnp.zeros((88, 128), jnp.float32)], 0)
    pick = place_of.T[:48, :48].astype(jnp.bfloat16)

    def source(lanes):
        parts = [box[:, lanes].astype(jnp.float32) for box in boxes]
        parts.append(own[:, lanes].astype(jnp.float32))
        parts.append(jnp.zeros((8, PAIR), jnp.float32))
        return jnp.concatenate(parts, 0).astype(jnp.bfloat16)

    lay_keys(pick, source, keys, REC_BLOCKS)

    absorb_blocks(REC_BLOCKS, rec_first, rec_valid, query_rows, keys, peak, total, acc, even, odd)
    for t in range(0, 32, 8):
        parts = []
        for r in range(4):
            part = acc[r, t * 8 : t * 8 + 64] * (1.0 / total[r, t * 8 : t * 8 + 64, :1])
            parts.append(part.reshape(8, 8, LAT))
        out[t : t + 8] = jnp.concatenate(parts, 1).astype(jnp.bfloat16)


def attend_received(route, plan, boxes, own, state):
    smem, vmem = pl.BlockSpec(memory_space=pltpu.SMEM), pl.BlockSpec(memory_space=pltpu.VMEM)
    return pl.pallas_call(
        received_kernel,
        out_shape=jax.ShapeDtypeStruct((32, 32, LAT), jnp.bfloat16),
        in_specs=[smem] * 4 + [vmem] * 8,
        out_specs=vmem,
        scratch_shapes=[
            pltpu.VMEM((REC_BLOCKS, KEYS, KVW), jnp.bfloat16),
            pltpu.VMEM((ROWS, KEYS), jnp.float32),
            pltpu.VMEM((ROWS, KEYS), jnp.float32),
            pltpu.VMEM((4, ROWS, 128), jnp.float32),
            pltpu.VMEM((4, ROWS, 128), jnp.float32),
            pltpu.VMEM((4, ROWS, LAT), jnp.float32),
        ],
        compiler_params=pltpu.CompilerParams(vmem_limit_bytes=20 * MIB),
        name="attend_received",
    )(route, *plan, *boxes, own, *state)


def product(rows, weight, store):
    width = PRODUCT_WIDTH

    def part(n, _):
        lanes = pl.ds(pl.multiple_of(n * width, 128), width)
        store(lanes, jnp.dot(rows, weight[:, lanes], preferred_element_type=jnp.float32))
        return 0

    lax.fori_loop(0, weight.shape[1] // width, part, 0, unroll=True)


def store_blocks(outs):
    def store(lanes, got):
        for k, out in enumerate(outs):
            out[:, lanes] = got[k * 32 : k * 32 + 32].astype(jnp.bfloat16)

    return store


def values_kernel(order, rows, value_up, out_proj, values_out, *theirs):
    wide = jnp.concatenate([value_up[h] for h in range(4)], 1)
    all_heads = jnp.dot(rows[...], wide, preferred_element_type=jnp.float32)
    at, column = iota((1024, 512), 0), iota((1024, 512), 1)
    own_head = ((at >> 1) & 3) == (column >> 7)
    values = jnp.where(own_head, all_heads, 0.0).astype(jnp.bfloat16)
    n = iota((256, 1024), 1)
    token = (n >> 5) * 8 + ((n >> 3) & 3) * 2 + (n & 1)
    pick = (order[...] == token).astype(jnp.float32).astype(jnp.bfloat16)
    values = jnp.dot(pick, values, preferred_element_type=jnp.float32).astype(jnp.bfloat16)
    values_out[...] = values[:128]
    product(values[128:], out_proj, store_blocks(theirs))


def project_values(order, rows, value_up, out_proj):
    vmem = pl.BlockSpec(memory_space=pltpu.VMEM)
    width = out_proj.shape[1]
    return pl.pallas_call(
        values_kernel,
        out_shape=[jax.ShapeDtypeStruct((128, 512), jnp.bfloat16)]
        + [jax.ShapeDtypeStruct((32, width), jnp.bfloat16)] * 4,
        in_specs=[vmem] * 4,
        out_specs=[vmem] * 5,
        compiler_params=pltpu.CompilerParams(vmem_limit_bytes=20 * MIB),
        cost_estimate=pl.CostEstimate(flops=2_500_000_000, bytes_accessed=12_000_000, transcendentals=0),
        name="values",
    )(order, rows, value_up, out_proj)


def project_kernel(rows, weight, *outs):
    def store(lanes, got):
        for k, out in enumerate(outs):
            out[:, lanes] = got[k * 32 : k * 32 + 32]

    product(rows[...], weight, store)


def project(rows, weight):
    vmem = pl.BlockSpec(memory_space=pltpu.VMEM)
    width = weight.shape[1]
    return pl.pallas_call(
        project_kernel,
        out_shape=[jax.ShapeDtypeStruct((32, width), jnp.float32)] * 4,
        in_specs=[vmem] * 2,
        out_specs=[vmem] * 4,
        compiler_params=pltpu.CompilerParams(vmem_limit_bytes=16 * MIB),
        cost_estimate=pl.CostEstimate(flops=1_000_000_000, bytes_accessed=11_000_000, transcendentals=0),
        name="project",
    )(rows, weight)


def hidden_kernel(*refs):
    rows, (gate_weight, up_weight, down_weight, act_out), theirs = refs[:8], refs[8:12], refs[12:16]
    gate, up_part = refs[16:]
    width = HIDDEN_WIDTH
    for n in range(rows[0].shape[1] // width):
        lanes = slice(n * width, n * width + width)
        block = jnp.concatenate([row[:, lanes] for row in rows], 0)
        for total, weight in ((gate, gate_weight), (up_part, up_weight)):
            got = lax.dot_general(weight[:, lanes], block, NT, preferred_element_type=jnp.float32)
            total[...] = got if n == 0 else total[...] + got
    g = gate[...]
    act = (g / (1.0 + jnp.exp(-g)) * up_part[...]).T.astype(jnp.bfloat16)
    act_out[...] = act[:128]
    product(act[128:], down_weight, store_blocks(theirs))


def hidden_units(rows, gate_weight, up_weight, down_weight):
    vmem = pl.BlockSpec(memory_space=pltpu.VMEM)
    units, width = down_weight.shape
    return pl.pallas_call(
        hidden_kernel,
        out_shape=[jax.ShapeDtypeStruct((128, units), jnp.bfloat16)]
        + [jax.ShapeDtypeStruct((32, width), jnp.bfloat16)] * 4,
        in_specs=[vmem] * 11,
        out_specs=[vmem] * 5,
        scratch_shapes=[pltpu.VMEM((units, 256), jnp.float32)] * 2,
        compiler_params=pltpu.CompilerParams(vmem_limit_bytes=20 * MIB),
        cost_estimate=pl.CostEstimate(flops=3_000_000_000, bytes_accessed=18_000_000, transcendentals=80_000),
        name="hidden_units",
    )(*rows, gate_weight.T, up_weight.T, down_weight)


def shards(
    residual,
    queries,
    fresh_latents,
    cache_pages,
    prefill_pages,
    prefill_owner,
    prefill_slot,
    page_lists,
    context_len,
    value_up,
    out_proj,
    norm_gain,
    gate_weight,
    up_weight,
    down_weight,
):
    route = ((prefill_owner - lax.axis_index("grp")) & 3) * 16 + prefill_slot
    boxes = outbox(route, prefill_pages)
    boxes = [
        lax.ppermute(box, "grp", [(g, (g + k) % 4) for g in range(4)])
        for k, box in enumerate(boxes, 1)
    ]
    *state, slot_row, rec_valid, rec_first = attend_resident(
        page_lists, context_len, queries, fresh_latents, cache_pages
    )
    attended = attend_received(
        route, (slot_row, rec_valid, rec_first), boxes, prefill_pages, state
    )
    by_heads = lax.all_to_all(attended, "tp", split_axis=0, concat_axis=0, tiled=True)
    values, *theirs = project_values(token_order()[:, None], by_heads.reshape(1024, LAT), value_up, out_proj)
    attn_out = reduce_rows(project(values, out_proj), theirs)
    hidden = (residual.astype(jnp.float32) + attn_out).astype(jnp.bfloat16)
    normed = rms_norm(hidden, norm_gain)
    act, *theirs = hidden_units(gather_rows(normed), gate_weight, up_weight, down_weight)
    mlp = reduce_rows(project(act, down_weight), theirs)
    return (hidden.astype(jnp.float32) + mlp).astype(jnp.bfloat16)


def solution(mesh):
    placed = (
        P(("grp", "tp"), None),
        P(("grp", "tp"), None),
        P(("grp", "tp"), None),
        P(("grp", "tp"), None),
        P(("grp", "tp"), None),
        P(("grp", "tp")),
        P(("grp", "tp")),
        P(("grp", "tp"), None),
        P(("grp", "tp")),
        P("tp", None, None),
        P("tp", None),
        P(),
        P(None, "tp"),
        P(None, "tp"),
        P("tp", None),
    )
    return jax.shard_map(
        shards, mesh=mesh, in_specs=placed, out_specs=P(("grp", "tp"), None), check_vma=False
    )
```

time: 382 us -> 159 us (0.42)
  waiting for transfers between devices: 224 us -> 82.6 us
  matrix products: 47 us -> 0 us
  local copies, waits for them, and re-layouts: 44.8 us -> 10.1 us
  starting transfers between devices: 9.84 us -> 38.4 us
  Pallas kernels: 0 us -> 24.5 us
  blocking collectives: 21.9 us -> 0 us
  other arithmetic: 19.6 us -> 2.98 us
  between operations: 13.3 us -> 0.26 us
    reduce_scatter x2 -> x0, waiting for transfers between devices: 160 us -> none  [the longest x1 80.7 us: shards(): lax.psum_scatter(jnp.dot(act, down_weight, preferred_element_type=jnp.flo...]
    ppermute x0 -> x33, waiting for transfers between devices: none -> 68.1 us  [the longest x9 37.1 us: along_first(): return lax.ppermute(block, 'tp', chip_pairs((0, k, 0), (k, 0, 0)))]
    dot_general x8 -> x0, matrix products: 47 us -> none  [the longest x1 13.2 us: shards(): jnp.einsum('rjhc,rkc->rjhk', query_rows, cache_keys, preferred_element_ty...]
    all_gather x1 -> x0, waiting for transfers between devices: 44.6 us -> none  [shards(): piece = lax.all_gather(normed, 'tp', axis=0, tiled=True)]
    ppermute x0 -> x33, starting transfers between devices: none -> 30.3 us  [the longest x9 11.4 us: along_first(): return lax.ppermute(block, 'tp', chip_pairs((0, k, 0), (k, 0, 0)))]
    pallas_call x0 -> x7, Pallas kernels: none -> 24.5 us  [the longest x1 9.28 us: attend_resident(): pl.pallas_call(resident_kernel, out_shape=shapes, in_specs=[smem, smem, v...]
    all_to_all x1 -> x0, blocking collectives: 21.9 us -> none  [shards(): lax.all_to_all(attended, 'tp', split_axis=1, concat_axis=0, tiled=True)]
    reshape x6 -> x0, local copies, waits for them, and re-layouts: 16.4 us -> none  [the longest x1 12 us: shards(): pool = jnp.concatenate([cache_pages, received], 0).reshape(-1, PAGE, KVW)]
  transfers between devices with their start and end apart: 5 -> 34, of which waited for: 5 -> 20; matrix products, arithmetic and copies ran while one was open for 4% -> 0% of each run, Pallas kernels for 0% -> 7%
where the time goes in v1:
time: 159 us
  waiting for transfers between devices  82.6 us (52%)
  starting transfers between devices  38.4 us (24%)
  Pallas kernels  24.5 us (15%)
  local copies, waits for them, and re-layouts  10.1 us (6%)
  other arithmetic  2.98 us (2%)
    ppermute x9, waiting for transfers between devices, along_first(): return lax.ppermute(block, 'tp', chip_pairs((0, k, 0), (k, 0, 0)))  37.1 us
    ppermute x9, waiting for transfers between devices, along_second(): return lax.ppermute(block, 'tp', chip_pairs((k, 0, 0), (0, k, 0)))  19 us
    all_to_all x1, waiting for transfers between devices, shards(): lax.all_to_all(attended, 'tp', split_axis=0, concat_axis=0, tiled=True)  14.4 us
    ppermute x9, starting transfers between devices, along_first(): return lax.ppermute(block, 'tp', chip_pairs((0, k, 0), (k, 0, 0)))  11.4 us
    unnamed x30, local copies, waits for them, and re-layouts  10 us
    ppermute x3, waiting for transfers between devices, shards(): lax.ppermute(box, 'grp', [(g, (g + k) % 4) for g in range(4)])  9.83 us
    pallas_call x1, Pallas kernels, attend_resident(): pl.pallas_call(resident_kernel, out_shape=shapes, in_specs=[smem, smem, v...  9.28 us
    ppermute x9, starting transfers between devices, along_second(): return lax.ppermute(block, 'tp', chip_pairs((k, 0, 0), (0, k, 0)))  8.71 us
  transfers between devices with their start and end apart: 34, of which 20 were waited for; matrix products, arithmetic and copies ran while one was open for 0% of the time, Pallas kernels for 7%

profile of v1, /device:TPU:6, one launch (start us, length us, event | category | flops | bytes accessed | tf_op | source)
XLA Modules:
  0.0 158.8 jit_solution(14071884751578393354)
XLA Ops:
  5.5 3.6 %collective-permute-start.1 = (bf16[8,36992]{1,0:T(8,128)(2,1)S(1)}, bf16[8,36992]{1,0:T(8,128)(2,1)S(1)}, u32[]{:S(2)}, u32[]{:S(2)}) collective-permute-start(bf16[8,36992]{1,0:T(8,128)(2,1)S(1)} %get-tuple-element.37), channel_id=1, source_target_pairs={{0,64},{32,96},{64,0},{96,32},{1,65},{33,97},{65,1},{97,33},{2,66}... | collective-permute-start | bytes 1775624 | tf_op jit(solution)/shard_map/ppermute | solution.py:498
  10.1 2.3 %copy-done.7 = bf16[64,36864]{1,0:T(8,128)(2,1)S(1)} copy-done((bf16[64,36864]{1,0:T(8,128)(2,1)S(1)}, bf16[64,36864]{1,0:T(8,128)(2,1)}, u32[]{:S(2)}) %copy-start.7) | copy-done | bytes 4718616
  15.7 9.3 %attend_resident.1 = (bf16[4,256,576]{2,1,0:T(8,128)(2,1)S(1)}, f32[4,256,128]{2,1,0:T(8,128)S(1)}, f32[4,256,128]{2,1,0:T(8,128)S(1)}, f32[4,256,512]{2,1,0:T(8...) custom-call(s32[4,40]{1,0:T(4,128)S(1)} %copy-done.11, s32[4]{0:T(128)S(1)} %copy-done.12, ...), custom_call_target="tpu_custom_call" | custom-call | flops 8000000000 | bytes 12000000 | tf_op jit(solution)/shard_map/attend_resident/pallas_call | solution.py:297
  25.0 9.8 %collective-permute-done.1.box2 = bf16[8,36992]{1,0:T(8,128)(2,1)S(1)} collective-permute-done((bf16[8,36992]{1,0:T(8,128)(2,1)S(1)}, bf16[8,36992]{1,0:T(8,128)(2,1)S(1)}, u32[]{:S(2)}, u32[]{:S(2)}) %collective-permute-start.1) | collective-permute-done | bytes 591904 | tf_op jit(solution)/shard_map/ppermute | solution.py:498
  34.8 5.9 %attend_received.1 = bf16[32,32,512]{2,1,0:T(8,128)(2,1)} custom-call(s32[16]{0:T(128)S(1)} %multiply_add_fusion.route, s32[24]{0:T(128)S(1)} %get-tuple-element.33.slot_row, s32[56]{0:T(128)S(1)} %get-tuple-element.34.rec_valid, s32[8]{0:T(128)S(1)} %get-tuple-element.35.rec_first, bf16[8,36992]{1,0:T(8,128)(2,1)S(1)} %collective-permute-done.box1, ...), custom_call_target="tpu_custom_call" | custom-call | tf_op jit(solution)/shard_map/attend_received/pallas_call | solution.py:358
  40.7 8.1 %all-to-all-start = ((bf16[32,32,512]{2,1,0:T(8,128)(2,1)}), bf16[32,32,512]{2,1,0:T(8,128)(2,1)S(1)}, u32[]{:S(2)}, u32[]{:S(2)}) async-start(bf16[32,32,512]{2,1,0:T(8,128)(2,1)} %attend_received.1), calls=%async_computation | async-start | bytes 2097152 | tf_op jit(solution)/shard_map/all_to_all | solution.py:507
  49.1 14.4 %all-to-all-done = bf16[32,32,512]{2,1,0:T(8,128)(2,1)S(1)} async-done(((bf16[32,32,512]{2,1,0:T(8,128)(2,1)}), bf16[32,32,512]{2,1,0:T(8,128)(2,1)S(1)}, u32[]{:S(2)}, u32[]{:S(2)}) %all-to-all-start) | async-done | bytes 1048608 | tf_op jit(solution)/shard_map/all_to_all | solution.py:507
  63.5 3.1 %copy-done.1 = bf16[512,7168]{1,0:T(8,128)(2,1)S(1)} copy-done((bf16[512,7168]{1,0:T(8,128)(2,1)S(1)}, bf16[512,7168]{1,0:T(8,128)(2,1)}, u32[]{:S(2)}) %copy-start.1) | copy-done | bytes 7340056
  66.6 2.1 %values.1 = (bf16[128,512]{1,0:T(8,128)(2,1)S(1)}, bf16[32,7168]{1,0:T(8,128)(2,1)S(1)}, bf16[32,7168]{1,0:T(8,128)(2,1)S(1)}, bf16[32,7168]{1,0:T(8,128)(2,1)S(1)}, bf16[32,7168]{1,0:T(8,128)(2,1)S(1)}) custom-call(s32[256,1]{1,0:T(8,128)S(1)} %fusion.15.order, bf16[1024,512]{1,0:T(8,128)(2,1)S(1)} %bitcast.5, bf16[4,512,128]{2,1,0:T(8,128)(2,1)S(1)} %copy-done.9, ...), custom_call_target="tpu_custom_call" | custom-call | flops 2500000000 | bytes 12000000 | tf_op jit(solution)/shard_map/values/pallas_call | solution.py:412
  76.4 8.5 %collective-permute-done.5 = bf16[32,7168]{1,0:T(8,128)(2,1)S(1)} collective-permute-done((bf16[32,7168]{1,0:T(8,128)(2,1)S(1)}, bf16[32,7168]{1,0:T(8,128)(2,1)S(1)}, u32[]{:S(2)}, u32[]{:S(2)}) %collective-permute-start.5) | collective-permute-done | bytes 458784 | tf_op jit(solution)/shard_map/ppermute | solution.py:55
  84.9 3.8 %collective-permute-done.7 = bf16[32,7168]{1,0:T(8,128)(2,1)S(1)} collective-permute-done((bf16[32,7168]{1,0:T(8,128)(2,1)S(1)}, bf16[32,7168]{1,0:T(8,128)(2,1)S(1)}, u32[]{:S(2)}, u32[]{:S(2)}) %collective-permute-start.7) | collective-permute-done | bytes 458784 | tf_op jit(solution)/shard_map/ppermute | solution.py:55
  89.2 3.2 %collective-permute-start.11 = (bf16[8,7168]{1,0:T(8,128)(2,1)S(1)}, bf16[8,7168]{1,0:T(8,128)(2,1)S(1)}, u32[]{:S(2)}, u32[]{:S(2)}) collective-permute-start(bf16[8,7168]{1,0:T(8,128)(2,1)S(1)} %get-tuple-element.72), channel_id=1, source_target_pairs={{0,24},{1,7},{2,26},{3,1},{4,28},{5,3},{6,30},{7,5},{8,0},{9,15},{... | collective-permute-start | bytes 344072 | tf_op jit(solution)/shard_map/ppermute | solution.py:59
  92.4 2.8 %collective-permute-done.10 = bf16[8,7168]{1,0:T(8,128)(2,1)S(1)} collective-permute-done((bf16[8,7168]{1,0:T(8,128)(2,1)S(1)}, bf16[8,7168]{1,0:T(8,128)(2,1)S(1)}, u32[]{:S(2)}, u32[]{:S(2)}) %collective-permute-start.10) | collective-permute-done | bytes 114720 | tf_op jit(solution)/shard_map/ppermute | solution.py:59
  96.0 2.7 %collective-permute-done.12 = bf16[8,7168]{1,0:T(8,128)(2,1)S(1)} collective-permute-done((bf16[8,7168]{1,0:T(8,128)(2,1)S(1)}, bf16[8,7168]{1,0:T(8,128)(2,1)S(1)}, u32[]{:S(2)}, u32[]{:S(2)}) %collective-permute-start.12) | collective-permute-done | bytes 114720 | tf_op jit(solution)/shard_map/ppermute | solution.py:59
  101.1 2.8 %collective-permute-done.13 = bf16[8,7168]{1,0:T(8,128)(2,1)S(1)} collective-permute-done((bf16[8,7168]{1,0:T(8,128)(2,1)S(1)}, bf16[8,7168]{1,0:T(8,128)(2,1)S(1)}, u32[]{:S(2)}, u32[]{:S(2)}) %collective-permute-start.13) | collective-permute-done | bytes 114720 | tf_op jit(solution)/shard_map/ppermute | solution.py:59
  103.9 2.5 %collective-permute-done.14 = bf16[8,7168]{1,0:T(8,128)(2,1)S(1)} collective-permute-done((bf16[8,7168]{1,0:T(8,128)(2,1)S(1)}, bf16[8,7168]{1,0:T(8,128)(2,1)S(1)}, u32[]{:S(2)}, u32[]{:S(2)}) %collective-permute-start.14) | collective-permute-done | bytes 114720 | tf_op jit(solution)/shard_map/ppermute | solution.py:59
  110.9 11.4 %collective-permute-done.16.refs_1_ = bf16[32,7168]{1,0:T(8,128)(2,1)S(1)} collective-permute-done((bf16[32,7168]{1,0:T(8,128)(2,1)S(1)}, bf16[32,7168]{1,0:T(8,128)(2,1)S(1)}, u32[]{:S(2)}, u32[]{:S(2)}) %collective-permute-start.16) | collective-permute-done | bytes 458784 | tf_op jit(solution)/shard_map/ppermute | solution.py:55
  125.4 3.5 %hidden_units.1 = (bf16[128,288]{1,0:T(8,128)(2,1)S(1)}, bf16[32,7168]{1,0:T(8,128)(2,1)S(1)}, bf16[32,7168]{1,0:T(8,128)(2,1)S(1)}, bf16[32,7168]{1,0:T(8,128)(2,1)S(1)}, bf16[32,7168]{1,0:T(8,128)(2,1)S(1)}) custom-call(bf16[32,7168]{1,0:T(8,128)(2,1)S(1)} %pad_maximum_fusion.refs_0_, bf16[32,7168]{1,0:T(8,128)(2,1)S(1)} %collective-permute-done.16.refs_1_, ...), custom_call_target="tpu_custom_call" | custom-call | flops 3000000000 | bytes 18000000 | tf_op jit(solution)/shard_map/hidden_units/pallas_call | solution.py:465
  131.2 2.2 %collective-permute-start.25 = (bf16[32,7168]{1,0:T(8,128)(2,1)S(1)}, bf16[32,7168]{1,0:T(8,128)(2,1)S(1)}, u32[]{:S(2)}, u32[]{:S(2)}) collective-permute-start(bf16[32,7168]{1,0:T(8,128)(2,1)S(1)} %add_convert_fusion.2), channel_id=1, source_target_pairs={{0,2},{1,9},{2,4},{3,11},{4,6},{5,13},{6,0},{7,15},{8,10},{9,17},{... | collective-permute-start | bytes 1376264 | tf_op jit(solution)/shard_map/ppermute | solution.py:55
  135.2 9.1 %collective-permute-done.25 = bf16[32,7168]{1,0:T(8,128)(2,1)S(1)} collective-permute-done((bf16[32,7168]{1,0:T(8,128)(2,1)S(1)}, bf16[32,7168]{1,0:T(8,128)(2,1)S(1)}, u32[]{:S(2)}, u32[]{:S(2)}) %collective-permute-start.25) | collective-permute-done | bytes 458784 | tf_op jit(solution)/shard_map/ppermute | solution.py:55
  144.3 3.8 %collective-permute-done.27 = bf16[32,7168]{1,0:T(8,128)(2,1)S(1)} collective-permute-done((bf16[32,7168]{1,0:T(8,128)(2,1)S(1)}, bf16[32,7168]{1,0:T(8,128)(2,1)S(1)}, u32[]{:S(2)}, u32[]{:S(2)}) %collective-permute-start.27) | collective-permute-done | bytes 458784 | tf_op jit(solution)/shard_map/ppermute | solution.py:55
  149.6 2.2 %collective-permute-start.31 = (bf16[8,7168]{1,0:T(8,128)(2,1)S(1)}, bf16[8,7168]{1,0:T(8,128)(2,1)S(1)}, u32[]{:S(2)}, u32[]{:S(2)}) collective-permute-start(bf16[8,7168]{1,0:T(8,128)(2,1)S(1)} %get-tuple-element.69), channel_id=1, source_target_pairs={{0,24},{1,7},{2,26},{3,1},{4,28},{5,3},{6,30},{7,5},{8,0},{9,15},{... | collective-permute-start | bytes 344072 | tf_op jit(solution)/shard_map/ppermute | solution.py:59
  151.8 2.8 %collective-permute-done.30 = bf16[8,7168]{1,0:T(8,128)(2,1)S(1)} collective-permute-done((bf16[8,7168]{1,0:T(8,128)(2,1)S(1)}, bf16[8,7168]{1,0:T(8,128)(2,1)S(1)}, u32[]{:S(2)}, u32[]{:S(2)}) %collective-permute-start.30) | collective-permute-done | bytes 114720 | tf_op jit(solution)/shard_map/ppermute | solution.py:59
  155.4 2.7 %collective-permute-done.32 = bf16[8,7168]{1,0:T(8,128)(2,1)S(1)} collective-permute-done((bf16[8,7168]{1,0:T(8,128)(2,1)S(1)}, bf16[8,7168]{1,0:T(8,128)(2,1)S(1)}, u32[]{:S(2)}, u32[]{:S(2)}) %collective-permute-start.32) | collective-permute-done | bytes 114720 | tf_op jit(solution)/shard_map/ppermute | solution.py:59
  (99 shorter events, 35.9 us)
Async XLA Ops:
  3.5 21.5 %collective-permute-start = (bf16[8,36992]{1,0:T(8,128)(2,1)S(1)}, bf16[8,36992]{1,0:T(8,128)(2,1)S(1)}, u32[]{:S(2)}, u32[]{:S(2)}) collective-permute-start(bf16[8,36992]{1,0:T(8,128)(2,1)S(1)} %get-tuple-element.36), channel_id=1, source_target_pairs={{0,32},{32,64},{64,96},{96,0},{1,33},{33,65},{65,97},{97,1},{2,34}... | collective-permute-start | bytes 1775624 | tf_op jit(solution)/shard_map/ppermute | solution.py:498
  5.5 29.3 %collective-permute-start.1 = (bf16[8,36992]{1,0:T(8,128)(2,1)S(1)}, bf16[8,36992]{1,0:T(8,128)(2,1)S(1)}, u32[]{:S(2)}, u32[]{:S(2)}) collective-permute-start(bf16[8,36992]{1,0:T(8,128)(2,1)S(1)} %get-tuple-element.37), channel_id=1, source_target_pairs={{0,64},{32,96},{64,0},{96,32},{1,65},{33,97},{65,1},{97,33},{2,66}... | collective-permute-start | bytes 1775624 | tf_op jit(solution)/shard_map/ppermute | solution.py:498
  9.1 25.8 %collective-permute-start.2 = (bf16[8,36992]{1,0:T(8,128)(2,1)S(1)}, bf16[8,36992]{1,0:T(8,128)(2,1)S(1)}, u32[]{:S(2)}, u32[]{:S(2)}) collective-permute-start(bf16[8,36992]{1,0:T(8,128)(2,1)S(1)} %get-tuple-element.38), channel_id=1, source_target_pairs={{0,96},{32,0},{64,32},{96,64},{1,97},{33,1},{65,33},{97,65},{2,98}... | collective-permute-start | bytes 1775624 | tf_op jit(solution)/shard_map/ppermute | solution.py:498
  40.7 22.7 %all-to-all-start = ((bf16[32,32,512]{2,1,0:T(8,128)(2,1)}), bf16[32,32,512]{2,1,0:T(8,128)(2,1)S(1)}, u32[]{:S(2)}, u32[]{:S(2)}) async-start(bf16[32,32,512]{2,1,0:T(8,128)(2,1)} %attend_received.1), calls=%async_computation | async-start | bytes 2097152 | tf_op jit(solution)/shard_map/all_to_all | solution.py:507
  70.6 5.8 %collective-permute-start.3 = (bf16[32,7168]{1,0:T(8,128)(2,1)S(1)}, bf16[32,7168]{1,0:T(8,128)(2,1)S(1)}, u32[]{:S(2)}, u32[]{:S(2)}) collective-permute-start(bf16[32,7168]{1,0:T(8,128)(2,1)S(1)} %get-tuple-element.45), channel_id=1, source_target_pairs={{0,1},{1,0},{2,3},{3,2},{4,5},{5,4},{6,7},{7,6},{8,9},{9,8},{10,11... | collective-permute-start | bytes 1376264 | tf_op jit(solution)/shard_map/ppermute | solution.py:51
  72.0 13.0 %collective-permute-start.5 = (bf16[32,7168]{1,0:T(8,128)(2,1)S(1)}, bf16[32,7168]{1,0:T(8,128)(2,1)S(1)}, u32[]{:S(2)}, u32[]{:S(2)}) collective-permute-start(bf16[32,7168]{1,0:T(8,128)(2,1)S(1)} %add_convert_fusion.5), channel_id=1, source_target_pairs={{0,2},{1,9},{2,4},{3,11},{4,6},{5,13},{6,0},{7,15},{8,10},{9,17},{... | collective-permute-start | bytes 1376264 | tf_op jit(solution)/shard_map/ppermute | solution.py:55
  74.1 14.7 %collective-permute-start.7 = (bf16[32,7168]{1,0:T(8,128)(2,1)S(1)}, bf16[32,7168]{1,0:T(8,128)(2,1)S(1)}, u32[]{:S(2)}, u32[]{:S(2)}) collective-permute-start(bf16[32,7168]{1,0:T(8,128)(2,1)S(1)} %add_convert_fusion.4), channel_id=1, source_target_pairs={{0,6},{1,25},{2,0},{3,27},{4,2},{5,29},{6,4},{7,31},{8,14},{9,1},{... | collective-permute-start | bytes 1376264 | tf_op jit(solution)/shard_map/ppermute | solution.py:55
  74.3 14.4 %collective-permute-start.9 = (bf16[32,7168]{1,0:T(8,128)(2,1)S(1)}, bf16[32,7168]{1,0:T(8,128)(2,1)S(1)}, u32[]{:S(2)}, u32[]{:S(2)}) collective-permute-start(bf16[32,7168]{1,0:T(8,128)(2,1)S(1)} %add_convert_fusion.3), channel_id=1, source_target_pairs={{0,4},{1,17},{2,6},{3,19},{4,0},{5,21},{6,2},{7,23},{8,12},{9,25},... | collective-permute-start | bytes 1376264 | tf_op jit(solution)/shard_map/ppermute | solution.py:55
  89.1 6.1 %collective-permute-start.10 = (bf16[8,7168]{1,0:T(8,128)(2,1)S(1)}, bf16[8,7168]{1,0:T(8,128)(2,1)S(1)}, u32[]{:S(2)}, u32[]{:S(2)}) collective-permute-start(bf16[8,7168]{1,0:T(8,128)(2,1)S(1)} %get-tuple-element.70), channel_id=1, source_target_pairs={{0,8},{1,3},{2,10},{3,5},{4,12},{5,7},{6,14},{7,1},{8,16},{9,11},{... | collective-permute-start | bytes 344072 | tf_op jit(solution)/shard_map/ppermute | solution.py:59
  89.2 6.8 %collective-permute-start.11 = (bf16[8,7168]{1,0:T(8,128)(2,1)S(1)}, bf16[8,7168]{1,0:T(8,128)(2,1)S(1)}, u32[]{:S(2)}, u32[]{:S(2)}) collective-permute-start(bf16[8,7168]{1,0:T(8,128)(2,1)S(1)} %get-tuple-element.72), channel_id=1, source_target_pairs={{0,24},{1,7},{2,26},{3,1},{4,28},{5,3},{6,30},{7,5},{8,0},{9,15},{... | collective-permute-start | bytes 344072 | tf_op jit(solution)/shard_map/ppermute | solution.py:59
  92.4 6.3 %collective-permute-start.12 = (bf16[8,7168]{1,0:T(8,128)(2,1)S(1)}, bf16[8,7168]{1,0:T(8,128)(2,1)S(1)}, u32[]{:S(2)}, u32[]{:S(2)}) collective-permute-start(bf16[8,7168]{1,0:T(8,128)(2,1)S(1)} %get-tuple-element.71), channel_id=1, source_target_pairs={{0,16},{1,5},{2,18},{3,7},{4,20},{5,1},{6,22},{7,3},{8,24},{9,13},... | collective-permute-start | bytes 344072 | tf_op jit(solution)/shard_map/ppermute | solution.py:59
  100.0 6.4 %collective-permute-start.14 = (bf16[8,7168]{1,0:T(8,128)(2,1)S(1)}, bf16[8,7168]{1,0:T(8,128)(2,1)S(1)}, u32[]{:S(2)}, u32[]{:S(2)}) collective-permute-start(bf16[8,7168]{1,0:T(8,128)(2,1)S(1)} %fusion.2), channel_id=1, source_target_pairs={{0,16},{1,5},{2,18},{3,7},{4,20},{5,1},{6,22},{7,3},{8,24},{9,13},... | collective-permute-start | bytes 344072 | tf_op jit(solution)/shard_map/ppermute | solution.py:59
  100.0 7.5 %collective-permute-start.15 = (bf16[8,7168]{1,0:T(8,128)(2,1)S(1)}, bf16[8,7168]{1,0:T(8,128)(2,1)S(1)}, u32[]{:S(2)}, u32[]{:S(2)}) collective-permute-start(bf16[8,7168]{1,0:T(8,128)(2,1)S(1)} %fusion.2), channel_id=1, source_target_pairs={{0,8},{1,3},{2,10},{3,5},{4,12},{5,7},{6,14},{7,1},{8,16},{9,11},{... | collective-permute-start | bytes 344072 | tf_op jit(solution)/shard_map/ppermute | solution.py:59
  107.6 14.7 %collective-permute-start.16 = (bf16[32,7168]{1,0:T(8,128)(2,1)S(1)}, bf16[32,7168]{1,0:T(8,128)(2,1)S(1)}, u32[]{:S(2)}, u32[]{:S(2)}) collective-permute-start(bf16[32,7168]{1,0:T(8,128)(2,1)S(1)} %pad_maximum_fusion.refs_0_), channel_id=1, source_target_pairs={{0,6},{1,25},{2,0},{3,27},{4,2},{5,29},{6,4},{7,31},{8,14},{9,1},{... | collective-permute-start | bytes 1376264 | tf_op jit(solution)/shard_map/ppermute | solution.py:55
  107.7 14.6 %collective-permute-start.17 = (bf16[32,7168]{1,0:T(8,128)(2,1)S(1)}, bf16[32,7168]{1,0:T(8,128)(2,1)S(1)}, u32[]{:S(2)}, u32[]{:S(2)}) collective-permute-start(bf16[32,7168]{1,0:T(8,128)(2,1)S(1)} %pad_maximum_fusion.refs_0_), channel_id=1, source_target_pairs={{0,4},{1,17},{2,6},{3,19},{4,0},{5,21},{6,2},{7,23},{8,12},{9,25},... | collective-permute-start | bytes 1376264 | tf_op jit(solution)/shard_map/ppermute | solution.py:55
  108.9 14.2 %collective-permute-start.18 = (bf16[32,7168]{1,0:T(8,128)(2,1)S(1)}, bf16[32,7168]{1,0:T(8,128)(2,1)S(1)}, u32[]{:S(2)}, u32[]{:S(2)}) collective-permute-start(bf16[32,7168]{1,0:T(8,128)(2,1)S(1)} %pad_maximum_fusion.refs_0_), channel_id=1, source_target_pairs={{0,2},{1,9},{2,4},{3,11},{4,6},{5,13},{6,0},{7,15},{8,10},{9,17},{... | collective-permute-start | bytes 1376264 | tf_op jit(solution)/shard_map/ppermute | solution.py:55
  110.9 12.3 %collective-permute-start.19 = (bf16[32,7168]{1,0:T(8,128)(2,1)S(1)}, bf16[32,7168]{1,0:T(8,128)(2,1)S(1)}, u32[]{:S(2)}, u32[]{:S(2)}) collective-permute-start(bf16[32,7168]{1,0:T(8,128)(2,1)S(1)} %pad_maximum_fusion.refs_0_), channel_id=1, source_target_pairs={{0,1},{1,0},{2,3},{3,2},{4,5},{5,4},{6,7},{7,6},{8,9},{9,8},{10,11... | collective-permute-start | bytes 1376264 | tf_op jit(solution)/shard_map/ppermute | solution.py:51
  129.6 5.6 %collective-permute-start.23 = (bf16[32,7168]{1,0:T(8,128)(2,1)S(1)}, bf16[32,7168]{1,0:T(8,128)(2,1)S(1)}, u32[]{:S(2)}, u32[]{:S(2)}) collective-permute-start(bf16[32,7168]{1,0:T(8,128)(2,1)S(1)} %get-tuple-element.54), channel_id=1, source_target_pairs={{0,1},{1,0},{2,3},{3,2},{4,5},{5,4},{6,7},{7,6},{8,9},{9,8},{10,11... | collective-permute-start | bytes 1376264 | tf_op jit(solution)/shard_map/ppermute | solution.py:51
  131.2 13.2 %collective-permute-start.25 = (bf16[32,7168]{1,0:T(8,128)(2,1)S(1)}, bf16[32,7168]{1,0:T(8,128)(2,1)S(1)}, u32[]{:S(2)}, u32[]{:S(2)}) collective-permute-start(bf16[32,7168]{1,0:T(8,128)(2,1)S(1)} %add_convert_fusion.2), channel_id=1, source_target_pairs={{0,2},{1,9},{2,4},{3,11},{4,6},{5,13},{6,0},{7,15},{8,10},{9,17},{... | collective-permute-start | bytes 1376264 | tf_op jit(solution)/shard_map/ppermute | solution.py:55
  133.5 14.7 %collective-permute-start.27 = (bf16[32,7168]{1,0:T(8,128)(2,1)S(1)}, bf16[32,7168]{1,0:T(8,128)(2,1)S(1)}, u32[]{:S(2)}, u32[]{:S(2)}) collective-permute-start(bf16[32,7168]{1,0:T(8,128)(2,1)S(1)} %add_convert_fusion.1), channel_id=1, source_target_pairs={{0,6},{1,25},{2,0},{3,27},{4,2},{5,29},{6,4},{7,31},{8,14},{9,1},{... | collective-permute-start | bytes 1376264 | tf_op jit(solution)/shard_map/ppermute | solution.py:55
  133.8 14.4 %collective-permute-start.29 = (bf16[32,7168]{1,0:T(8,128)(2,1)S(1)}, bf16[32,7168]{1,0:T(8,128)(2,1)S(1)}, u32[]{:S(2)}, u32[]{:S(2)}) collective-permute-start(bf16[32,7168]{1,0:T(8,128)(2,1)S(1)} %add_convert_fusion), channel_id=1, source_target_pairs={{0,4},{1,17},{2,6},{3,19},{4,0},{5,21},{6,2},{7,23},{8,12},{9,25},... | collective-permute-start | bytes 1376264 | tf_op jit(solution)/shard_map/ppermute | solution.py:55
  148.5 6.1 %collective-permute-start.30 = (bf16[8,7168]{1,0:T(8,128)(2,1)S(1)}, bf16[8,7168]{1,0:T(8,128)(2,1)S(1)}, u32[]{:S(2)}, u32[]{:S(2)}) collective-permute-start(bf16[8,7168]{1,0:T(8,128)(2,1)S(1)} %get-tuple-element.67), channel_id=1, source_target_pairs={{0,8},{1,3},{2,10},{3,5},{4,12},{5,7},{6,14},{7,1},{8,16},{9,11},{... | collective-permute-start | bytes 344072 | tf_op jit(solution)/shard_map/ppermute | solution.py:59
  149.6 5.8 %collective-permute-start.31 = (bf16[8,7168]{1,0:T(8,128)(2,1)S(1)}, bf16[8,7168]{1,0:T(8,128)(2,1)S(1)}, u32[]{:S(2)}, u32[]{:S(2)}) collective-permute-start(bf16[8,7168]{1,0:T(8,128)(2,1)S(1)} %get-tuple-element.69), channel_id=1, source_target_pairs={{0,24},{1,7},{2,26},{3,1},{4,28},{5,3},{6,30},{7,5},{8,0},{9,15},{... | collective-permute-start | bytes 344072 | tf_op jit(solution)/shard_map/ppermute | solution.py:59
  151.8 6.3 %collective-permute-start.32 = (bf16[8,7168]{1,0:T(8,128)(2,1)S(1)}, bf16[8,7168]{1,0:T(8,128)(2,1)S(1)}, u32[]{:S(2)}, u32[]{:S(2)}) collective-permute-start(bf16[8,7168]{1,0:T(8,128)(2,1)S(1)} %get-tuple-element.68), channel_id=1, source_target_pairs={{0,16},{1,5},{2,18},{3,7},{4,20},{5,1},{6,22},{7,3},{8,24},{9,13},... | collective-permute-start | bytes 344072 | tf_op jit(solution)/shard_map/ppermute | solution.py:59
  (25 other events, 301.8 us)

commit v2 on v1

--- a/solution.py
+++ b/solution.py
@@ -31,12 +31,6 @@
 MIB = 1024 * 1024
 
 
-def rms_norm(hidden, norm_gain):
-    values = hidden.astype(jnp.float32)
-    spread = jnp.mean(values * values, -1, keepdims=True)
-    return (values * lax.rsqrt(spread + 1e-06) * norm_gain.astype(jnp.float32)).astype(jnp.bfloat16)
-
-
 def chip_pairs(step0, step1):
     pairs = []
     for y in range(4):
@@ -77,18 +71,80 @@
     return total
 
 
-def reduce_rows(mine, theirs):
+def reduce_first(mine, theirs):
     got = {k: swap_cores(theirs[k]) for k in (1, 3, 2, 0)}
-    chunks = {k: add_up(mine[k], [got[k]]) for k in (1, 3, 2, 0)}
-    arrived = [along_first(chunks[k].astype(jnp.bfloat16), k) for k in (1, 3, 2)]
-    chunks = add_up(chunks[0], arrived).reshape(4, 8, -1)
+    chunks = {k: add_up(mine[k], [got[k]]).astype(jnp.bfloat16) for k in (1, 3, 2)}
+    return [mine[0], got[0]] + [along_first(chunks[k], k) for k in (1, 3, 2)]
+
+
+def reduce_second(terms):
+    chunks = add_up(terms[0], terms[1:]).reshape(4, 8, -1)
     arrived = [along_second(chunks[k].astype(jnp.bfloat16), k) for k in (1, 3, 2)]
     return add_up(chunks[0], arrived)
 
 
-def gather_rows(block):
-    arrived = {k: along_second(block, 4 - k) for k in (1, 3, 2)}
-    rows = jnp.concatenate([block] + [arrived[k] for k in (1, 2, 3)], 0)
+def share_kernel(residual, *refs):
+    terms, (total, sent) = refs[:-2], refs[-2:]
+    for n in range(0, total.shape[1], 1024):
+        lanes = slice(n, n + 1024)
+        own = terms[0][:, lanes]
+        for term in terms[1:]:
+            own = own + term[:, lanes].astype(jnp.float32)
+        first = own[:8] + residual[:, lanes].astype(jnp.float32)
+        own = jnp.concatenate([first, own[8:]], 0)
+        total[:, lanes] = own
+        sent[:, lanes] = own.astype(jnp.bfloat16)
+
+
+def settle_kernel(total, got1, got2, got3, norm_gain, hidden_out, normed, hidden):
+    width = total.shape[1]
+    squares = jnp.zeros((32, 1), jnp.float32)
+    for n in range(0, width, 1024):
+        lanes = slice(n, n + 1024)
+        block = total[:, lanes]
+        for k, got in ((1, got1), (2, got2), (3, got3)):
+            got = got[:, lanes].astype(jnp.float32)
+            block = block + jnp.concatenate([got[k * 8 :], got[: k * 8]], 0)
+        block = block.astype(jnp.bfloat16)
+        hidden_out[:, lanes] = block[:8]
+        block = block.astype(jnp.float32)
+        hidden[:, lanes] = block
+        squares = squares + jnp.sum(block * block, -1, keepdims=True)
+    spread = lax.rsqrt(squares * (1.0 / width) + 1e-06)
+    for n in range(0, width, 1024):
+        lanes = slice(n, n + 1024)
+        gain = norm_gain[:, lanes].astype(jnp.float32)
+        normed[:, lanes] = (hidden[:, lanes] * spread * gain).astype(jnp.bfloat16)
+
+
+def settle(terms, residual, norm_gain):
+    vmem = pl.BlockSpec(memory_space=pltpu.VMEM)
+    params = pltpu.CompilerParams(vmem_limit_bytes=12 * MIB)
+    shape = terms[0].shape
+    total, sent = pl.pallas_call(
+        share_kernel,
+        out_shape=[jax.ShapeDtypeStruct(shape, jnp.float32), jax.ShapeDtypeStruct(shape, jnp.bfloat16)],
+        in_specs=[vmem] * 6,
+        out_specs=[vmem] * 2,
+        compiler_params=params,
+        name="share",
+    )(residual, *terms)
+    got = {k: along_second(sent, k) for k in (1, 3, 2)}
+    return pl.pallas_call(
+        settle_kernel,
+        out_shape=[
+            jax.ShapeDtypeStruct(residual.shape, jnp.bfloat16),
+            jax.ShapeDtypeStruct(shape, jnp.bfloat16),
+        ],
+        in_specs=[vmem] * 5,
+        out_specs=[vmem] * 2,
+        scratch_shapes=[pltpu.VMEM(shape, jnp.float32)],
+        compiler_params=params,
+        name="settle",
+    )(total, got[1], got[2], got[3], norm_gain[None, :])
+
+
+def gather_first(rows):
     arrived = {k: along_first(rows, 4 - k) for k in (1, 3, 2)}
     mine = [rows] + [arrived[k] for k in (1, 2, 3)]
     return mine + [swap_cores(part) for part in mine]
@@ -206,10 +262,12 @@
 
 
 def resident_kernel(
-    lists, lengths, queries, fresh, cache,
-    query_rows, peak, total, acc, slot_row, rec_valid, rec_first,
-    keys, even, odd, head_rows, res_page, res_valid, res_first,
+    lists, lengths, queries, fresh, cache, out_proj,
+    query_rows, peak, total, acc, slot_row, rec_valid, rec_first, staged,
+    keys, even, odd, head_rows, res_page, res_valid, res_first, sem,
 ):
+    staging = pltpu.make_async_copy(out_proj, staged, sem)
+    staging.start()
     for i in range(RES_BLOCKS * 8):
         res_page[i] = 0
     for i in range(RES_SPARE):
@@ -281,9 +339,10 @@
     lay_keys(pick, lambda lanes: cache[:, lanes], keys, RES_BLOCKS)
 
     absorb_blocks(RES_BLOCKS, res_first, res_valid, query_rows, keys, peak, total, acc, even, odd)
-
-
-def attend_resident(lists, lengths, queries, fresh, cache):
+    staging.wait()
+
+
+def attend_resident(lists, lengths, queries, fresh, cache, out_proj):
     smem, vmem = pl.BlockSpec(memory_space=pltpu.SMEM), pl.BlockSpec(memory_space=pltpu.VMEM)
     shapes = [
         jax.ShapeDtypeStruct((4, ROWS, KVW), jnp.bfloat16),
@@ -293,12 +352,13 @@
         jax.ShapeDtypeStruct((24,), jnp.int32),
         jax.ShapeDtypeStruct((REC_SPARE + 8,), jnp.int32),
         jax.ShapeDtypeStruct((8,), jnp.int32),
+        jax.ShapeDtypeStruct(out_proj.shape, out_proj.dtype),
     ]
     return pl.pallas_call(
         resident_kernel,
         out_shape=shapes,
-        in_specs=[smem, smem, vmem, vmem, vmem],
-        out_specs=[vmem] * 4 + [smem] * 3,
+        in_specs=[smem, smem, vmem, vmem, vmem, pl.BlockSpec(memory_space=pl.ANY)],
+        out_specs=[vmem] * 4 + [smem] * 3 + [vmem],
         scratch_shapes=[
             pltpu.VMEM((RES_BLOCKS, KEYS, KVW), jnp.bfloat16),
             pltpu.VMEM((ROWS, KEYS), jnp.float32),
@@ -307,11 +367,12 @@
             pltpu.SMEM((RES_SPARE + 8,), jnp.int32),
             pltpu.SMEM((RES_SPARE + 8,), jnp.int32),
             pltpu.SMEM((8,), jnp.int32),
+            pltpu.SemaphoreType.DMA,
         ],
         compiler_params=pltpu.CompilerParams(vmem_limit_bytes=20 * MIB),
         cost_estimate=pl.CostEstimate(flops=8_000_000_000, bytes_accessed=12_000_000, transcendentals=2_000_000),
         name="attend_resident",
-    )(lists, lengths, queries, fresh, cache)
+    )(lists, lengths, queries, fresh, cache, out_proj)
 
 
 def received_kernel(
@@ -498,19 +559,18 @@
         lax.ppermute(box, "grp", [(g, (g + k) % 4) for g in range(4)])
         for k, box in enumerate(boxes, 1)
     ]
-    *state, slot_row, rec_valid, rec_first = attend_resident(
-        page_lists, context_len, queries, fresh_latents, cache_pages
+    *state, slot_row, rec_valid, rec_first, out_proj = attend_resident(
+        page_lists, context_len, queries, fresh_latents, cache_pages, out_proj
     )
     attended = attend_received(
         route, (slot_row, rec_valid, rec_first), boxes, prefill_pages, state
     )
     by_heads = lax.all_to_all(attended, "tp", split_axis=0, concat_axis=0, tiled=True)
     values, *theirs = project_values(token_order()[:, None], by_heads.reshape(1024, LAT), value_up, out_proj)
-    attn_out = reduce_rows(project(values, out_proj), theirs)
-    hidden = (residual.astype(jnp.float32) + attn_out).astype(jnp.bfloat16)
-    normed = rms_norm(hidden, norm_gain)
-    act, *theirs = hidden_units(gather_rows(normed), gate_weight, up_weight, down_weight)
-    mlp = reduce_rows(project(act, down_weight), theirs)
+    terms = reduce_first(project(values, out_proj), theirs)
+    hidden, normed = settle(terms, residual, norm_gain)
+    act, *theirs = hidden_units(gather_first(normed), gate_weight, up_weight, down_weight)
+    mlp = reduce_second(reduce_first(project(act, down_weight), theirs))
     return (hidden.astype(jnp.float32) + mlp).astype(jnp.bfloat16)
 
 

time: 159 us -> 155 us (0.975)
  waiting for transfers between devices: 82.6 us -> 69 us
  local copies, waits for them, and re-layouts: 10.1 us -> 16 us
  Pallas kernels: 24.5 us -> 26.8 us
  starting transfers between devices: 38.4 us -> 40.3 us
    ppermute x3, waiting for transfers between devices: 9.83 us -> 2.29 us  [shards(): lax.ppermute(box, 'grp', [(g, (g + k) % 4) for g in range(4)])]
    unnamed x30 -> x34, local copies, waits for them, and re-layouts: 10 us -> 16 us
    ppermute x9, waiting for transfers between devices: 37.1 us -> 33.1 us  [along_first(): return lax.ppermute(block, 'tp', chip_pairs((0, k, 0), (k, 0, 0)))]
    ppermute x9, starting transfers between devices: 11.4 us -> 14.5 us  [along_first(): return lax.ppermute(block, 'tp', chip_pairs((0, k, 0), (k, 0, 0)))]
    ppermute x9 -> x6, waiting for transfers between devices: 19 us -> 17.4 us  [along_second(): return lax.ppermute(block, 'tp', chip_pairs((k, 0, 0), (0, k, 0)))]
    ppermute x9 -> x6, starting transfers between devices: 8.71 us -> 7.77 us  [along_second(): return lax.ppermute(block, 'tp', chip_pairs((k, 0, 0), (0, k, 0)))]
  transfers between devices with their start and end apart: 34 -> 31, of which waited for: 20 -> 15; matrix products, arithmetic and copies ran while one was open for 0% -> 0% of each run, Pallas kernels for 7% -> 8%
where the time goes in v2:
time: 155 us
  waiting for transfers between devices  69 us (45%)
  starting transfers between devices  40.3 us (26%)
  Pallas kernels  26.8 us (17%)
  local copies, waits for them, and re-layouts  16 us (10%)
  other arithmetic  2.32 us (1%)
    ppermute x9, waiting for transfers between devices, along_first(): return lax.ppermute(block, 'tp', chip_pairs((0, k, 0), (k, 0, 0)))  33.1 us
    ppermute x6, waiting for transfers between devices, along_second(): return lax.ppermute(block, 'tp', chip_pairs((k, 0, 0), (0, k, 0)))  17.4 us
    unnamed x34, local copies, waits for them, and re-layouts  16 us
    ppermute x9, starting transfers between devices, along_first(): return lax.ppermute(block, 'tp', chip_pairs((0, k, 0), (k, 0, 0)))  14.5 us
    all_to_all x1, waiting for transfers between devices, shards(): lax.all_to_all(attended, 'tp', split_axis=0, concat_axis=0, tiled=True)  14.4 us
    pallas_call x1, Pallas kernels, attend_resident(): pl.pallas_call(resident_kernel, out_shape=shapes, in_specs=[smem, smem, v...  10.8 us
    all_to_all x1, starting transfers between devices, shards(): lax.all_to_all(attended, 'tp', split_axis=0, concat_axis=0, tiled=True)  8.29 us
    ppermute x6, starting transfers between devices, along_second(): return lax.ppermute(block, 'tp', chip_pairs((k, 0, 0), (0, k, 0)))  7.77 us
  transfers between devices with their start and end apart: 31, of which 15 were waited for; matrix products, arithmetic and copies ran while one was open for 0% of the time, Pallas kernels for 8%

profile of v2, /device:TPU:6, one launch (start us, length us, event | category | flops | bytes accessed | tf_op | source)
XLA Modules:
  0.0 154.7 jit_solution(17536898322955269196)
XLA Ops:
  5.5 3.6 %collective-permute-start.1 = (bf16[8,36992]{1,0:T(8,128)(2,1)S(1)}, bf16[8,36992]{1,0:T(8,128)(2,1)S(1)}, u32[]{:S(2)}, u32[]{:S(2)}) collective-permute-start(bf16[8,36992]{1,0:T(8,128)(2,1)S(1)} %get-tuple-element.42), channel_id=1, source_target_pairs={{0,64},{32,96},{64,0},{96,32},{1,65},{33,97},{65,1},{97,33},{2,66}... | collective-permute-start | bytes 1775624 | tf_op jit(solution)/shard_map/ppermute | solution.py:559
  10.1 3.1 %copy-done.9 = bf16[512,7168]{1,0:T(8,128)(2,1)S(1)} copy-done((bf16[512,7168]{1,0:T(8,128)(2,1)S(1)}, bf16[512,7168]{1,0:T(8,128)(2,1)}, u32[]{:S(2)}) %copy-start.9) | copy-done | bytes 7340056
  13.1 2.3 %copy-done.10 = bf16[64,36864]{1,0:T(8,128)(2,1)S(1)} copy-done((bf16[64,36864]{1,0:T(8,128)(2,1)S(1)}, bf16[64,36864]{1,0:T(8,128)(2,1)}, u32[]{:S(2)}) %copy-start.10) | copy-done | bytes 4718616
  18.8 10.8 %attend_resident.1 = (bf16[4,256,576]{2,1,0:T(8,128)(2,1)S(1)}, f32[4,256,128]{2,1,0:T(8,128)S(1)}, f32[4,256,128]{2,1,0:T(8,128)S(1)}, f32[4,256,512]{2,1,0:T(8...) custom-call(s32[4,40]{1,0:T(4,128)S(1)} %copy-done.14, ...), custom_call_target="tpu_custom_call" | custom-call | flops 8000000000 | bytes 12000000 | tf_op jit(solution)/shard_map/attend_resident/pallas_call | solution.py:357
  29.7 2.9 %copy-done.1 = bf16[512,7168]{1,0:T(8,128)(2,1)} copy-done((bf16[512,7168]{1,0:T(8,128)(2,1)}, bf16[512,7168]{1,0:T(8,128)(2,1)S(1)}, u32[]{:S(2)}) %copy-start.1) | copy-done | bytes 7340056
  32.5 2.3 %collective-permute-done.1.box2 = bf16[8,36992]{1,0:T(8,128)(2,1)S(1)} collective-permute-done((bf16[8,36992]{1,0:T(8,128)(2,1)S(1)}, bf16[8,36992]{1,0:T(8,128)(2,1)S(1)}, u32[]{:S(2)}, u32[]{:S(2)}) %collective-permute-start.1) | collective-permute-done | bytes 591904 | tf_op jit(solution)/shard_map/ppermute | solution.py:559
  34.8 5.9 %attend_received.1 = bf16[32,32,512]{2,1,0:T(8,128)(2,1)} custom-call(s32[16]{0:T(128)S(1)} %multiply_add_fusion.route, s32[24]{0:T(128)S(1)} %get-tuple-element.38.slot_row, s32[56]{0:T(128)S(1)} %get-tuple-element.39.rec_valid, s32[8]{0:T(128)S(1)} %get-tuple-element.40.rec_first, bf16[8,36992]{1,0:T(8,128)(2,1)S(1)} %collective-permute-done.box1, ...), custom_call_target="tpu_custom_call" | custom-call | tf_op jit(solution)/shard_map/attend_received/pallas_call | solution.py:419
  40.7 8.3 %all-to-all-start = ((bf16[32,32,512]{2,1,0:T(8,128)(2,1)}), bf16[32,32,512]{2,1,0:T(8,128)(2,1)S(1)}, u32[]{:S(2)}, u32[]{:S(2)}) async-start(bf16[32,32,512]{2,1,0:T(8,128)(2,1)} %attend_received.1), calls=%async_computation | async-start | bytes 2097152 | tf_op jit(solution)/shard_map/all_to_all | solution.py:568
  49.3 14.4 %all-to-all-done = bf16[32,32,512]{2,1,0:T(8,128)(2,1)S(1)} async-done(((bf16[32,32,512]{2,1,0:T(8,128)(2,1)}), bf16[32,32,512]{2,1,0:T(8,128)(2,1)S(1)}, u32[]{:S(2)}, u32[]{:S(2)}) %all-to-all-start) | async-done | bytes 1048608 | tf_op jit(solution)/shard_map/all_to_all | solution.py:568
  63.7 3.1 %copy-done.2 = bf16[512,7168]{1,0:T(8,128)(2,1)S(1)} copy-done((bf16[512,7168]{1,0:T(8,128)(2,1)S(1)}, bf16[512,7168]{1,0:T(8,128)(2,1)}, u32[]{:S(2)}) %copy-start.2) | copy-done | bytes 7340056
  66.8 2.1 %values.1 = (bf16[128,512]{1,0:T(8,128)(2,1)S(1)}, bf16[32,7168]{1,0:T(8,128)(2,1)S(1)}, bf16[32,7168]{1,0:T(8,128)(2,1)S(1)}, bf16[32,7168]{1,0:T(8,128)(2,1)S(1)}, bf16[32,7168]{1,0:T(8,128)(2,1)S(1)}) custom-call(s32[256,1]{1,0:T(8,128)S(1)} %fusion.9.order, bf16[1024,512]{1,0:T(8,128)(2,1)S(1)} %bitcast.5, bf16[4,512,128]{2,1,0:T(8,128)(2,1)S(1)} %copy-done.12, ...), custom_call_target="tpu_custom_call" | custom-call | flops 2500000000 | bytes 12000000 | tf_op jit(solution)/shard_map/values/pallas_call | solution.py:473
  75.3 2.4 %collective-permute-start.5 = (bf16[32,7168]{1,0:T(8,128)(2,1)S(1)}, bf16[32,7168]{1,0:T(8,128)(2,1)S(1)}, u32[]{:S(2)}, u32[]{:S(2)}) collective-permute-start(bf16[32,7168]{1,0:T(8,128)(2,1)S(1)} %add_convert_fusion.5), channel_id=1, source_target_pairs={{0,2},{1,9},{2,4},{3,11},{4,6},{5,13},{6,0},{7,15},{8,10},{9,17},{... | collective-permute-start | bytes 1376264 | tf_op jit(solution)/shard_map/ppermute | solution.py:49
  77.8 4.6 %collective-permute-done.9.refs_4_ = bf16[32,7168]{1,0:T(8,128)(2,1)S(1)} collective-permute-done((bf16[32,7168]{1,0:T(8,128)(2,1)S(1)}, bf16[32,7168]{1,0:T(8,128)(2,1)S(1)}, u32[]{:S(2)}, u32[]{:S(2)}) %collective-permute-start.9) | collective-permute-done | bytes 458784 | tf_op jit(solution)/shard_map/ppermute | solution.py:49
  82.3 4.8 %collective-permute-done.7.refs_3_ = bf16[32,7168]{1,0:T(8,128)(2,1)S(1)} collective-permute-done((bf16[32,7168]{1,0:T(8,128)(2,1)S(1)}, bf16[32,7168]{1,0:T(8,128)(2,1)S(1)}, u32[]{:S(2)}, u32[]{:S(2)}) %collective-permute-start.7) | collective-permute-done | bytes 458784 | tf_op jit(solution)/shard_map/ppermute | solution.py:49
  91.1 11.0 %collective-permute-done.10.got1 = bf16[32,7168]{1,0:T(8,128)(2,1)S(1)} collective-permute-done((bf16[32,7168]{1,0:T(8,128)(2,1)S(1)}, bf16[32,7168]{1,0:T(8,128)(2,1)S(1)}, u32[]{:S(2)}, u32[]{:S(2)}) %collective-permute-start.10) | collective-permute-done | bytes 458784 | tf_op jit(solution)/shard_map/ppermute | solution.py:53
  104.1 2.9 %collective-permute-start.14 = (bf16[32,7168]{1,0:T(8,128)(2,1)S(1)}, bf16[32,7168]{1,0:T(8,128)(2,1)S(1)}, u32[]{:S(2)}, u32[]{:S(2)}) collective-permute-start(bf16[32,7168]{1,0:T(8,128)(2,1)S(1)} %get-tuple-element.61.refs_0_), channel_id=1, source_target_pairs={{0,4},{1,17},{2,6},{3,19},{4,0},{5,21},{6,2},{7,23},{8,12},{9,25},... | collective-permute-start | bytes 1376264 | tf_op jit(solution)/shard_map/ppermute | solution.py:49
  108.1 5.1 %collective-permute-done.13.refs_1_ = bf16[32,7168]{1,0:T(8,128)(2,1)S(1)} collective-permute-done((bf16[32,7168]{1,0:T(8,128)(2,1)S(1)}, bf16[32,7168]{1,0:T(8,128)(2,1)S(1)}, u32[]{:S(2)}, u32[]{:S(2)}) %collective-permute-start.13) | collective-permute-done | bytes 458784 | tf_op jit(solution)/shard_map/ppermute | solution.py:49
  113.2 5.1 %collective-permute-done.14.refs_2_ = bf16[32,7168]{1,0:T(8,128)(2,1)S(1)} collective-permute-done((bf16[32,7168]{1,0:T(8,128)(2,1)S(1)}, bf16[32,7168]{1,0:T(8,128)(2,1)S(1)}, u32[]{:S(2)}, u32[]{:S(2)}) %collective-permute-start.14) | collective-permute-done | bytes 458784 | tf_op jit(solution)/shard_map/ppermute | solution.py:49
  120.8 3.5 %hidden_units.1 = (bf16[128,288]{1,0:T(8,128)(2,1)S(1)}, bf16[32,7168]{1,0:T(8,128)(2,1)S(1)}, bf16[32,7168]{1,0:T(8,128)(2,1)S(1)}, bf16[32,7168]{1,0:T(8,128)(2,1)S(1)}, bf16[32,7168]{1,0:T(8,128)(2,1)S(1)}) custom-call(bf16[32,7168]{1,0:T(8,128)(2,1)S(1)} %get-tuple-element.61.refs_0_, bf16[32,7168]{1,0:T(8,128)(2,1)S(1)} %collective-permute-done.13.refs_1_, ...), custom_call_target="tpu_custom_call" | custom-call | flops 3000000000 | bytes 18000000 | tf_op jit(solution)/shard_map/hidden_units/pallas_call | solution.py:526
  126.7 2.7 %collective-permute-start.22 = (bf16[32,7168]{1,0:T(8,128)(2,1)S(1)}, bf16[32,7168]{1,0:T(8,128)(2,1)S(1)}, u32[]{:S(2)}, u32[]{:S(2)}) collective-permute-start(bf16[32,7168]{1,0:T(8,128)(2,1)S(1)} %add_convert_fusion.2), channel_id=1, source_target_pairs={{0,2},{1,9},{2,4},{3,11},{4,6},{5,13},{6,0},{7,15},{8,10},{9,17},{... | collective-permute-start | bytes 1376264 | tf_op jit(solution)/shard_map/ppermute | solution.py:49
  131.3 9.0 %collective-permute-done.22 = bf16[32,7168]{1,0:T(8,128)(2,1)S(1)} collective-permute-done((bf16[32,7168]{1,0:T(8,128)(2,1)S(1)}, bf16[32,7168]{1,0:T(8,128)(2,1)S(1)}, u32[]{:S(2)}, u32[]{:S(2)}) %collective-permute-start.22) | collective-permute-done | bytes 458784 | tf_op jit(solution)/shard_map/ppermute | solution.py:49
  140.3 3.8 %collective-permute-done.24 = bf16[32,7168]{1,0:T(8,128)(2,1)S(1)} collective-permute-done((bf16[32,7168]{1,0:T(8,128)(2,1)S(1)}, bf16[32,7168]{1,0:T(8,128)(2,1)S(1)}, u32[]{:S(2)}, u32[]{:S(2)}) %collective-permute-start.24) | collective-permute-done | bytes 458784 | tf_op jit(solution)/shard_map/ppermute | solution.py:49
  144.7 3.0 %collective-permute-start.28 = (bf16[8,7168]{1,0:T(8,128)(2,1)S(1)}, bf16[8,7168]{1,0:T(8,128)(2,1)S(1)}, u32[]{:S(2)}, u32[]{:S(2)}) collective-permute-start(bf16[8,7168]{1,0:T(8,128)(2,1)S(1)} %get-tuple-element.75), channel_id=1, source_target_pairs={{0,24},{1,7},{2,26},{3,1},{4,28},{5,3},{6,30},{7,5},{8,0},{9,15},{... | collective-permute-start | bytes 344072 | tf_op jit(solution)/shard_map/ppermute | solution.py:53
  150.5 3.5 %collective-permute-done.29 = bf16[8,7168]{1,0:T(8,128)(2,1)S(1)} collective-permute-done((bf16[8,7168]{1,0:T(8,128)(2,1)S(1)}, bf16[8,7168]{1,0:T(8,128)(2,1)S(1)}, u32[]{:S(2)}, u32[]{:S(2)}) %collective-permute-start.29) | collective-permute-done | bytes 114720 | tf_op jit(solution)/shard_map/ppermute | solution.py:53
  (93 shorter events, 34.3 us)
Async XLA Ops:
  3.5 29.1 %collective-permute-start = (bf16[8,36992]{1,0:T(8,128)(2,1)S(1)}, bf16[8,36992]{1,0:T(8,128)(2,1)S(1)}, u32[]{:S(2)}, u32[]{:S(2)}) collective-permute-start(bf16[8,36992]{1,0:T(8,128)(2,1)S(1)} %get-tuple-element.41), channel_id=1, source_target_pairs={{0,32},{32,64},{64,96},{96,0},{1,33},{33,65},{65,97},{97,1},{2,34}... | collective-permute-start | bytes 1775624 | tf_op jit(solution)/shard_map/ppermute | solution.py:559
  5.5 29.3 %collective-permute-start.1 = (bf16[8,36992]{1,0:T(8,128)(2,1)S(1)}, bf16[8,36992]{1,0:T(8,128)(2,1)S(1)}, u32[]{:S(2)}, u32[]{:S(2)}) collective-permute-start(bf16[8,36992]{1,0:T(8,128)(2,1)S(1)} %get-tuple-element.42), channel_id=1, source_target_pairs={{0,64},{32,96},{64,0},{96,32},{1,65},{33,97},{65,1},{97,33},{2,66}... | collective-permute-start | bytes 1775624 | tf_op jit(solution)/shard_map/ppermute | solution.py:559
  9.1 25.8 %collective-permute-start.2 = (bf16[8,36992]{1,0:T(8,128)(2,1)S(1)}, bf16[8,36992]{1,0:T(8,128)(2,1)S(1)}, u32[]{:S(2)}, u32[]{:S(2)}) collective-permute-start(bf16[8,36992]{1,0:T(8,128)(2,1)S(1)} %get-tuple-element.43), channel_id=1, source_target_pairs={{0,96},{32,0},{64,32},{96,64},{1,97},{33,1},{65,33},{97,65},{2,98}... | collective-permute-start | bytes 1775624 | tf_op jit(solution)/shard_map/ppermute | solution.py:559
  40.7 22.9 %all-to-all-start = ((bf16[32,32,512]{2,1,0:T(8,128)(2,1)}), bf16[32,32,512]{2,1,0:T(8,128)(2,1)S(1)}, u32[]{:S(2)}, u32[]{:S(2)}) async-start(bf16[32,32,512]{2,1,0:T(8,128)(2,1)} %attend_received.1), calls=%async_computation | async-start | bytes 2097152 | tf_op jit(solution)/shard_map/all_to_all | solution.py:568
  70.4 4.8 %collective-permute-start.4 = (bf16[32,7168]{1,0:T(8,128)(2,1)S(1)}, bf16[32,7168]{1,0:T(8,128)(2,1)S(1)}, u32[]{:S(2)}, u32[]{:S(2)}) collective-permute-start(bf16[32,7168]{1,0:T(8,128)(2,1)S(1)} %get-tuple-element.53), channel_id=1, source_target_pairs={{0,1},{1,0},{2,3},{3,2},{4,5},{5,4},{6,7},{7,6},{8,9},{9,8},{10,11... | collective-permute-start | bytes 1376264 | tf_op jit(solution)/shard_map/ppermute | solution.py:45
  70.8 7.0 %collective-permute-start.3 = (bf16[32,7168]{1,0:T(8,128)(2,1)S(1)}, bf16[32,7168]{1,0:T(8,128)(2,1)S(1)}, u32[]{:S(2)}, u32[]{:S(2)}) collective-permute-start(bf16[32,7168]{1,0:T(8,128)(2,1)S(1)} %get-tuple-element.51), channel_id=1, source_target_pairs={{0,1},{1,0},{2,3},{3,2},{4,5},{5,4},{6,7},{7,6},{8,9},{9,8},{10,11... | collective-permute-start | bytes 1376264 | tf_op jit(solution)/shard_map/ppermute | solution.py:45
  72.2 10.2 %collective-permute-start.9 = (bf16[32,7168]{1,0:T(8,128)(2,1)S(1)}, bf16[32,7168]{1,0:T(8,128)(2,1)S(1)}, u32[]{:S(2)}, u32[]{:S(2)}) collective-permute-start(bf16[32,7168]{1,0:T(8,128)(2,1)S(1)} %add_convert_fusion.3), channel_id=1, source_target_pairs={{0,4},{1,17},{2,6},{3,19},{4,0},{5,21},{6,2},{7,23},{8,12},{9,25},... | collective-permute-start | bytes 1376264 | tf_op jit(solution)/shard_map/ppermute | solution.py:49
  74.3 12.8 %collective-permute-start.7 = (bf16[32,7168]{1,0:T(8,128)(2,1)S(1)}, bf16[32,7168]{1,0:T(8,128)(2,1)S(1)}, u32[]{:S(2)}, u32[]{:S(2)}) collective-permute-start(bf16[32,7168]{1,0:T(8,128)(2,1)S(1)} %add_convert_fusion.4), channel_id=1, source_target_pairs={{0,6},{1,25},{2,0},{3,27},{4,2},{5,29},{6,4},{7,31},{8,14},{9,1},{... | collective-permute-start | bytes 1376264 | tf_op jit(solution)/shard_map/ppermute | solution.py:49
  75.3 11.8 %collective-permute-start.5 = (bf16[32,7168]{1,0:T(8,128)(2,1)S(1)}, bf16[32,7168]{1,0:T(8,128)(2,1)S(1)}, u32[]{:S(2)}, u32[]{:S(2)}) collective-permute-start(bf16[32,7168]{1,0:T(8,128)(2,1)S(1)} %add_convert_fusion.5), channel_id=1, source_target_pairs={{0,2},{1,9},{2,4},{3,11},{4,6},{5,13},{6,0},{7,15},{8,10},{9,17},{... | collective-permute-start | bytes 1376264 | tf_op jit(solution)/shard_map/ppermute | solution.py:49
  87.4 14.7 %collective-permute-start.10 = (bf16[32,7168]{1,0:T(8,128)(2,1)S(1)}, bf16[32,7168]{1,0:T(8,128)(2,1)S(1)}, u32[]{:S(2)}, u32[]{:S(2)}) collective-permute-start(bf16[32,7168]{1,0:T(8,128)(2,1)S(1)} %get-tuple-element.59), channel_id=1, source_target_pairs={{0,8},{1,3},{2,10},{3,5},{4,12},{5,7},{6,14},{7,1},{8,16},{9,11},{... | collective-permute-start | bytes 1376264 | tf_op jit(solution)/shard_map/ppermute | solution.py:53
  88.1 14.0 %collective-permute-start.11 = (bf16[32,7168]{1,0:T(8,128)(2,1)S(1)}, bf16[32,7168]{1,0:T(8,128)(2,1)S(1)}, u32[]{:S(2)}, u32[]{:S(2)}) collective-permute-start(bf16[32,7168]{1,0:T(8,128)(2,1)S(1)} %get-tuple-element.59), channel_id=1, source_target_pairs={{0,16},{1,5},{2,18},{3,7},{4,20},{5,1},{6,22},{7,3},{8,24},{9,13},... | collective-permute-start | bytes 1376264 | tf_op jit(solution)/shard_map/ppermute | solution.py:53
  90.1 12.9 %collective-permute-start.12 = (bf16[32,7168]{1,0:T(8,128)(2,1)S(1)}, bf16[32,7168]{1,0:T(8,128)(2,1)S(1)}, u32[]{:S(2)}, u32[]{:S(2)}) collective-permute-start(bf16[32,7168]{1,0:T(8,128)(2,1)S(1)} %get-tuple-element.59), channel_id=1, source_target_pairs={{0,24},{1,7},{2,26},{3,1},{4,28},{5,3},{6,30},{7,5},{8,0},{9,15},{... | collective-permute-start | bytes 1376264 | tf_op jit(solution)/shard_map/ppermute | solution.py:53
  103.4 9.8 %collective-permute-start.13 = (bf16[32,7168]{1,0:T(8,128)(2,1)S(1)}, bf16[32,7168]{1,0:T(8,128)(2,1)S(1)}, u32[]{:S(2)}, u32[]{:S(2)}) collective-permute-start(bf16[32,7168]{1,0:T(8,128)(2,1)S(1)} %get-tuple-element.61.refs_0_), channel_id=1, source_target_pairs={{0,6},{1,25},{2,0},{3,27},{4,2},{5,29},{6,4},{7,31},{8,14},{9,1},{... | collective-permute-start | bytes 1376264 | tf_op jit(solution)/shard_map/ppermute | solution.py:49
  104.1 14.2 %collective-permute-start.14 = (bf16[32,7168]{1,0:T(8,128)(2,1)S(1)}, bf16[32,7168]{1,0:T(8,128)(2,1)S(1)}, u32[]{:S(2)}, u32[]{:S(2)}) collective-permute-start(bf16[32,7168]{1,0:T(8,128)(2,1)S(1)} %get-tuple-element.61.refs_0_), channel_id=1, source_target_pairs={{0,4},{1,17},{2,6},{3,19},{4,0},{5,21},{6,2},{7,23},{8,12},{9,25},... | collective-permute-start | bytes 1376264 | tf_op jit(solution)/shard_map/ppermute | solution.py:49
  106.9 12.1 %collective-permute-start.15 = (bf16[32,7168]{1,0:T(8,128)(2,1)S(1)}, bf16[32,7168]{1,0:T(8,128)(2,1)S(1)}, u32[]{:S(2)}, u32[]{:S(2)}) collective-permute-start(bf16[32,7168]{1,0:T(8,128)(2,1)S(1)} %get-tuple-element.61.refs_0_), channel_id=1, source_target_pairs={{0,2},{1,9},{2,4},{3,11},{4,6},{5,13},{6,0},{7,15},{8,10},{9,17},{... | collective-permute-start | bytes 1376264 | tf_op jit(solution)/shard_map/ppermute | solution.py:49
  108.1 10.9 %collective-permute-start.16 = (bf16[32,7168]{1,0:T(8,128)(2,1)S(1)}, bf16[32,7168]{1,0:T(8,128)(2,1)S(1)}, u32[]{:S(2)}, u32[]{:S(2)}) collective-permute-start(bf16[32,7168]{1,0:T(8,128)(2,1)S(1)} %get-tuple-element.61.refs_0_), channel_id=1, source_target_pairs={{0,1},{1,0},{2,3},{3,2},{4,5},{5,4},{6,7},{7,6},{8,9},{9,8},{10,11... | collective-permute-start | bytes 1376264 | tf_op jit(solution)/shard_map/ppermute | solution.py:45
  113.2 5.8 %collective-permute-start.17 = (bf16[32,7168]{1,0:T(8,128)(2,1)S(1)}, bf16[32,7168]{1,0:T(8,128)(2,1)S(1)}, u32[]{:S(2)}, u32[]{:S(2)}) collective-permute-start(bf16[32,7168]{1,0:T(8,128)(2,1)S(1)} %collective-permute-done.13.refs_1_), channel_id=1, source_target_pairs={{0,1},{1,0},{2,3},{3,2},{4,5},{5,4},{6,7},{7,6},{8,9},{9,8},{10,11... | collective-permute-start | bytes 1376264 | tf_op jit(solution)/shard_map/ppermute | solution.py:45
  125.0 6.2 %collective-permute-start.20 = (bf16[32,7168]{1,0:T(8,128)(2,1)S(1)}, bf16[32,7168]{1,0:T(8,128)(2,1)S(1)}, u32[]{:S(2)}, u32[]{:S(2)}) collective-permute-start(bf16[32,7168]{1,0:T(8,128)(2,1)S(1)} %get-tuple-element.64), channel_id=1, source_target_pairs={{0,1},{1,0},{2,3},{3,2},{4,5},{5,4},{6,7},{7,6},{8,9},{9,8},{10,11... | collective-permute-start | bytes 1376264 | tf_op jit(solution)/shard_map/ppermute | solution.py:45
  126.7 13.6 %collective-permute-start.22 = (bf16[32,7168]{1,0:T(8,128)(2,1)S(1)}, bf16[32,7168]{1,0:T(8,128)(2,1)S(1)}, u32[]{:S(2)}, u32[]{:S(2)}) collective-permute-start(bf16[32,7168]{1,0:T(8,128)(2,1)S(1)} %add_convert_fusion.2), channel_id=1, source_target_pairs={{0,2},{1,9},{2,4},{3,11},{4,6},{5,13},{6,0},{7,15},{8,10},{9,17},{... | collective-permute-start | bytes 1376264 | tf_op jit(solution)/shard_map/ppermute | solution.py:49
  129.4 14.7 %collective-permute-start.24 = (bf16[32,7168]{1,0:T(8,128)(2,1)S(1)}, bf16[32,7168]{1,0:T(8,128)(2,1)S(1)}, u32[]{:S(2)}, u32[]{:S(2)}) collective-permute-start(bf16[32,7168]{1,0:T(8,128)(2,1)S(1)} %add_convert_fusion.1), channel_id=1, source_target_pairs={{0,6},{1,25},{2,0},{3,27},{4,2},{5,29},{6,4},{7,31},{8,14},{9,1},{... | collective-permute-start | bytes 1376264 | tf_op jit(solution)/shard_map/ppermute | solution.py:49
  129.6 14.5 %collective-permute-start.26 = (bf16[32,7168]{1,0:T(8,128)(2,1)S(1)}, bf16[32,7168]{1,0:T(8,128)(2,1)S(1)}, u32[]{:S(2)}, u32[]{:S(2)}) collective-permute-start(bf16[32,7168]{1,0:T(8,128)(2,1)S(1)} %add_convert_fusion), channel_id=1, source_target_pairs={{0,4},{1,17},{2,6},{3,19},{4,0},{5,21},{6,2},{7,23},{8,12},{9,25},... | collective-permute-start | bytes 1376264 | tf_op jit(solution)/shard_map/ppermute | solution.py:49
  144.4 6.1 %collective-permute-start.27 = (bf16[8,7168]{1,0:T(8,128)(2,1)S(1)}, bf16[8,7168]{1,0:T(8,128)(2,1)S(1)}, u32[]{:S(2)}, u32[]{:S(2)}) collective-permute-start(bf16[8,7168]{1,0:T(8,128)(2,1)S(1)} %get-tuple-element.73), channel_id=1, source_target_pairs={{0,8},{1,3},{2,10},{3,5},{4,12},{5,7},{6,14},{7,1},{8,16},{9,11},{... | collective-permute-start | bytes 344072 | tf_op jit(solution)/shard_map/ppermute | solution.py:53
  144.7 5.8 %collective-permute-start.28 = (bf16[8,7168]{1,0:T(8,128)(2,1)S(1)}, bf16[8,7168]{1,0:T(8,128)(2,1)S(1)}, u32[]{:S(2)}, u32[]{:S(2)}) collective-permute-start(bf16[8,7168]{1,0:T(8,128)(2,1)S(1)} %get-tuple-element.75), channel_id=1, source_target_pairs={{0,24},{1,7},{2,26},{3,1},{4,28},{5,3},{6,30},{7,5},{8,0},{9,15},{... | collective-permute-start | bytes 344072 | tf_op jit(solution)/shard_map/ppermute | solution.py:53
  147.7 6.3 %collective-permute-start.29 = (bf16[8,7168]{1,0:T(8,128)(2,1)S(1)}, bf16[8,7168]{1,0:T(8,128)(2,1)S(1)}, u32[]{:S(2)}, u32[]{:S(2)}) collective-permute-start(bf16[8,7168]{1,0:T(8,128)(2,1)S(1)} %get-tuple-element.74), channel_id=1, source_target_pairs={{0,16},{1,5},{2,18},{3,7},{4,20},{5,1},{6,22},{7,3},{8,24},{9,13},... | collective-permute-start | bytes 344072 | tf_op jit(solution)/shard_map/ppermute | solution.py:53
  (24 other events, 274.3 us)

commit v3 on v2

--- a/solution.py
+++ b/solution.py
@@ -18,7 +18,8 @@
 PAIR = 2 * KVW
 RES_BLOCKS = 11
 UNROLL = 16
-PRODUCT_WIDTH = 512
+CUTS = (1792, 5376)
+PRODUCT_WIDTH = 256
 HIDDEN_WIDTH = 1792
 REC_BLOCKS = 5
 RES_SPARE = (RES_BLOCKS + 1) * 8
@@ -262,12 +263,10 @@
 
 
 def resident_kernel(
-    lists, lengths, queries, fresh, cache, out_proj,
-    query_rows, peak, total, acc, slot_row, rec_valid, rec_first, staged,
-    keys, even, odd, head_rows, res_page, res_valid, res_first, sem,
+    lists, lengths, queries, fresh, cache,
+    query_rows, peak, total, acc, slot_row, rec_valid, rec_first,
+    keys, even, odd, head_rows, res_page, res_valid, res_first,
 ):
-    staging = pltpu.make_async_copy(out_proj, staged, sem)
-    staging.start()
     for i in range(RES_BLOCKS * 8):
         res_page[i] = 0
     for i in range(RES_SPARE):
@@ -339,10 +338,9 @@
     lay_keys(pick, lambda lanes: cache[:, lanes], keys, RES_BLOCKS)
 
     absorb_blocks(RES_BLOCKS, res_first, res_valid, query_rows, keys, peak, total, acc, even, odd)
-    staging.wait()
-
-
-def attend_resident(lists, lengths, queries, fresh, cache, out_proj):
+
+
+def attend_resident(lists, lengths, queries, fresh, cache):
     smem, vmem = pl.BlockSpec(memory_space=pltpu.SMEM), pl.BlockSpec(memory_space=pltpu.VMEM)
     shapes = [
         jax.ShapeDtypeStruct((4, ROWS, KVW), jnp.bfloat16),
@@ -352,13 +350,12 @@
         jax.ShapeDtypeStruct((24,), jnp.int32),
         jax.ShapeDtypeStruct((REC_SPARE + 8,), jnp.int32),
         jax.ShapeDtypeStruct((8,), jnp.int32),
-        jax.ShapeDtypeStruct(out_proj.shape, out_proj.dtype),
     ]
     return pl.pallas_call(
         resident_kernel,
         out_shape=shapes,
-        in_specs=[smem, smem, vmem, vmem, vmem, pl.BlockSpec(memory_space=pl.ANY)],
-        out_specs=[vmem] * 4 + [smem] * 3 + [vmem],
+        in_specs=[smem, smem, vmem, vmem, vmem],
+        out_specs=[vmem] * 4 + [smem] * 3,
         scratch_shapes=[
             pltpu.VMEM((RES_BLOCKS, KEYS, KVW), jnp.bfloat16),
             pltpu.VMEM((ROWS, KEYS), jnp.float32),
@@ -367,22 +364,24 @@
             pltpu.SMEM((RES_SPARE + 8,), jnp.int32),
             pltpu.SMEM((RES_SPARE + 8,), jnp.int32),
             pltpu.SMEM((8,), jnp.int32),
-            pltpu.SemaphoreType.DMA,
         ],
         compiler_params=pltpu.CompilerParams(vmem_limit_bytes=20 * MIB),
         cost_estimate=pl.CostEstimate(flops=8_000_000_000, bytes_accessed=12_000_000, transcendentals=2_000_000),
         name="attend_resident",
-    )(lists, lengths, queries, fresh, cache, out_proj)
+    )(lists, lengths, queries, fresh, cache)
 
 
 def received_kernel(
     route, slot_row, rec_valid, rec_first,
     box1, box2, box3, own, query_rows, peak_in, total_in, acc_in,
-    out, keys, even, odd, peak, total, acc,
+    out, keys, even, odd, peak, total, acc, sems,
 ):
-    peak[...] = peak_in[...]
-    total[...] = total_in[...]
-    acc[...] = acc_in[...]
+    state = [
+        pltpu.make_async_copy(kept, held, sems.at[n])
+        for n, (kept, held) in enumerate(((peak_in, peak), (total_in, total), (acc_in, acc)))
+    ]
+    for copy in state:
+        copy.start()
     boxes = (box1, box2, box3)
     cols = iota((24, 128), 1)
     slots = jnp.concatenate([box[:, PAGE_WIDTH:].astype(jnp.float32) for box in boxes], 0)
@@ -404,7 +403,8 @@
         return jnp.concatenate(parts, 0).astype(jnp.bfloat16)
 
     lay_keys(pick, source, keys, REC_BLOCKS)
-
+    for copy in state:
+        copy.wait()
     absorb_blocks(REC_BLOCKS, rec_first, rec_valid, query_rows, keys, peak, total, acc, even, odd)
     for t in range(0, 32, 8):
         parts = []
@@ -428,32 +428,57 @@
             pltpu.VMEM((4, ROWS, 128), jnp.float32),
             pltpu.VMEM((4, ROWS, 128), jnp.float32),
             pltpu.VMEM((4, ROWS, LAT), jnp.float32),
+            pltpu.SemaphoreType.DMA((3,)),
         ],
         compiler_params=pltpu.CompilerParams(vmem_limit_bytes=20 * MIB),
         name="attend_received",
     )(route, *plan, *boxes, own, *state)
 
 
-def product(rows, weight, store):
-    width = PRODUCT_WIDTH
-
-    def part(n, _):
-        lanes = pl.ds(pl.multiple_of(n * width, 128), width)
-        store(lanes, jnp.dot(rows, weight[:, lanes], preferred_element_type=jnp.float32))
-        return 0
-
-    lax.fori_loop(0, weight.shape[1] // width, part, 0, unroll=True)
+def product(rows, weights, store):
+    start = 0
+    for weight in weights:
+        for at in range(0, weight.shape[1], PRODUCT_WIDTH):
+            got = jnp.dot(rows, weight[:, at : at + PRODUCT_WIDTH], preferred_element_type=jnp.float32)
+            store(slice(start + at, start + at + PRODUCT_WIDTH), got)
+        start += weight.shape[1]
 
 
 def store_blocks(outs):
     def store(lanes, got):
         for k, out in enumerate(outs):
-            out[:, lanes] = got[k * 32 : k * 32 + 32].astype(jnp.bfloat16)
+            out[:, lanes] = got[k * 32 : k * 32 + 32].astype(out.dtype)
 
     return store
 
 
-def values_kernel(order, rows, value_up, out_proj, values_out, *theirs):
+def stage_kernel(_after, weight, *refs):
+    staged, sems = refs[:-1], refs[-1]
+    copies, start = [], 0
+    for n, out in enumerate(staged):
+        width = out.shape[1]
+        copies.append(pltpu.make_async_copy(weight.at[:, pl.ds(start, width)], out, sems.at[n]))
+        copies[n].start()
+        start += width
+    for copy in copies:
+        copy.wait()
+
+
+def stage(after, weight):
+    anywhere = pl.BlockSpec(memory_space=pl.ANY)
+    return pl.pallas_call(
+        stage_kernel,
+        out_shape=[jax.ShapeDtypeStruct((weight.shape[0], width), weight.dtype) for width in CUTS],
+        in_specs=[anywhere] * 2,
+        out_specs=[pl.BlockSpec(memory_space=pltpu.VMEM)] * len(CUTS),
+        scratch_shapes=[pltpu.SemaphoreType.DMA((len(CUTS),))],
+        compiler_params=pltpu.CompilerParams(vmem_limit_bytes=4 * MIB),
+        cost_estimate=pl.CostEstimate(flops=4_000_000_000, bytes_accessed=15_000_000, transcendentals=0),
+        name="stage",
+    )(after, weight)
+
+
+def values_kernel(order, rows, value_up, mine, theirs):
     wide = jnp.concatenate([value_up[h] for h in range(4)], 1)
     all_heads = jnp.dot(rows[...], wide, preferred_element_type=jnp.float32)
     at, column = iota((1024, 512), 0), iota((1024, 512), 1)
@@ -463,45 +488,39 @@
     token = (n >> 5) * 8 + ((n >> 3) & 3) * 2 + (n & 1)
     pick = (order[...] == token).astype(jnp.float32).astype(jnp.bfloat16)
     values = jnp.dot(pick, values, preferred_element_type=jnp.float32).astype(jnp.bfloat16)
-    values_out[...] = values[:128]
-    product(values[128:], out_proj, store_blocks(theirs))
-
-
-def project_values(order, rows, value_up, out_proj):
+    mine[...] = values[:128]
+    theirs[...] = values[128:]
+
+
+def find_values(order, rows, value_up):
     vmem = pl.BlockSpec(memory_space=pltpu.VMEM)
-    width = out_proj.shape[1]
     return pl.pallas_call(
         values_kernel,
-        out_shape=[jax.ShapeDtypeStruct((128, 512), jnp.bfloat16)]
-        + [jax.ShapeDtypeStruct((32, width), jnp.bfloat16)] * 4,
-        in_specs=[vmem] * 4,
-        out_specs=[vmem] * 5,
-        compiler_params=pltpu.CompilerParams(vmem_limit_bytes=20 * MIB),
-        cost_estimate=pl.CostEstimate(flops=2_500_000_000, bytes_accessed=12_000_000, transcendentals=0),
+        out_shape=[jax.ShapeDtypeStruct((128, 512), jnp.bfloat16)] * 2,
+        in_specs=[vmem] * 3,
+        out_specs=[vmem] * 2,
+        compiler_params=pltpu.CompilerParams(vmem_limit_bytes=16 * MIB),
+        cost_estimate=pl.CostEstimate(flops=4_000_000_000, bytes_accessed=4_000_000, transcendentals=0),
         name="values",
-    )(order, rows, value_up, out_proj)
-
-
-def project_kernel(rows, weight, *outs):
-    def store(lanes, got):
-        for k, out in enumerate(outs):
-            out[:, lanes] = got[k * 32 : k * 32 + 32]
-
-    product(rows[...], weight, store)
-
-
-def project(rows, weight):
+    )(order, rows, value_up)
+
+
+def project_kernel(rows, *refs):
+    product(rows[...], refs[:-4], store_blocks(refs[-4:]))
+
+
+def project(rows, weights, dtype):
     vmem = pl.BlockSpec(memory_space=pltpu.VMEM)
-    width = weight.shape[1]
+    width = sum(weight.shape[1] for weight in weights)
     return pl.pallas_call(
         project_kernel,
-        out_shape=[jax.ShapeDtypeStruct((32, width), jnp.float32)] * 4,
-        in_specs=[vmem] * 2,
+        out_shape=[jax.ShapeDtypeStruct((32, width), dtype)] * 4,
+        in_specs=[vmem] * (1 + len(weights)),
         out_specs=[vmem] * 4,
         compiler_params=pltpu.CompilerParams(vmem_limit_bytes=16 * MIB),
         cost_estimate=pl.CostEstimate(flops=1_000_000_000, bytes_accessed=11_000_000, transcendentals=0),
         name="project",
-    )(rows, weight)
+    )(rows, *weights)
 
 
 def hidden_kernel(*refs):
@@ -517,7 +536,7 @@
     g = gate[...]
     act = (g / (1.0 + jnp.exp(-g)) * up_part[...]).T.astype(jnp.bfloat16)
     act_out[...] = act[:128]
-    product(act[128:], down_weight, store_blocks(theirs))
+    product(act[128:], [down_weight], store_blocks(theirs))
 
 
 def hidden_units(rows, gate_weight, up_weight, down_weight):
@@ -555,22 +574,22 @@
 ):
     route = ((prefill_owner - lax.axis_index("grp")) & 3) * 16 + prefill_slot
     boxes = outbox(route, prefill_pages)
-    boxes = [
-        lax.ppermute(box, "grp", [(g, (g + k) % 4) for g in range(4)])
-        for k, box in enumerate(boxes, 1)
-    ]
-    *state, slot_row, rec_valid, rec_first, out_proj = attend_resident(
-        page_lists, context_len, queries, fresh_latents, cache_pages, out_proj
+    boxes = {k: lax.ppermute(boxes[k - 1], "grp", [(g, (g + k) % 4) for g in range(4)]) for k in (1, 3, 2)}
+    boxes = [boxes[k] for k in (1, 2, 3)]
+    *state, slot_row, rec_valid, rec_first = attend_resident(
+        page_lists, context_len, queries, fresh_latents, cache_pages
     )
     attended = attend_received(
         route, (slot_row, rec_valid, rec_first), boxes, prefill_pages, state
     )
+    out_proj = stage(attended, out_proj)
     by_heads = lax.all_to_all(attended, "tp", split_axis=0, concat_axis=0, tiled=True)
-    values, *theirs = project_values(token_order()[:, None], by_heads.reshape(1024, LAT), value_up, out_proj)
-    terms = reduce_first(project(values, out_proj), theirs)
+    mine, theirs = find_values(token_order()[:, None], by_heads.reshape(1024, LAT), value_up)
+    theirs = project(theirs, out_proj, jnp.bfloat16)
+    terms = reduce_first(project(mine, out_proj, jnp.float32), theirs)
     hidden, normed = settle(terms, residual, norm_gain)
     act, *theirs = hidden_units(gather_first(normed), gate_weight, up_weight, down_weight)
-    mlp = reduce_second(reduce_first(project(act, down_weight), theirs))
+    mlp = reduce_second(reduce_first(project(act, [down_weight], jnp.float32), theirs))
     return (hidden.astype(jnp.float32) + mlp).astype(jnp.bfloat16)
 
 

time: 155 us -> 154 us (level)
  local copies, waits for them, and re-layouts: 16 us -> 14 us
  starting transfers between devices: 40.3 us -> 38.6 us
  Pallas kernels: 26.8 us -> 28.4 us
    all_to_all x1, waiting for transfers between devices: 14.4 us -> 7.91 us  [shards(): lax.all_to_all(attended, 'tp', split_axis=0, concat_axis=0, tiled=True)]
    ppermute x3, waiting for transfers between devices: 2.29 us -> 8.71 us  [shards(): lax.ppermute(boxes[k - 1], 'grp', [(g, (g + k) % 4) for g in range(4)])]
    unnamed x34 -> x32, local copies, waits for them, and re-layouts: 16 us -> 14 us
    all_to_all x1, starting transfers between devices: 8.29 us -> 6.57 us  [shards(): lax.all_to_all(attended, 'tp', split_axis=0, concat_axis=0, tiled=True)]
    pallas_call x2 -> x3, Pallas kernels: 2.25 us -> 3.35 us  [project(): pl.pallas_call(project_kernel, out_shape=[jax.ShapeDtypeStruct((32, width...]
  transfers between devices with their start and end apart: 31 -> 31, of which waited for: 15 -> 15; matrix products, arithmetic and copies ran while one was open for 0% -> 0% of each run, Pallas kernels for 8% -> 9%
where the time goes in v3:
time: 154 us; the launch traced here: 153 us
  waiting for transfers between devices  68.9 us (45%)
  starting transfers between devices  38.6 us (25%)
  Pallas kernels  28.4 us (18%)
  local copies, waits for them, and re-layouts  14 us (9%)
  other arithmetic  2.33 us (2%)
    ppermute x9, waiting for transfers between devices, along_first(): return lax.ppermute(block, 'tp', chip_pairs((0, k, 0), (k, 0, 0)))  33.1 us
    ppermute x6, waiting for transfers between devices, along_second(): return lax.ppermute(block, 'tp', chip_pairs((k, 0, 0), (0, k, 0)))  17.4 us
    ppermute x9, starting transfers between devices, along_first(): return lax.ppermute(block, 'tp', chip_pairs((0, k, 0), (k, 0, 0)))  14.5 us
    unnamed x32, local copies, waits for them, and re-layouts  14 us
    pallas_call x1, Pallas kernels, attend_resident(): pl.pallas_call(resident_kernel, out_shape=shapes, in_specs=[smem, smem, v...  10.4 us
    ppermute x3, waiting for transfers between devices, shards(): lax.ppermute(boxes[k - 1], 'grp', [(g, (g + k) % 4) for g in range(4)])  8.71 us
    all_to_all x1, waiting for transfers between devices, shards(): lax.all_to_all(attended, 'tp', split_axis=0, concat_axis=0, tiled=True)  7.91 us
    ppermute x6, starting transfers between devices, along_second(): return lax.ppermute(block, 'tp', chip_pairs((k, 0, 0), (0, k, 0)))  7.77 us
  transfers between devices with their start and end apart: 31, of which 15 were waited for; matrix products, arithmetic and copies ran while one was open for 0% of the time, Pallas kernels for 9%

profile of v3, /device:TPU:6, one launch (start us, length us, event | category | flops | bytes accessed | tf_op | source)
XLA Modules:
  0.0 152.6 jit_solution(7337101230618242316)
XLA Ops:
  5.5 3.6 %collective-permute-start.1 = (bf16[8,36992]{1,0:T(8,128)(2,1)S(1)}, bf16[8,36992]{1,0:T(8,128)(2,1)S(1)}, u32[]{:S(2)}, u32[]{:S(2)}) collective-permute-start(bf16[8,36992]{1,0:T(8,128)(2,1)S(1)} %get-tuple-element.44), channel_id=1, source_target_pairs={{0,64},{32,96},{64,0},{96,32},{1,65},{33,97},{65,1},{97,33},{2,66}... | collective-permute-start | bytes 1775624 | tf_op jit(solution)/shard_map/ppermute | solution.py:577
  10.1 2.3 %copy-done.9 = bf16[64,36864]{1,0:T(8,128)(2,1)S(1)} copy-done((bf16[64,36864]{1,0:T(8,128)(2,1)S(1)}, bf16[64,36864]{1,0:T(8,128)(2,1)}, u32[]{:S(2)}) %copy-start.9) | copy-done | bytes 4718616
  15.7 10.4 %attend_resident.1 = (bf16[4,256,576]{2,1,0:T(8,128)(2,1)S(1)}, f32[4,256,128]{2,1,0:T(8,128)S(1)}, f32[4,256,128]{2,1,0:T(8,128)S(1)}, f32[4,256,512]{2,1,0:T(8...) custom-call(s32[4,40]{1,0:T(4,128)S(1)} %copy-done.13, s32[4]{0:T(128)S(1)} %copy-done.14, ...), custom_call_target="tpu_custom_call" | custom-call | flops 8000000000 | bytes 12000000 | tf_op jit(solution)/shard_map/attend_resident/pallas_call | solution.py:354
  26.1 8.7 %collective-permute-done.1.box2 = bf16[8,36992]{1,0:T(8,128)(2,1)S(1)} collective-permute-done((bf16[8,36992]{1,0:T(8,128)(2,1)S(1)}, bf16[8,36992]{1,0:T(8,128)(2,1)S(1)}, u32[]{:S(2)}, u32[]{:S(2)}) %collective-permute-start.1) | collective-permute-done | bytes 591904 | tf_op jit(solution)/shard_map/ppermute | solution.py:577
  34.8 7.0 %attend_received.1._after = bf16[32,32,512]{2,1,0:T(8,128)(2,1)} custom-call(s32[16]{0:T(128)S(1)} %multiply_add_fusion.route, s32[24]{0:T(128)S(1)} %get-tuple-element.40.slot_row, s32[56]{0:T(128)S(1)} %get-tuple-element.41.rec_valid, s32[8]{0:T(128)S(1)} %get-tuple-element.42.rec_first, bf16[8,36992]{1,0:T(8,128)(2,1)S(1)} %collective-permute-done.box1, ...), custom_call_target="tpu_custom_call" | custom-call | tf_op jit(solution)/shard_map/attend_received/pallas_call | solution.py:419
  41.8 6.6 %all-to-all-start = ((bf16[32,32,512]{2,1,0:T(8,128)(2,1)}), bf16[32,32,512]{2,1,0:T(8,128)(2,1)S(1)}, u32[]{:S(2)}, u32[]{:S(2)}) async-start(bf16[32,32,512]{2,1,0:T(8,128)(2,1)} %attend_received.1._after), calls=%async_computation | async-start | bytes 2097152 | tf_op jit(solution)/shard_map/all_to_all | solution.py:586
  48.6 3.1 %copy-done.8 = bf16[512,7168]{1,0:T(8,128)(2,1)S(1)} copy-done((bf16[512,7168]{1,0:T(8,128)(2,1)S(1)}, bf16[512,7168]{1,0:T(8,128)(2,1)}, u32[]{:S(2)}) %copy-start.8) | copy-done | bytes 7340056
  52.7 2.4 %copy-done = bf16[512,5376]{1,0:T(8,128)(2,1)} copy-done((bf16[512,5376]{1,0:T(8,128)(2,1)}, bf16[512,5376]{1,0:T(8,128)(2,1)S(1)}, u32[]{:S(2)}) %copy-start) | copy-done | bytes 5505048
  55.1 7.9 %all-to-all-done = bf16[32,32,512]{2,1,0:T(8,128)(2,1)S(1)} async-done(((bf16[32,32,512]{2,1,0:T(8,128)(2,1)}), bf16[32,32,512]{2,1,0:T(8,128)(2,1)S(1)}, u32[]{:S(2)}, u32[]{:S(2)}) %all-to-all-start) | async-done | bytes 1048608 | tf_op jit(solution)/shard_map/all_to_all | solution.py:586
  70.1 2.0 %collective-permute-start.9 = (bf16[32,7168]{1,0:T(8,128)(2,1)S(1)}, bf16[32,7168]{1,0:T(8,128)(2,1)S(1)}, u32[]{:S(2)}, u32[]{:S(2)}) collective-permute-start(bf16[32,7168]{1,0:T(8,128)(2,1)S(1)} %add_convert_fusion.3), channel_id=1, source_target_pairs={{0,4},{1,17},{2,6},{3,19},{4,0},{5,21},{6,2},{7,23},{8,12},{9,25},... | collective-permute-start | bytes 1376264 | tf_op jit(solution)/shard_map/ppermute | solution.py:50
  73.2 2.5 %collective-permute-start.5 = (bf16[32,7168]{1,0:T(8,128)(2,1)S(1)}, bf16[32,7168]{1,0:T(8,128)(2,1)S(1)}, u32[]{:S(2)}, u32[]{:S(2)}) collective-permute-start(bf16[32,7168]{1,0:T(8,128)(2,1)S(1)} %add_convert_fusion.5), channel_id=1, source_target_pairs={{0,2},{1,9},{2,4},{3,11},{4,6},{5,13},{6,0},{7,15},{8,10},{9,17},{... | collective-permute-start | bytes 1376264 | tf_op jit(solution)/shard_map/ppermute | solution.py:50
  75.7 4.6 %collective-permute-done.9.refs_4_ = bf16[32,7168]{1,0:T(8,128)(2,1)S(1)} collective-permute-done((bf16[32,7168]{1,0:T(8,128)(2,1)S(1)}, bf16[32,7168]{1,0:T(8,128)(2,1)S(1)}, u32[]{:S(2)}, u32[]{:S(2)}) %collective-permute-start.9) | collective-permute-done | bytes 458784 | tf_op jit(solution)/shard_map/ppermute | solution.py:50
  80.2 4.8 %collective-permute-done.7.refs_3_ = bf16[32,7168]{1,0:T(8,128)(2,1)S(1)} collective-permute-done((bf16[32,7168]{1,0:T(8,128)(2,1)S(1)}, bf16[32,7168]{1,0:T(8,128)(2,1)S(1)}, u32[]{:S(2)}, u32[]{:S(2)}) %collective-permute-start.7) | collective-permute-done | bytes 458784 | tf_op jit(solution)/shard_map/ppermute | solution.py:50
  86.0 2.0 %collective-permute-start.11 = (bf16[32,7168]{1,0:T(8,128)(2,1)S(1)}, bf16[32,7168]{1,0:T(8,128)(2,1)S(1)}, u32[]{:S(2)}, u32[]{:S(2)}) collective-permute-start(bf16[32,7168]{1,0:T(8,128)(2,1)S(1)} %get-tuple-element.63), channel_id=1, source_target_pairs={{0,16},{1,5},{2,18},{3,7},{4,20},{5,1},{6,22},{7,3},{8,24},{9,13},... | collective-permute-start | bytes 1376264 | tf_op jit(solution)/shard_map/ppermute | solution.py:54
  88.9 11.0 %collective-permute-done.10.got1 = bf16[32,7168]{1,0:T(8,128)(2,1)S(1)} collective-permute-done((bf16[32,7168]{1,0:T(8,128)(2,1)S(1)}, bf16[32,7168]{1,0:T(8,128)(2,1)S(1)}, u32[]{:S(2)}, u32[]{:S(2)}) %collective-permute-start.10) | collective-permute-done | bytes 458784 | tf_op jit(solution)/shard_map/ppermute | solution.py:54
  101.9 2.9 %collective-permute-start.14 = (bf16[32,7168]{1,0:T(8,128)(2,1)S(1)}, bf16[32,7168]{1,0:T(8,128)(2,1)S(1)}, u32[]{:S(2)}, u32[]{:S(2)}) collective-permute-start(bf16[32,7168]{1,0:T(8,128)(2,1)S(1)} %get-tuple-element.65.refs_0_), channel_id=1, source_target_pairs={{0,4},{1,17},{2,6},{3,19},{4,0},{5,21},{6,2},{7,23},{8,12},{9,25},... | collective-permute-start | bytes 1376264 | tf_op jit(solution)/shard_map/ppermute | solution.py:50
  106.0 5.1 %collective-permute-done.13.refs_1_ = bf16[32,7168]{1,0:T(8,128)(2,1)S(1)} collective-permute-done((bf16[32,7168]{1,0:T(8,128)(2,1)S(1)}, bf16[32,7168]{1,0:T(8,128)(2,1)S(1)}, u32[]{:S(2)}, u32[]{:S(2)}) %collective-permute-start.13) | collective-permute-done | bytes 458784 | tf_op jit(solution)/shard_map/ppermute | solution.py:50
  111.1 5.1 %collective-permute-done.14.refs_2_ = bf16[32,7168]{1,0:T(8,128)(2,1)S(1)} collective-permute-done((bf16[32,7168]{1,0:T(8,128)(2,1)S(1)}, bf16[32,7168]{1,0:T(8,128)(2,1)S(1)}, u32[]{:S(2)}, u32[]{:S(2)}) %collective-permute-start.14) | collective-permute-done | bytes 458784 | tf_op jit(solution)/shard_map/ppermute | solution.py:50
  118.7 3.5 %hidden_units.1 = (bf16[128,288]{1,0:T(8,128)(2,1)S(1)}, bf16[32,7168]{1,0:T(8,128)(2,1)S(1)}, bf16[32,7168]{1,0:T(8,128)(2,1)S(1)}, bf16[32,7168]{1,0:T(8,128)(2,1)S(1)}, bf16[32,7168]{1,0:T(8,128)(2,1)S(1)}) custom-call(bf16[32,7168]{1,0:T(8,128)(2,1)S(1)} %get-tuple-element.65.refs_0_, bf16[32,7168]{1,0:T(8,128)(2,1)S(1)} %collective-permute-done.13.refs_1_, ...), custom_call_target="tpu_custom_call" | custom-call | flops 3000000000 | bytes 18000000 | tf_op jit(solution)/shard_map/hidden_units/pallas_call | solution.py:545
  124.5 2.7 %collective-permute-start.22 = (bf16[32,7168]{1,0:T(8,128)(2,1)S(1)}, bf16[32,7168]{1,0:T(8,128)(2,1)S(1)}, u32[]{:S(2)}, u32[]{:S(2)}) collective-permute-start(bf16[32,7168]{1,0:T(8,128)(2,1)S(1)} %add_convert_fusion.2), channel_id=1, source_target_pairs={{0,2},{1,9},{2,4},{3,11},{4,6},{5,13},{6,0},{7,15},{8,10},{9,17},{... | collective-permute-start | bytes 1376264 | tf_op jit(solution)/shard_map/ppermute | solution.py:50
  129.2 9.0 %collective-permute-done.22 = bf16[32,7168]{1,0:T(8,128)(2,1)S(1)} collective-permute-done((bf16[32,7168]{1,0:T(8,128)(2,1)S(1)}, bf16[32,7168]{1,0:T(8,128)(2,1)S(1)}, u32[]{:S(2)}, u32[]{:S(2)}) %collective-permute-start.22) | collective-permute-done | bytes 458784 | tf_op jit(solution)/shard_map/ppermute | solution.py:50
  138.2 3.8 %collective-permute-done.24 = bf16[32,7168]{1,0:T(8,128)(2,1)S(1)} collective-permute-done((bf16[32,7168]{1,0:T(8,128)(2,1)S(1)}, bf16[32,7168]{1,0:T(8,128)(2,1)S(1)}, u32[]{:S(2)}, u32[]{:S(2)}) %collective-permute-start.24) | collective-permute-done | bytes 458784 | tf_op jit(solution)/shard_map/ppermute | solution.py:50
  142.6 3.0 %collective-permute-start.28 = (bf16[8,7168]{1,0:T(8,128)(2,1)S(1)}, bf16[8,7168]{1,0:T(8,128)(2,1)S(1)}, u32[]{:S(2)}, u32[]{:S(2)}) collective-permute-start(bf16[8,7168]{1,0:T(8,128)(2,1)S(1)} %get-tuple-element.79), channel_id=1, source_target_pairs={{0,24},{1,7},{2,26},{3,1},{4,28},{5,3},{6,30},{7,5},{8,0},{9,15},{... | collective-permute-start | bytes 344072 | tf_op jit(solution)/shard_map/ppermute | solution.py:54
  148.4 3.5 %collective-permute-done.29 = bf16[8,7168]{1,0:T(8,128)(2,1)S(1)} collective-permute-done((bf16[8,7168]{1,0:T(8,128)(2,1)S(1)}, bf16[8,7168]{1,0:T(8,128)(2,1)S(1)}, u32[]{:S(2)}, u32[]{:S(2)}) %collective-permute-start.29) | collective-permute-done | bytes 114720 | tf_op jit(solution)/shard_map/ppermute | solution.py:54
  (93 shorter events, 34.9 us)
Async XLA Ops:
  3.5 22.6 %collective-permute-start = (bf16[8,36992]{1,0:T(8,128)(2,1)S(1)}, bf16[8,36992]{1,0:T(8,128)(2,1)S(1)}, u32[]{:S(2)}, u32[]{:S(2)}) collective-permute-start(bf16[8,36992]{1,0:T(8,128)(2,1)S(1)} %get-tuple-element.43), channel_id=1, source_target_pairs={{0,32},{32,64},{64,96},{96,0},{1,33},{33,65},{65,97},{97,1},{2,34}... | collective-permute-start | bytes 1775624 | tf_op jit(solution)/shard_map/ppermute | solution.py:577
  5.5 29.3 %collective-permute-start.1 = (bf16[8,36992]{1,0:T(8,128)(2,1)S(1)}, bf16[8,36992]{1,0:T(8,128)(2,1)S(1)}, u32[]{:S(2)}, u32[]{:S(2)}) collective-permute-start(bf16[8,36992]{1,0:T(8,128)(2,1)S(1)} %get-tuple-element.44), channel_id=1, source_target_pairs={{0,64},{32,96},{64,0},{96,32},{1,65},{33,97},{65,1},{97,33},{2,66}... | collective-permute-start | bytes 1775624 | tf_op jit(solution)/shard_map/ppermute | solution.py:577
  9.1 25.8 %collective-permute-start.2 = (bf16[8,36992]{1,0:T(8,128)(2,1)S(1)}, bf16[8,36992]{1,0:T(8,128)(2,1)S(1)}, u32[]{:S(2)}, u32[]{:S(2)}) collective-permute-start(bf16[8,36992]{1,0:T(8,128)(2,1)S(1)} %get-tuple-element.45), channel_id=1, source_target_pairs={{0,96},{32,0},{64,32},{96,64},{1,97},{33,1},{65,33},{97,65},{2,98}... | collective-permute-start | bytes 1775624 | tf_op jit(solution)/shard_map/ppermute | solution.py:577
  41.8 21.2 %all-to-all-start = ((bf16[32,32,512]{2,1,0:T(8,128)(2,1)}), bf16[32,32,512]{2,1,0:T(8,128)(2,1)S(1)}, u32[]{:S(2)}, u32[]{:S(2)}) async-start(bf16[32,32,512]{2,1,0:T(8,128)(2,1)} %attend_received.1._after), calls=%async_computation | async-start | bytes 2097152 | tf_op jit(solution)/shard_map/all_to_all | solution.py:586
  68.3 4.8 %collective-permute-start.4 = (bf16[32,7168]{1,0:T(8,128)(2,1)S(1)}, bf16[32,7168]{1,0:T(8,128)(2,1)S(1)}, u32[]{:S(2)}, u32[]{:S(2)}) collective-permute-start(bf16[32,7168]{1,0:T(8,128)(2,1)S(1)} %get-tuple-element.57), channel_id=1, source_target_pairs={{0,1},{1,0},{2,3},{3,2},{4,5},{5,4},{6,7},{7,6},{8,9},{9,8},{10,11... | collective-permute-start | bytes 1376264 | tf_op jit(solution)/shard_map/ppermute | solution.py:46
  68.7 6.9 %collective-permute-start.3 = (bf16[32,7168]{1,0:T(8,128)(2,1)S(1)}, bf16[32,7168]{1,0:T(8,128)(2,1)S(1)}, u32[]{:S(2)}, u32[]{:S(2)}) collective-permute-start(bf16[32,7168]{1,0:T(8,128)(2,1)S(1)} %get-tuple-element.55), channel_id=1, source_target_pairs={{0,1},{1,0},{2,3},{3,2},{4,5},{5,4},{6,7},{7,6},{8,9},{9,8},{10,11... | collective-permute-start | bytes 1376264 | tf_op jit(solution)/shard_map/ppermute | solution.py:46
  70.1 10.2 %collective-permute-start.9 = (bf16[32,7168]{1,0:T(8,128)(2,1)S(1)}, bf16[32,7168]{1,0:T(8,128)(2,1)S(1)}, u32[]{:S(2)}, u32[]{:S(2)}) collective-permute-start(bf16[32,7168]{1,0:T(8,128)(2,1)S(1)} %add_convert_fusion.3), channel_id=1, source_target_pairs={{0,4},{1,17},{2,6},{3,19},{4,0},{5,21},{6,2},{7,23},{8,12},{9,25},... | collective-permute-start | bytes 1376264 | tf_op jit(solution)/shard_map/ppermute | solution.py:50
  72.2 12.8 %collective-permute-start.7 = (bf16[32,7168]{1,0:T(8,128)(2,1)S(1)}, bf16[32,7168]{1,0:T(8,128)(2,1)S(1)}, u32[]{:S(2)}, u32[]{:S(2)}) collective-permute-start(bf16[32,7168]{1,0:T(8,128)(2,1)S(1)} %add_convert_fusion.4), channel_id=1, source_target_pairs={{0,6},{1,25},{2,0},{3,27},{4,2},{5,29},{6,4},{7,31},{8,14},{9,1},{... | collective-permute-start | bytes 1376264 | tf_op jit(solution)/shard_map/ppermute | solution.py:50
  73.2 11.8 %collective-permute-start.5 = (bf16[32,7168]{1,0:T(8,128)(2,1)S(1)}, bf16[32,7168]{1,0:T(8,128)(2,1)S(1)}, u32[]{:S(2)}, u32[]{:S(2)}) collective-permute-start(bf16[32,7168]{1,0:T(8,128)(2,1)S(1)} %add_convert_fusion.5), channel_id=1, source_target_pairs={{0,2},{1,9},{2,4},{3,11},{4,6},{5,13},{6,0},{7,15},{8,10},{9,17},{... | collective-permute-start | bytes 1376264 | tf_op jit(solution)/shard_map/ppermute | solution.py:50
  85.3 14.7 %collective-permute-start.10 = (bf16[32,7168]{1,0:T(8,128)(2,1)S(1)}, bf16[32,7168]{1,0:T(8,128)(2,1)S(1)}, u32[]{:S(2)}, u32[]{:S(2)}) collective-permute-start(bf16[32,7168]{1,0:T(8,128)(2,1)S(1)} %get-tuple-element.63), channel_id=1, source_target_pairs={{0,8},{1,3},{2,10},{3,5},{4,12},{5,7},{6,14},{7,1},{8,16},{9,11},{... | collective-permute-start | bytes 1376264 | tf_op jit(solution)/shard_map/ppermute | solution.py:54
  86.0 14.0 %collective-permute-start.11 = (bf16[32,7168]{1,0:T(8,128)(2,1)S(1)}, bf16[32,7168]{1,0:T(8,128)(2,1)S(1)}, u32[]{:S(2)}, u32[]{:S(2)}) collective-permute-start(bf16[32,7168]{1,0:T(8,128)(2,1)S(1)} %get-tuple-element.63), channel_id=1, source_target_pairs={{0,16},{1,5},{2,18},{3,7},{4,20},{5,1},{6,22},{7,3},{8,24},{9,13},... | collective-permute-start | bytes 1376264 | tf_op jit(solution)/shard_map/ppermute | solution.py:54
  88.0 12.9 %collective-permute-start.12 = (bf16[32,7168]{1,0:T(8,128)(2,1)S(1)}, bf16[32,7168]{1,0:T(8,128)(2,1)S(1)}, u32[]{:S(2)}, u32[]{:S(2)}) collective-permute-start(bf16[32,7168]{1,0:T(8,128)(2,1)S(1)} %get-tuple-element.63), channel_id=1, source_target_pairs={{0,24},{1,7},{2,26},{3,1},{4,28},{5,3},{6,30},{7,5},{8,0},{9,15},{... | collective-permute-start | bytes 1376264 | tf_op jit(solution)/shard_map/ppermute | solution.py:54
  101.3 9.8 %collective-permute-start.13 = (bf16[32,7168]{1,0:T(8,128)(2,1)S(1)}, bf16[32,7168]{1,0:T(8,128)(2,1)S(1)}, u32[]{:S(2)}, u32[]{:S(2)}) collective-permute-start(bf16[32,7168]{1,0:T(8,128)(2,1)S(1)} %get-tuple-element.65.refs_0_), channel_id=1, source_target_pairs={{0,6},{1,25},{2,0},{3,27},{4,2},{5,29},{6,4},{7,31},{8,14},{9,1},{... | collective-permute-start | bytes 1376264 | tf_op jit(solution)/shard_map/ppermute | solution.py:50
  101.9 14.2 %collective-permute-start.14 = (bf16[32,7168]{1,0:T(8,128)(2,1)S(1)}, bf16[32,7168]{1,0:T(8,128)(2,1)S(1)}, u32[]{:S(2)}, u32[]{:S(2)}) collective-permute-start(bf16[32,7168]{1,0:T(8,128)(2,1)S(1)} %get-tuple-element.65.refs_0_), channel_id=1, source_target_pairs={{0,4},{1,17},{2,6},{3,19},{4,0},{5,21},{6,2},{7,23},{8,12},{9,25},... | collective-permute-start | bytes 1376264 | tf_op jit(solution)/shard_map/ppermute | solution.py:50
  104.8 12.1 %collective-permute-start.15 = (bf16[32,7168]{1,0:T(8,128)(2,1)S(1)}, bf16[32,7168]{1,0:T(8,128)(2,1)S(1)}, u32[]{:S(2)}, u32[]{:S(2)}) collective-permute-start(bf16[32,7168]{1,0:T(8,128)(2,1)S(1)} %get-tuple-element.65.refs_0_), channel_id=1, source_target_pairs={{0,2},{1,9},{2,4},{3,11},{4,6},{5,13},{6,0},{7,15},{8,10},{9,17},{... | collective-permute-start | bytes 1376264 | tf_op jit(solution)/shard_map/ppermute | solution.py:50
  106.0 10.9 %collective-permute-start.16 = (bf16[32,7168]{1,0:T(8,128)(2,1)S(1)}, bf16[32,7168]{1,0:T(8,128)(2,1)S(1)}, u32[]{:S(2)}, u32[]{:S(2)}) collective-permute-start(bf16[32,7168]{1,0:T(8,128)(2,1)S(1)} %get-tuple-element.65.refs_0_), channel_id=1, source_target_pairs={{0,1},{1,0},{2,3},{3,2},{4,5},{5,4},{6,7},{7,6},{8,9},{9,8},{10,11... | collective-permute-start | bytes 1376264 | tf_op jit(solution)/shard_map/ppermute | solution.py:46
  111.1 5.8 %collective-permute-start.17 = (bf16[32,7168]{1,0:T(8,128)(2,1)S(1)}, bf16[32,7168]{1,0:T(8,128)(2,1)S(1)}, u32[]{:S(2)}, u32[]{:S(2)}) collective-permute-start(bf16[32,7168]{1,0:T(8,128)(2,1)S(1)} %collective-permute-done.13.refs_1_), channel_id=1, source_target_pairs={{0,1},{1,0},{2,3},{3,2},{4,5},{5,4},{6,7},{7,6},{8,9},{9,8},{10,11... | collective-permute-start | bytes 1376264 | tf_op jit(solution)/shard_map/ppermute | solution.py:46
  122.9 6.2 %collective-permute-start.20 = (bf16[32,7168]{1,0:T(8,128)(2,1)S(1)}, bf16[32,7168]{1,0:T(8,128)(2,1)S(1)}, u32[]{:S(2)}, u32[]{:S(2)}) collective-permute-start(bf16[32,7168]{1,0:T(8,128)(2,1)S(1)} %get-tuple-element.68), channel_id=1, source_target_pairs={{0,1},{1,0},{2,3},{3,2},{4,5},{5,4},{6,7},{7,6},{8,9},{9,8},{10,11... | collective-permute-start | bytes 1376264 | tf_op jit(solution)/shard_map/ppermute | solution.py:46
  124.5 13.7 %collective-permute-start.22 = (bf16[32,7168]{1,0:T(8,128)(2,1)S(1)}, bf16[32,7168]{1,0:T(8,128)(2,1)S(1)}, u32[]{:S(2)}, u32[]{:S(2)}) collective-permute-start(bf16[32,7168]{1,0:T(8,128)(2,1)S(1)} %add_convert_fusion.2), channel_id=1, source_target_pairs={{0,2},{1,9},{2,4},{3,11},{4,6},{5,13},{6,0},{7,15},{8,10},{9,17},{... | collective-permute-start | bytes 1376264 | tf_op jit(solution)/shard_map/ppermute | solution.py:50
  127.3 14.7 %collective-permute-start.24 = (bf16[32,7168]{1,0:T(8,128)(2,1)S(1)}, bf16[32,7168]{1,0:T(8,128)(2,1)S(1)}, u32[]{:S(2)}, u32[]{:S(2)}) collective-permute-start(bf16[32,7168]{1,0:T(8,128)(2,1)S(1)} %add_convert_fusion.1), channel_id=1, source_target_pairs={{0,6},{1,25},{2,0},{3,27},{4,2},{5,29},{6,4},{7,31},{8,14},{9,1},{... | collective-permute-start | bytes 1376264 | tf_op jit(solution)/shard_map/ppermute | solution.py:50
  127.5 14.5 %collective-permute-start.26 = (bf16[32,7168]{1,0:T(8,128)(2,1)S(1)}, bf16[32,7168]{1,0:T(8,128)(2,1)S(1)}, u32[]{:S(2)}, u32[]{:S(2)}) collective-permute-start(bf16[32,7168]{1,0:T(8,128)(2,1)S(1)} %add_convert_fusion), channel_id=1, source_target_pairs={{0,4},{1,17},{2,6},{3,19},{4,0},{5,21},{6,2},{7,23},{8,12},{9,25},... | collective-permute-start | bytes 1376264 | tf_op jit(solution)/shard_map/ppermute | solution.py:50
  142.3 6.1 %collective-permute-start.27 = (bf16[8,7168]{1,0:T(8,128)(2,1)S(1)}, bf16[8,7168]{1,0:T(8,128)(2,1)S(1)}, u32[]{:S(2)}, u32[]{:S(2)}) collective-permute-start(bf16[8,7168]{1,0:T(8,128)(2,1)S(1)} %get-tuple-element.77), channel_id=1, source_target_pairs={{0,8},{1,3},{2,10},{3,5},{4,12},{5,7},{6,14},{7,1},{8,16},{9,11},{... | collective-permute-start | bytes 344072 | tf_op jit(solution)/shard_map/ppermute | solution.py:54
  142.6 5.8 %collective-permute-start.28 = (bf16[8,7168]{1,0:T(8,128)(2,1)S(1)}, bf16[8,7168]{1,0:T(8,128)(2,1)S(1)}, u32[]{:S(2)}, u32[]{:S(2)}) collective-permute-start(bf16[8,7168]{1,0:T(8,128)(2,1)S(1)} %get-tuple-element.79), channel_id=1, source_target_pairs={{0,24},{1,7},{2,26},{3,1},{4,28},{5,3},{6,30},{7,5},{8,0},{9,15},{... | collective-permute-start | bytes 344072 | tf_op jit(solution)/shard_map/ppermute | solution.py:54
  145.6 6.3 %collective-permute-start.29 = (bf16[8,7168]{1,0:T(8,128)(2,1)S(1)}, bf16[8,7168]{1,0:T(8,128)(2,1)S(1)}, u32[]{:S(2)}, u32[]{:S(2)}) collective-permute-start(bf16[8,7168]{1,0:T(8,128)(2,1)S(1)} %get-tuple-element.78), channel_id=1, source_target_pairs={{0,16},{1,5},{2,18},{3,7},{4,20},{5,1},{6,22},{7,3},{8,24},{9,13},... | collective-permute-start | bytes 344072 | tf_op jit(solution)/shard_map/ppermute | solution.py:54
  (23 other events, 251.7 us)

commit v4 on v3

--- a/solution.py
+++ b/solution.py
@@ -73,9 +73,9 @@
 
 
 def reduce_first(mine, theirs):
-    got = {k: swap_cores(theirs[k]) for k in (1, 3, 2, 0)}
-    chunks = {k: add_up(mine[k], [got[k]]).astype(jnp.bfloat16) for k in (1, 3, 2)}
-    return [mine[0], got[0]] + [along_first(chunks[k], k) for k in (1, 3, 2)]
+    got = {k: swap_cores(theirs[k]) for k in (2, 1, 3, 0)}
+    chunks = {k: add_up(mine[k], [got[k]]).astype(jnp.bfloat16) for k in (2, 1, 3)}
+    return [mine[0], got[0]] + [along_first(chunks[k], k) for k in (2, 1, 3)]
 
 
 def reduce_second(terms):
@@ -146,7 +146,7 @@
 
 
 def gather_first(rows):
-    arrived = {k: along_first(rows, 4 - k) for k in (1, 3, 2)}
+    arrived = {k: along_first(rows, 4 - k) for k in (2, 1, 3)}
     mine = [rows] + [arrived[k] for k in (1, 2, 3)]
     return mine + [swap_cores(part) for part in mine]
 

time: 154 us -> 153 us (level)
    ppermute x9, starting transfers between devices: 14.5 us -> 11.7 us  [along_first(): return lax.ppermute(block, 'tp', chip_pairs((0, k, 0), (k, 0, 0)))]
  transfers between devices with their start and end apart: 31 -> 31, of which waited for: 15 -> 16; matrix products, arithmetic and copies ran while one was open for 0% -> 0% of each run, Pallas kernels for 9% -> 9%
where the time goes in v4:
time: 153 us; the launch traced here: 151 us
  waiting for transfers between devices  69.8 us (46%)
  starting transfers between devices  37.5 us (25%)
  Pallas kernels  27.3 us (18%)
  local copies, waits for them, and re-layouts  14 us (9%)
  other arithmetic  2.32 us (2%)
    ppermute x9, waiting for transfers between devices, along_first(): return lax.ppermute(block, 'tp', chip_pairs((0, k, 0), (k, 0, 0)))  33.8 us
    ppermute x6, waiting for transfers between devices, along_second(): return lax.ppermute(block, 'tp', chip_pairs((k, 0, 0), (0, k, 0)))  17.2 us
    unnamed x32, local copies, waits for them, and re-layouts  14 us
    ppermute x9, starting transfers between devices, along_first(): return lax.ppermute(block, 'tp', chip_pairs((0, k, 0), (k, 0, 0)))  11.7 us
    pallas_call x1, Pallas kernels, attend_resident(): pl.pallas_call(resident_kernel, out_shape=shapes, in_specs=[smem, smem, v...  10.3 us
    ppermute x3, waiting for transfers between devices, shards(): lax.ppermute(boxes[k - 1], 'grp', [(g, (g + k) % 4) for g in range(4)])  8.85 us
    ppermute x6, starting transfers between devices, along_second(): return lax.ppermute(block, 'tp', chip_pairs((k, 0, 0), (0, k, 0)))  7.97 us
    all_to_all x1, waiting for transfers between devices, shards(): lax.all_to_all(attended, 'tp', split_axis=0, concat_axis=0, tiled=True)  7.91 us
  transfers between devices with their start and end apart: 31, of which 16 were waited for; matrix products, arithmetic and copies ran while one was open for 0% of the time, Pallas kernels for 9%

profile of v4, /device:TPU:6, one launch (start us, length us, event | category | flops | bytes accessed | tf_op | source)
XLA Modules:
  0.0 151.2 jit_solution(10771126116037773205)
XLA Ops:
  3.5 2.0 %collective-permute-start = (bf16[8,36992]{1,0:T(8,128)(2,1)S(1)}, bf16[8,36992]{1,0:T(8,128)(2,1)S(1)}, u32[]{:S(2)}, u32[]{:S(2)}) collective-permute-start(bf16[8,36992]{1,0:T(8,128)(2,1)S(1)} %get-tuple-element.43), channel_id=1, source_target_pairs={{0,32},{32,64},{64,96},{96,0},{1,33},{33,65},{65,97},{97,1},{2,34}... | collective-permute-start | bytes 1775624 | tf_op jit(solution)/shard_map/ppermute | solution.py:577
  5.5 3.6 %collective-permute-start.1 = (bf16[8,36992]{1,0:T(8,128)(2,1)S(1)}, bf16[8,36992]{1,0:T(8,128)(2,1)S(1)}, u32[]{:S(2)}, u32[]{:S(2)}) collective-permute-start(bf16[8,36992]{1,0:T(8,128)(2,1)S(1)} %get-tuple-element.44), channel_id=1, source_target_pairs={{0,64},{32,96},{64,0},{96,32},{1,65},{33,97},{65,1},{97,33},{2,66}... | collective-permute-start | bytes 1775624 | tf_op jit(solution)/shard_map/ppermute | solution.py:577
  10.1 2.3 %copy-done.9 = bf16[64,36864]{1,0:T(8,128)(2,1)S(1)} copy-done((bf16[64,36864]{1,0:T(8,128)(2,1)S(1)}, bf16[64,36864]{1,0:T(8,128)(2,1)}, u32[]{:S(2)}) %copy-start.9) | copy-done | bytes 4718616
  15.7 10.3 %attend_resident.1 = (bf16[4,256,576]{2,1,0:T(8,128)(2,1)S(1)}, f32[4,256,128]{2,1,0:T(8,128)S(1)}, f32[4,256,128]{2,1,0:T(8,128)S(1)}, f32[4,256,512]{2,1,0:T(8...) custom-call(s32[4,40]{1,0:T(4,128)S(1)} %copy-done.13, s32[4]{0:T(128)S(1)} %copy-done.14, ...), custom_call_target="tpu_custom_call" | custom-call | flops 8000000000 | bytes 12000000 | tf_op jit(solution)/shard_map/attend_resident/pallas_call | solution.py:354
  26.0 8.8 %collective-permute-done.1.box2 = bf16[8,36992]{1,0:T(8,128)(2,1)S(1)} collective-permute-done((bf16[8,36992]{1,0:T(8,128)(2,1)S(1)}, bf16[8,36992]{1,0:T(8,128)(2,1)S(1)}, u32[]{:S(2)}, u32[]{:S(2)}) %collective-permute-start.1) | collective-permute-done | bytes 591904 | tf_op jit(solution)/shard_map/ppermute | solution.py:577
  34.8 6.0 %attend_received.1._after = bf16[32,32,512]{2,1,0:T(8,128)(2,1)} custom-call(s32[16]{0:T(128)S(1)} %multiply_add_fusion.route, s32[24]{0:T(128)S(1)} %get-tuple-element.40.slot_row, s32[56]{0:T(128)S(1)} %get-tuple-element.41.rec_valid, s32[8]{0:T(128)S(1)} %get-tuple-element.42.rec_first, bf16[8,36992]{1,0:T(8,128)(2,1)S(1)} %collective-permute-done.box1, ...), custom_call_target="tpu_custom_call" | custom-call | tf_op jit(solution)/shard_map/attend_received/pallas_call | solution.py:419
  40.8 7.6 %all-to-all-start = ((bf16[32,32,512]{2,1,0:T(8,128)(2,1)}), bf16[32,32,512]{2,1,0:T(8,128)(2,1)S(1)}, u32[]{:S(2)}, u32[]{:S(2)}) async-start(bf16[32,32,512]{2,1,0:T(8,128)(2,1)} %attend_received.1._after), calls=%async_computation | async-start | bytes 2097152 | tf_op jit(solution)/shard_map/all_to_all | solution.py:586
  48.6 3.1 %copy-done.8 = bf16[512,7168]{1,0:T(8,128)(2,1)S(1)} copy-done((bf16[512,7168]{1,0:T(8,128)(2,1)S(1)}, bf16[512,7168]{1,0:T(8,128)(2,1)}, u32[]{:S(2)}) %copy-start.8) | copy-done | bytes 7340056
  52.7 2.4 %copy-done = bf16[512,5376]{1,0:T(8,128)(2,1)} copy-done((bf16[512,5376]{1,0:T(8,128)(2,1)}, bf16[512,5376]{1,0:T(8,128)(2,1)S(1)}, u32[]{:S(2)}) %copy-start) | copy-done | bytes 5505048
  55.1 7.9 %all-to-all-done = bf16[32,32,512]{2,1,0:T(8,128)(2,1)S(1)} async-done(((bf16[32,32,512]{2,1,0:T(8,128)(2,1)}), bf16[32,32,512]{2,1,0:T(8,128)(2,1)S(1)}, u32[]{:S(2)}, u32[]{:S(2)}) %all-to-all-start) | async-done | bytes 1048608 | tf_op jit(solution)/shard_map/all_to_all | solution.py:586
  70.8 2.8 %collective-permute-start.7 = (bf16[32,7168]{1,0:T(8,128)(2,1)S(1)}, bf16[32,7168]{1,0:T(8,128)(2,1)S(1)}, u32[]{:S(2)}, u32[]{:S(2)}) collective-permute-start(bf16[32,7168]{1,0:T(8,128)(2,1)S(1)} %add_convert_fusion.4), channel_id=1, source_target_pairs={{0,2},{1,9},{2,4},{3,11},{4,6},{5,13},{6,0},{7,15},{8,10},{9,17},{... | collective-permute-start | bytes 1376264 | tf_op jit(solution)/shard_map/ppermute | solution.py:50
  74.4 5.4 %collective-permute-done.9.refs_4_ = bf16[32,7168]{1,0:T(8,128)(2,1)S(1)} collective-permute-done((bf16[32,7168]{1,0:T(8,128)(2,1)S(1)}, bf16[32,7168]{1,0:T(8,128)(2,1)S(1)}, u32[]{:S(2)}, u32[]{:S(2)}) %collective-permute-start.9) | collective-permute-done | bytes 458784 | tf_op jit(solution)/shard_map/ppermute | solution.py:50
  79.8 4.7 %collective-permute-done.7.refs_3_ = bf16[32,7168]{1,0:T(8,128)(2,1)S(1)} collective-permute-done((bf16[32,7168]{1,0:T(8,128)(2,1)S(1)}, bf16[32,7168]{1,0:T(8,128)(2,1)S(1)}, u32[]{:S(2)}, u32[]{:S(2)}) %collective-permute-start.7) | collective-permute-done | bytes 458784 | tf_op jit(solution)/shard_map/ppermute | solution.py:50
  85.7 2.0 %collective-permute-start.11 = (bf16[32,7168]{1,0:T(8,128)(2,1)S(1)}, bf16[32,7168]{1,0:T(8,128)(2,1)S(1)}, u32[]{:S(2)}, u32[]{:S(2)}) collective-permute-start(bf16[32,7168]{1,0:T(8,128)(2,1)S(1)} %get-tuple-element.63), channel_id=1, source_target_pairs={{0,16},{1,5},{2,18},{3,7},{4,20},{5,1},{6,22},{7,3},{8,24},{9,13},... | collective-permute-start | bytes 1376264 | tf_op jit(solution)/shard_map/ppermute | solution.py:54
  88.9 11.0 %collective-permute-done.10.got1 = bf16[32,7168]{1,0:T(8,128)(2,1)S(1)} collective-permute-done((bf16[32,7168]{1,0:T(8,128)(2,1)S(1)}, bf16[32,7168]{1,0:T(8,128)(2,1)S(1)}, u32[]{:S(2)}, u32[]{:S(2)}) %collective-permute-start.10) | collective-permute-done | bytes 458784 | tf_op jit(solution)/shard_map/ppermute | solution.py:54
  102.8 3.1 %collective-permute-start.14 = (bf16[32,7168]{1,0:T(8,128)(2,1)S(1)}, bf16[32,7168]{1,0:T(8,128)(2,1)S(1)}, u32[]{:S(2)}, u32[]{:S(2)}) collective-permute-start(bf16[32,7168]{1,0:T(8,128)(2,1)S(1)} %get-tuple-element.65.refs_0_), channel_id=1, source_target_pairs={{0,4},{1,17},{2,6},{3,19},{4,0},{5,21},{6,2},{7,23},{8,12},{9,25},... | collective-permute-start | bytes 1376264 | tf_op jit(solution)/shard_map/ppermute | solution.py:50
  105.9 5.0 %collective-permute-done.13.refs_1_ = bf16[32,7168]{1,0:T(8,128)(2,1)S(1)} collective-permute-done((bf16[32,7168]{1,0:T(8,128)(2,1)S(1)}, bf16[32,7168]{1,0:T(8,128)(2,1)S(1)}, u32[]{:S(2)}, u32[]{:S(2)}) %collective-permute-start.13) | collective-permute-done | bytes 458784 | tf_op jit(solution)/shard_map/ppermute | solution.py:50
  110.9 6.3 %collective-permute-done.14.refs_2_ = bf16[32,7168]{1,0:T(8,128)(2,1)S(1)} collective-permute-done((bf16[32,7168]{1,0:T(8,128)(2,1)S(1)}, bf16[32,7168]{1,0:T(8,128)(2,1)S(1)}, u32[]{:S(2)}, u32[]{:S(2)}) %collective-permute-start.14) | collective-permute-done | bytes 458784 | tf_op jit(solution)/shard_map/ppermute | solution.py:50
  119.8 3.5 %hidden_units.1 = (bf16[128,288]{1,0:T(8,128)(2,1)S(1)}, bf16[32,7168]{1,0:T(8,128)(2,1)S(1)}, bf16[32,7168]{1,0:T(8,128)(2,1)S(1)}, bf16[32,7168]{1,0:T(8,128)(2,1)S(1)}, bf16[32,7168]{1,0:T(8,128)(2,1)S(1)}) custom-call(bf16[32,7168]{1,0:T(8,128)(2,1)S(1)} %get-tuple-element.65.refs_0_, bf16[32,7168]{1,0:T(8,128)(2,1)S(1)} %collective-permute-done.13.refs_1_, ...), custom_call_target="tpu_custom_call" | custom-call | flops 3000000000 | bytes 18000000 | tf_op jit(solution)/shard_map/hidden_units/pallas_call | solution.py:545
  126.3 2.1 %collective-permute-start.24 = (bf16[32,7168]{1,0:T(8,128)(2,1)S(1)}, bf16[32,7168]{1,0:T(8,128)(2,1)S(1)}, u32[]{:S(2)}, u32[]{:S(2)}) collective-permute-start(bf16[32,7168]{1,0:T(8,128)(2,1)S(1)} %add_convert_fusion.1), channel_id=1, source_target_pairs={{0,2},{1,9},{2,4},{3,11},{4,6},{5,13},{6,0},{7,15},{8,10},{9,17},{... | collective-permute-start | bytes 1376264 | tf_op jit(solution)/shard_map/ppermute | solution.py:50
  128.6 7.2 %collective-permute-done.22 = bf16[32,7168]{1,0:T(8,128)(2,1)S(1)} collective-permute-done((bf16[32,7168]{1,0:T(8,128)(2,1)S(1)}, bf16[32,7168]{1,0:T(8,128)(2,1)S(1)}, u32[]{:S(2)}, u32[]{:S(2)}) %collective-permute-start.22) | collective-permute-done | bytes 458784 | tf_op jit(solution)/shard_map/ppermute | solution.py:50
  135.8 3.7 %collective-permute-done.24 = bf16[32,7168]{1,0:T(8,128)(2,1)S(1)} collective-permute-done((bf16[32,7168]{1,0:T(8,128)(2,1)S(1)}, bf16[32,7168]{1,0:T(8,128)(2,1)S(1)}, u32[]{:S(2)}, u32[]{:S(2)}) %collective-permute-start.24) | collective-permute-done | bytes 458784 | tf_op jit(solution)/shard_map/ppermute | solution.py:50
  141.2 3.0 %collective-permute-start.28 = (bf16[8,7168]{1,0:T(8,128)(2,1)S(1)}, bf16[8,7168]{1,0:T(8,128)(2,1)S(1)}, u32[]{:S(2)}, u32[]{:S(2)}) collective-permute-start(bf16[8,7168]{1,0:T(8,128)(2,1)S(1)} %get-tuple-element.79), channel_id=1, source_target_pairs={{0,24},{1,7},{2,26},{3,1},{4,28},{5,3},{6,30},{7,5},{8,0},{9,15},{... | collective-permute-start | bytes 344072 | tf_op jit(solution)/shard_map/ppermute | solution.py:54
  147.0 3.5 %collective-permute-done.29 = bf16[8,7168]{1,0:T(8,128)(2,1)S(1)} collective-permute-done((bf16[8,7168]{1,0:T(8,128)(2,1)S(1)}, bf16[8,7168]{1,0:T(8,128)(2,1)S(1)}, u32[]{:S(2)}, u32[]{:S(2)}) %collective-permute-start.29) | collective-permute-done | bytes 114720 | tf_op jit(solution)/shard_map/ppermute | solution.py:54
  (93 shorter events, 33.8 us)
Async XLA Ops:
  3.5 22.5 %collective-permute-start = (bf16[8,36992]{1,0:T(8,128)(2,1)S(1)}, bf16[8,36992]{1,0:T(8,128)(2,1)S(1)}, u32[]{:S(2)}, u32[]{:S(2)}) collective-permute-start(bf16[8,36992]{1,0:T(8,128)(2,1)S(1)} %get-tuple-element.43), channel_id=1, source_target_pairs={{0,32},{32,64},{64,96},{96,0},{1,33},{33,65},{65,97},{97,1},{2,34}... | collective-permute-start | bytes 1775624 | tf_op jit(solution)/shard_map/ppermute | solution.py:577
  5.5 29.3 %collective-permute-start.1 = (bf16[8,36992]{1,0:T(8,128)(2,1)S(1)}, bf16[8,36992]{1,0:T(8,128)(2,1)S(1)}, u32[]{:S(2)}, u32[]{:S(2)}) collective-permute-start(bf16[8,36992]{1,0:T(8,128)(2,1)S(1)} %get-tuple-element.44), channel_id=1, source_target_pairs={{0,64},{32,96},{64,0},{96,32},{1,65},{33,97},{65,1},{97,33},{2,66}... | collective-permute-start | bytes 1775624 | tf_op jit(solution)/shard_map/ppermute | solution.py:577
  9.1 25.8 %collective-permute-start.2 = (bf16[8,36992]{1,0:T(8,128)(2,1)S(1)}, bf16[8,36992]{1,0:T(8,128)(2,1)S(1)}, u32[]{:S(2)}, u32[]{:S(2)}) collective-permute-start(bf16[8,36992]{1,0:T(8,128)(2,1)S(1)} %get-tuple-element.45), channel_id=1, source_target_pairs={{0,96},{32,0},{64,32},{96,64},{1,97},{33,1},{65,33},{97,65},{2,98}... | collective-permute-start | bytes 1775624 | tf_op jit(solution)/shard_map/ppermute | solution.py:577
  40.8 22.2 %all-to-all-start = ((bf16[32,32,512]{2,1,0:T(8,128)(2,1)}), bf16[32,32,512]{2,1,0:T(8,128)(2,1)S(1)}, u32[]{:S(2)}, u32[]{:S(2)}) async-start(bf16[32,32,512]{2,1,0:T(8,128)(2,1)} %attend_received.1._after), calls=%async_computation | async-start | bytes 2097152 | tf_op jit(solution)/shard_map/all_to_all | solution.py:586
  68.3 5.2 %collective-permute-start.4 = (bf16[32,7168]{1,0:T(8,128)(2,1)S(1)}, bf16[32,7168]{1,0:T(8,128)(2,1)S(1)}, u32[]{:S(2)}, u32[]{:S(2)}) collective-permute-start(bf16[32,7168]{1,0:T(8,128)(2,1)S(1)} %get-tuple-element.57), channel_id=1, source_target_pairs={{0,1},{1,0},{2,3},{3,2},{4,5},{5,4},{6,7},{7,6},{8,9},{9,8},{10,11... | collective-permute-start | bytes 1376264 | tf_op jit(solution)/shard_map/ppermute | solution.py:46
  68.7 5.7 %collective-permute-start.3 = (bf16[32,7168]{1,0:T(8,128)(2,1)S(1)}, bf16[32,7168]{1,0:T(8,128)(2,1)S(1)}, u32[]{:S(2)}, u32[]{:S(2)}) collective-permute-start(bf16[32,7168]{1,0:T(8,128)(2,1)S(1)} %get-tuple-element.55), channel_id=1, source_target_pairs={{0,1},{1,0},{2,3},{3,2},{4,5},{5,4},{6,7},{7,6},{8,9},{9,8},{10,11... | collective-permute-start | bytes 1376264 | tf_op jit(solution)/shard_map/ppermute | solution.py:46
  70.1 9.8 %collective-permute-start.9 = (bf16[32,7168]{1,0:T(8,128)(2,1)S(1)}, bf16[32,7168]{1,0:T(8,128)(2,1)S(1)}, u32[]{:S(2)}, u32[]{:S(2)}) collective-permute-start(bf16[32,7168]{1,0:T(8,128)(2,1)S(1)} %add_convert_fusion.3), channel_id=1, source_target_pairs={{0,6},{1,25},{2,0},{3,27},{4,2},{5,29},{6,4},{7,31},{8,14},{9,1},{... | collective-permute-start | bytes 1376264 | tf_op jit(solution)/shard_map/ppermute | solution.py:50
  70.8 13.7 %collective-permute-start.7 = (bf16[32,7168]{1,0:T(8,128)(2,1)S(1)}, bf16[32,7168]{1,0:T(8,128)(2,1)S(1)}, u32[]{:S(2)}, u32[]{:S(2)}) collective-permute-start(bf16[32,7168]{1,0:T(8,128)(2,1)S(1)} %add_convert_fusion.4), channel_id=1, source_target_pairs={{0,2},{1,9},{2,4},{3,11},{4,6},{5,13},{6,0},{7,15},{8,10},{9,17},{... | collective-permute-start | bytes 1376264 | tf_op jit(solution)/shard_map/ppermute | solution.py:50
  73.6 11.3 %collective-permute-start.5 = (bf16[32,7168]{1,0:T(8,128)(2,1)S(1)}, bf16[32,7168]{1,0:T(8,128)(2,1)S(1)}, u32[]{:S(2)}, u32[]{:S(2)}) collective-permute-start(bf16[32,7168]{1,0:T(8,128)(2,1)S(1)} %add_convert_fusion.5), channel_id=1, source_target_pairs={{0,4},{1,17},{2,6},{3,19},{4,0},{5,21},{6,2},{7,23},{8,12},{9,25},... | collective-permute-start | bytes 1376264 | tf_op jit(solution)/shard_map/ppermute | solution.py:50
  85.2 14.7 %collective-permute-start.10 = (bf16[32,7168]{1,0:T(8,128)(2,1)S(1)}, bf16[32,7168]{1,0:T(8,128)(2,1)S(1)}, u32[]{:S(2)}, u32[]{:S(2)}) collective-permute-start(bf16[32,7168]{1,0:T(8,128)(2,1)S(1)} %get-tuple-element.63), channel_id=1, source_target_pairs={{0,8},{1,3},{2,10},{3,5},{4,12},{5,7},{6,14},{7,1},{8,16},{9,11},{... | collective-permute-start | bytes 1376264 | tf_op jit(solution)/shard_map/ppermute | solution.py:54
  85.7 14.2 %collective-permute-start.11 = (bf16[32,7168]{1,0:T(8,128)(2,1)S(1)}, bf16[32,7168]{1,0:T(8,128)(2,1)S(1)}, u32[]{:S(2)}, u32[]{:S(2)}) collective-permute-start(bf16[32,7168]{1,0:T(8,128)(2,1)S(1)} %get-tuple-element.63), channel_id=1, source_target_pairs={{0,16},{1,5},{2,18},{3,7},{4,20},{5,1},{6,22},{7,3},{8,24},{9,13},... | collective-permute-start | bytes 1376264 | tf_op jit(solution)/shard_map/ppermute | solution.py:54
  87.7 13.1 %collective-permute-start.12 = (bf16[32,7168]{1,0:T(8,128)(2,1)S(1)}, bf16[32,7168]{1,0:T(8,128)(2,1)S(1)}, u32[]{:S(2)}, u32[]{:S(2)}) collective-permute-start(bf16[32,7168]{1,0:T(8,128)(2,1)S(1)} %get-tuple-element.63), channel_id=1, source_target_pairs={{0,24},{1,7},{2,26},{3,1},{4,28},{5,3},{6,30},{7,5},{8,0},{9,15},{... | collective-permute-start | bytes 1376264 | tf_op jit(solution)/shard_map/ppermute | solution.py:54
  101.2 9.8 %collective-permute-start.13 = (bf16[32,7168]{1,0:T(8,128)(2,1)S(1)}, bf16[32,7168]{1,0:T(8,128)(2,1)S(1)}, u32[]{:S(2)}, u32[]{:S(2)}) collective-permute-start(bf16[32,7168]{1,0:T(8,128)(2,1)S(1)} %get-tuple-element.65.refs_0_), channel_id=1, source_target_pairs={{0,6},{1,25},{2,0},{3,27},{4,2},{5,29},{6,4},{7,31},{8,14},{9,1},{... | collective-permute-start | bytes 1376264 | tf_op jit(solution)/shard_map/ppermute | solution.py:50
  102.8 14.5 %collective-permute-start.14 = (bf16[32,7168]{1,0:T(8,128)(2,1)S(1)}, bf16[32,7168]{1,0:T(8,128)(2,1)S(1)}, u32[]{:S(2)}, u32[]{:S(2)}) collective-permute-start(bf16[32,7168]{1,0:T(8,128)(2,1)S(1)} %get-tuple-element.65.refs_0_), channel_id=1, source_target_pairs={{0,4},{1,17},{2,6},{3,19},{4,0},{5,21},{6,2},{7,23},{8,12},{9,25},... | collective-permute-start | bytes 1376264 | tf_op jit(solution)/shard_map/ppermute | solution.py:50
  105.9 11.4 %collective-permute-start.15 = (bf16[32,7168]{1,0:T(8,128)(2,1)S(1)}, bf16[32,7168]{1,0:T(8,128)(2,1)S(1)}, u32[]{:S(2)}, u32[]{:S(2)}) collective-permute-start(bf16[32,7168]{1,0:T(8,128)(2,1)S(1)} %get-tuple-element.65.refs_0_), channel_id=1, source_target_pairs={{0,2},{1,9},{2,4},{3,11},{4,6},{5,13},{6,0},{7,15},{8,10},{9,17},{... | collective-permute-start | bytes 1376264 | tf_op jit(solution)/shard_map/ppermute | solution.py:50
  105.9 11.9 %collective-permute-start.16 = (bf16[32,7168]{1,0:T(8,128)(2,1)S(1)}, bf16[32,7168]{1,0:T(8,128)(2,1)S(1)}, u32[]{:S(2)}, u32[]{:S(2)}) collective-permute-start(bf16[32,7168]{1,0:T(8,128)(2,1)S(1)} %get-tuple-element.65.refs_0_), channel_id=1, source_target_pairs={{0,1},{1,0},{2,3},{3,2},{4,5},{5,4},{6,7},{7,6},{8,9},{9,8},{10,11... | collective-permute-start | bytes 1376264 | tf_op jit(solution)/shard_map/ppermute | solution.py:46
  110.9 6.9 %collective-permute-start.17 = (bf16[32,7168]{1,0:T(8,128)(2,1)S(1)}, bf16[32,7168]{1,0:T(8,128)(2,1)S(1)}, u32[]{:S(2)}, u32[]{:S(2)}) collective-permute-start(bf16[32,7168]{1,0:T(8,128)(2,1)S(1)} %collective-permute-done.13.refs_1_), channel_id=1, source_target_pairs={{0,1},{1,0},{2,3},{3,2},{4,5},{5,4},{6,7},{7,6},{8,9},{9,8},{10,11... | collective-permute-start | bytes 1376264 | tf_op jit(solution)/shard_map/ppermute | solution.py:46
  124.0 4.6 %collective-permute-start.20 = (bf16[32,7168]{1,0:T(8,128)(2,1)S(1)}, bf16[32,7168]{1,0:T(8,128)(2,1)S(1)}, u32[]{:S(2)}, u32[]{:S(2)}) collective-permute-start(bf16[32,7168]{1,0:T(8,128)(2,1)S(1)} %get-tuple-element.68), channel_id=1, source_target_pairs={{0,1},{1,0},{2,3},{3,2},{4,5},{5,4},{6,7},{7,6},{8,9},{9,8},{10,11... | collective-permute-start | bytes 1376264 | tf_op jit(solution)/shard_map/ppermute | solution.py:46
  125.6 10.2 %collective-permute-start.22 = (bf16[32,7168]{1,0:T(8,128)(2,1)S(1)}, bf16[32,7168]{1,0:T(8,128)(2,1)S(1)}, u32[]{:S(2)}, u32[]{:S(2)}) collective-permute-start(bf16[32,7168]{1,0:T(8,128)(2,1)S(1)} %add_convert_fusion.2), channel_id=1, source_target_pairs={{0,4},{1,17},{2,6},{3,19},{4,0},{5,21},{6,2},{7,23},{8,12},{9,25},... | collective-permute-start | bytes 1376264 | tf_op jit(solution)/shard_map/ppermute | solution.py:50
  126.3 13.2 %collective-permute-start.24 = (bf16[32,7168]{1,0:T(8,128)(2,1)S(1)}, bf16[32,7168]{1,0:T(8,128)(2,1)S(1)}, u32[]{:S(2)}, u32[]{:S(2)}) collective-permute-start(bf16[32,7168]{1,0:T(8,128)(2,1)S(1)} %add_convert_fusion.1), channel_id=1, source_target_pairs={{0,2},{1,9},{2,4},{3,11},{4,6},{5,13},{6,0},{7,15},{8,10},{9,17},{... | collective-permute-start | bytes 1376264 | tf_op jit(solution)/shard_map/ppermute | solution.py:50
  128.5 12.1 %collective-permute-start.26 = (bf16[32,7168]{1,0:T(8,128)(2,1)S(1)}, bf16[32,7168]{1,0:T(8,128)(2,1)S(1)}, u32[]{:S(2)}, u32[]{:S(2)}) collective-permute-start(bf16[32,7168]{1,0:T(8,128)(2,1)S(1)} %add_convert_fusion), channel_id=1, source_target_pairs={{0,6},{1,25},{2,0},{3,27},{4,2},{5,29},{6,4},{7,31},{8,14},{9,1},{... | collective-permute-start | bytes 1376264 | tf_op jit(solution)/shard_map/ppermute | solution.py:50
  140.9 6.1 %collective-permute-start.27 = (bf16[8,7168]{1,0:T(8,128)(2,1)S(1)}, bf16[8,7168]{1,0:T(8,128)(2,1)S(1)}, u32[]{:S(2)}, u32[]{:S(2)}) collective-permute-start(bf16[8,7168]{1,0:T(8,128)(2,1)S(1)} %get-tuple-element.77), channel_id=1, source_target_pairs={{0,8},{1,3},{2,10},{3,5},{4,12},{5,7},{6,14},{7,1},{8,16},{9,11},{... | collective-permute-start | bytes 344072 | tf_op jit(solution)/shard_map/ppermute | solution.py:54
  141.2 5.8 %collective-permute-start.28 = (bf16[8,7168]{1,0:T(8,128)(2,1)S(1)}, bf16[8,7168]{1,0:T(8,128)(2,1)S(1)}, u32[]{:S(2)}, u32[]{:S(2)}) collective-permute-start(bf16[8,7168]{1,0:T(8,128)(2,1)S(1)} %get-tuple-element.79), channel_id=1, source_target_pairs={{0,24},{1,7},{2,26},{3,1},{4,28},{5,3},{6,30},{7,5},{8,0},{9,15},{... | collective-permute-start | bytes 344072 | tf_op jit(solution)/shard_map/ppermute | solution.py:54
  144.2 6.3 %collective-permute-start.29 = (bf16[8,7168]{1,0:T(8,128)(2,1)S(1)}, bf16[8,7168]{1,0:T(8,128)(2,1)S(1)}, u32[]{:S(2)}, u32[]{:S(2)}) collective-permute-start(bf16[8,7168]{1,0:T(8,128)(2,1)S(1)} %get-tuple-element.78), channel_id=1, source_target_pairs={{0,16},{1,5},{2,18},{3,7},{4,20},{5,1},{6,22},{7,3},{8,24},{9,13},... | collective-permute-start | bytes 344072 | tf_op jit(solution)/shard_map/ppermute | solution.py:54
  (23 other events, 254.6 us)

commit v5 on v4

--- a/solution.py
+++ b/solution.py
@@ -80,7 +80,7 @@
 
 def reduce_second(terms):
     chunks = add_up(terms[0], terms[1:]).reshape(4, 8, -1)
-    arrived = [along_second(chunks[k].astype(jnp.bfloat16), k) for k in (1, 3, 2)]
+    arrived = [along_second(chunks[k].astype(jnp.bfloat16), k) for k in (2, 1, 3)]
     return add_up(chunks[0], arrived)
 
 
@@ -130,7 +130,7 @@
         compiler_params=params,
         name="share",
     )(residual, *terms)
-    got = {k: along_second(sent, k) for k in (1, 3, 2)}
+    got = {k: along_second(sent, k) for k in (2, 1, 3)}
     return pl.pallas_call(
         settle_kernel,
         out_shape=[

time: 153 us -> 152 us (level)
  waiting for transfers between devices: 69.8 us -> 67.4 us
  Pallas kernels: 27.3 us -> 29.5 us
  transfers between devices with their start and end apart: 31 -> 31, of which waited for: 16 -> 17; matrix products, arithmetic and copies ran while one was open for 0% -> 0% of each run, Pallas kernels for 9% -> 10%
where the time goes in v5:
time: 152 us; the launch traced here: 150 us
  waiting for transfers between devices  67.4 us (44%)
  starting transfers between devices  36.5 us (24%)
  Pallas kernels  29.5 us (19%)
  local copies, waits for them, and re-layouts  14 us (9%)
  other arithmetic  2.32 us (2%)
    ppermute x9, waiting for transfers between devices, along_first(): return lax.ppermute(block, 'tp', chip_pairs((0, k, 0), (k, 0, 0)))  33.8 us
    ppermute x6, waiting for transfers between devices, along_second(): return lax.ppermute(block, 'tp', chip_pairs((k, 0, 0), (0, k, 0)))  16.1 us
    unnamed x32, local copies, waits for them, and re-layouts  14 us
    ppermute x9, starting transfers between devices, along_first(): return lax.ppermute(block, 'tp', chip_pairs((0, k, 0), (k, 0, 0)))  11.7 us
    pallas_call x1, Pallas kernels, attend_resident(): pl.pallas_call(resident_kernel, out_shape=shapes, in_specs=[smem, smem, v...  11.5 us
    ppermute x6, starting transfers between devices, along_second(): return lax.ppermute(block, 'tp', chip_pairs((k, 0, 0), (0, k, 0)))  7.91 us
    all_to_all x1, waiting for transfers between devices, shards(): lax.all_to_all(attended, 'tp', split_axis=0, concat_axis=0, tiled=True)  7.91 us
    ppermute x3, waiting for transfers between devices, shards(): lax.ppermute(boxes[k - 1], 'grp', [(g, (g + k) % 4) for g in range(4)])  7.59 us
  transfers between devices with their start and end apart: 31, of which 17 were waited for; matrix products, arithmetic and copies ran while one was open for 0% of the time, Pallas kernels for 10%

profile of v5, /device:TPU:6, one launch (start us, length us, event | category | flops | bytes accessed | tf_op | source)
XLA Modules:
  0.0 150.1 jit_solution(11107194057478934080)
XLA Ops:
  3.5 2.0 %collective-permute-start = (bf16[8,36992]{1,0:T(8,128)(2,1)S(1)}, bf16[8,36992]{1,0:T(8,128)(2,1)S(1)}, u32[]{:S(2)}, u32[]{:S(2)}) collective-permute-start(bf16[8,36992]{1,0:T(8,128)(2,1)S(1)} %get-tuple-element.43), channel_id=1, source_target_pairs={{0,32},{32,64},{64,96},{96,0},{1,33},{33,65},{65,97},{97,1},{2,34}... | collective-permute-start | bytes 1775624 | tf_op jit(solution)/shard_map/ppermute | solution.py:577
  5.5 3.6 %collective-permute-start.1 = (bf16[8,36992]{1,0:T(8,128)(2,1)S(1)}, bf16[8,36992]{1,0:T(8,128)(2,1)S(1)}, u32[]{:S(2)}, u32[]{:S(2)}) collective-permute-start(bf16[8,36992]{1,0:T(8,128)(2,1)S(1)} %get-tuple-element.44), channel_id=1, source_target_pairs={{0,64},{32,96},{64,0},{96,32},{1,65},{33,97},{65,1},{97,33},{2,66}... | collective-permute-start | bytes 1775624 | tf_op jit(solution)/shard_map/ppermute | solution.py:577
  10.1 2.3 %copy-done.9 = bf16[64,36864]{1,0:T(8,128)(2,1)S(1)} copy-done((bf16[64,36864]{1,0:T(8,128)(2,1)S(1)}, bf16[64,36864]{1,0:T(8,128)(2,1)}, u32[]{:S(2)}) %copy-start.9) | copy-done | bytes 4718616
  15.7 11.5 %attend_resident.1 = (bf16[4,256,576]{2,1,0:T(8,128)(2,1)S(1)}, f32[4,256,128]{2,1,0:T(8,128)S(1)}, f32[4,256,128]{2,1,0:T(8,128)S(1)}, f32[4,256,512]{2,1,0:T(8...) custom-call(s32[4,40]{1,0:T(4,128)S(1)} %copy-done.13, s32[4]{0:T(128)S(1)} %copy-done.14, ...), custom_call_target="tpu_custom_call" | custom-call | flops 8000000000 | bytes 12000000 | tf_op jit(solution)/shard_map/attend_resident/pallas_call | solution.py:354
  27.3 7.6 %collective-permute-done.1.box2 = bf16[8,36992]{1,0:T(8,128)(2,1)S(1)} collective-permute-done((bf16[8,36992]{1,0:T(8,128)(2,1)S(1)}, bf16[8,36992]{1,0:T(8,128)(2,1)S(1)}, u32[]{:S(2)}, u32[]{:S(2)}) %collective-permute-start.1) | collective-permute-done | bytes 591904 | tf_op jit(solution)/shard_map/ppermute | solution.py:577
  34.8 7.0 %attend_received.1._after = bf16[32,32,512]{2,1,0:T(8,128)(2,1)} custom-call(s32[16]{0:T(128)S(1)} %multiply_add_fusion.route, s32[24]{0:T(128)S(1)} %get-tuple-element.40.slot_row, s32[56]{0:T(128)S(1)} %get-tuple-element.41.rec_valid, s32[8]{0:T(128)S(1)} %get-tuple-element.42.rec_first, bf16[8,36992]{1,0:T(8,128)(2,1)S(1)} %collective-permute-done.box1, ...), custom_call_target="tpu_custom_call" | custom-call | tf_op jit(solution)/shard_map/attend_received/pallas_call | solution.py:419
  41.8 6.6 %all-to-all-start = ((bf16[32,32,512]{2,1,0:T(8,128)(2,1)}), bf16[32,32,512]{2,1,0:T(8,128)(2,1)S(1)}, u32[]{:S(2)}, u32[]{:S(2)}) async-start(bf16[32,32,512]{2,1,0:T(8,128)(2,1)} %attend_received.1._after), calls=%async_computation | async-start | bytes 2097152 | tf_op jit(solution)/shard_map/all_to_all | solution.py:586
  48.6 3.1 %copy-done.8 = bf16[512,7168]{1,0:T(8,128)(2,1)S(1)} copy-done((bf16[512,7168]{1,0:T(8,128)(2,1)S(1)}, bf16[512,7168]{1,0:T(8,128)(2,1)}, u32[]{:S(2)}) %copy-start.8) | copy-done | bytes 7340056
  52.7 2.4 %copy-done = bf16[512,5376]{1,0:T(8,128)(2,1)} copy-done((bf16[512,5376]{1,0:T(8,128)(2,1)}, bf16[512,5376]{1,0:T(8,128)(2,1)S(1)}, u32[]{:S(2)}) %copy-start) | copy-done | bytes 5505048
  55.1 7.9 %all-to-all-done = bf16[32,32,512]{2,1,0:T(8,128)(2,1)S(1)} async-done(((bf16[32,32,512]{2,1,0:T(8,128)(2,1)}), bf16[32,32,512]{2,1,0:T(8,128)(2,1)S(1)}, u32[]{:S(2)}, u32[]{:S(2)}) %all-to-all-start) | async-done | bytes 1048608 | tf_op jit(solution)/shard_map/all_to_all | solution.py:586
  70.8 2.8 %collective-permute-start.7 = (bf16[32,7168]{1,0:T(8,128)(2,1)S(1)}, bf16[32,7168]{1,0:T(8,128)(2,1)S(1)}, u32[]{:S(2)}, u32[]{:S(2)}) collective-permute-start(bf16[32,7168]{1,0:T(8,128)(2,1)S(1)} %add_convert_fusion.4), channel_id=1, source_target_pairs={{0,2},{1,9},{2,4},{3,11},{4,6},{5,13},{6,0},{7,15},{8,10},{9,17},{... | collective-permute-start | bytes 1376264 | tf_op jit(solution)/shard_map/ppermute | solution.py:50
  74.4 5.4 %collective-permute-done.9.refs_4_ = bf16[32,7168]{1,0:T(8,128)(2,1)S(1)} collective-permute-done((bf16[32,7168]{1,0:T(8,128)(2,1)S(1)}, bf16[32,7168]{1,0:T(8,128)(2,1)S(1)}, u32[]{:S(2)}, u32[]{:S(2)}) %collective-permute-start.9) | collective-permute-done | bytes 458784 | tf_op jit(solution)/shard_map/ppermute | solution.py:50
  79.8 4.7 %collective-permute-done.7.refs_3_ = bf16[32,7168]{1,0:T(8,128)(2,1)S(1)} collective-permute-done((bf16[32,7168]{1,0:T(8,128)(2,1)S(1)}, bf16[32,7168]{1,0:T(8,128)(2,1)S(1)}, u32[]{:S(2)}, u32[]{:S(2)}) %collective-permute-start.7) | collective-permute-done | bytes 458784 | tf_op jit(solution)/shard_map/ppermute | solution.py:50
  85.7 2.0 %collective-permute-start.11 = (bf16[32,7168]{1,0:T(8,128)(2,1)S(1)}, bf16[32,7168]{1,0:T(8,128)(2,1)S(1)}, u32[]{:S(2)}, u32[]{:S(2)}) collective-permute-start(bf16[32,7168]{1,0:T(8,128)(2,1)S(1)} %get-tuple-element.63), channel_id=1, source_target_pairs={{0,16},{1,5},{2,18},{3,7},{4,20},{5,1},{6,22},{7,3},{8,24},{9,13},... | collective-permute-start | bytes 1376264 | tf_op jit(solution)/shard_map/ppermute | solution.py:54
  88.9 11.0 %collective-permute-done.10.got1 = bf16[32,7168]{1,0:T(8,128)(2,1)S(1)} collective-permute-done((bf16[32,7168]{1,0:T(8,128)(2,1)S(1)}, bf16[32,7168]{1,0:T(8,128)(2,1)S(1)}, u32[]{:S(2)}, u32[]{:S(2)}) %collective-permute-start.10) | collective-permute-done | bytes 458784 | tf_op jit(solution)/shard_map/ppermute | solution.py:54
  102.8 3.1 %collective-permute-start.14 = (bf16[32,7168]{1,0:T(8,128)(2,1)S(1)}, bf16[32,7168]{1,0:T(8,128)(2,1)S(1)}, u32[]{:S(2)}, u32[]{:S(2)}) collective-permute-start(bf16[32,7168]{1,0:T(8,128)(2,1)S(1)} %get-tuple-element.65.refs_0_), channel_id=1, source_target_pairs={{0,4},{1,17},{2,6},{3,19},{4,0},{5,21},{6,2},{7,23},{8,12},{9,25},... | collective-permute-start | bytes 1376264 | tf_op jit(solution)/shard_map/ppermute | solution.py:50
  105.9 5.0 %collective-permute-done.13.refs_1_ = bf16[32,7168]{1,0:T(8,128)(2,1)S(1)} collective-permute-done((bf16[32,7168]{1,0:T(8,128)(2,1)S(1)}, bf16[32,7168]{1,0:T(8,128)(2,1)S(1)}, u32[]{:S(2)}, u32[]{:S(2)}) %collective-permute-start.13) | collective-permute-done | bytes 458784 | tf_op jit(solution)/shard_map/ppermute | solution.py:50
  110.9 6.3 %collective-permute-done.14.refs_2_ = bf16[32,7168]{1,0:T(8,128)(2,1)S(1)} collective-permute-done((bf16[32,7168]{1,0:T(8,128)(2,1)S(1)}, bf16[32,7168]{1,0:T(8,128)(2,1)S(1)}, u32[]{:S(2)}, u32[]{:S(2)}) %collective-permute-start.14) | collective-permute-done | bytes 458784 | tf_op jit(solution)/shard_map/ppermute | solution.py:50
  119.8 3.5 %hidden_units.1 = (bf16[128,288]{1,0:T(8,128)(2,1)S(1)}, bf16[32,7168]{1,0:T(8,128)(2,1)S(1)}, bf16[32,7168]{1,0:T(8,128)(2,1)S(1)}, bf16[32,7168]{1,0:T(8,128)(2,1)S(1)}, bf16[32,7168]{1,0:T(8,128)(2,1)S(1)}) custom-call(bf16[32,7168]{1,0:T(8,128)(2,1)S(1)} %get-tuple-element.65.refs_0_, bf16[32,7168]{1,0:T(8,128)(2,1)S(1)} %collective-permute-done.13.refs_1_, ...), custom_call_target="tpu_custom_call" | custom-call | flops 3000000000 | bytes 18000000 | tf_op jit(solution)/shard_map/hidden_units/pallas_call | solution.py:545
  126.3 2.1 %collective-permute-start.24 = (bf16[32,7168]{1,0:T(8,128)(2,1)S(1)}, bf16[32,7168]{1,0:T(8,128)(2,1)S(1)}, u32[]{:S(2)}, u32[]{:S(2)}) collective-permute-start(bf16[32,7168]{1,0:T(8,128)(2,1)S(1)} %add_convert_fusion.1), channel_id=1, source_target_pairs={{0,2},{1,9},{2,4},{3,11},{4,6},{5,13},{6,0},{7,15},{8,10},{9,17},{... | collective-permute-start | bytes 1376264 | tf_op jit(solution)/shard_map/ppermute | solution.py:50
  128.6 7.2 %collective-permute-done.22 = bf16[32,7168]{1,0:T(8,128)(2,1)S(1)} collective-permute-done((bf16[32,7168]{1,0:T(8,128)(2,1)S(1)}, bf16[32,7168]{1,0:T(8,128)(2,1)S(1)}, u32[]{:S(2)}, u32[]{:S(2)}) %collective-permute-start.22) | collective-permute-done | bytes 458784 | tf_op jit(solution)/shard_map/ppermute | solution.py:50
  135.8 3.7 %collective-permute-done.24 = bf16[32,7168]{1,0:T(8,128)(2,1)S(1)} collective-permute-done((bf16[32,7168]{1,0:T(8,128)(2,1)S(1)}, bf16[32,7168]{1,0:T(8,128)(2,1)S(1)}, u32[]{:S(2)}, u32[]{:S(2)}) %collective-permute-start.24) | collective-permute-done | bytes 458784 | tf_op jit(solution)/shard_map/ppermute | solution.py:50
  141.9 2.7 %collective-permute-start.28 = (bf16[8,7168]{1,0:T(8,128)(2,1)S(1)}, bf16[8,7168]{1,0:T(8,128)(2,1)S(1)}, u32[]{:S(2)}, u32[]{:S(2)}) collective-permute-start(bf16[8,7168]{1,0:T(8,128)(2,1)S(1)} %get-tuple-element.79), channel_id=1, source_target_pairs={{0,8},{1,3},{2,10},{3,5},{4,12},{5,7},{6,14},{7,1},{8,16},{9,11},{... | collective-permute-start | bytes 344072 | tf_op jit(solution)/shard_map/ppermute | solution.py:54
  145.1 2.2 %collective-permute-done.27 = bf16[8,7168]{1,0:T(8,128)(2,1)S(1)} collective-permute-done((bf16[8,7168]{1,0:T(8,128)(2,1)S(1)}, bf16[8,7168]{1,0:T(8,128)(2,1)S(1)}, u32[]{:S(2)}, u32[]{:S(2)}) %collective-permute-start.27) | collective-permute-done | bytes 114720 | tf_op jit(solution)/shard_map/ppermute | solution.py:54
  (93 shorter events, 34.2 us)
Async XLA Ops:
  3.5 23.8 %collective-permute-start = (bf16[8,36992]{1,0:T(8,128)(2,1)S(1)}, bf16[8,36992]{1,0:T(8,128)(2,1)S(1)}, u32[]{:S(2)}, u32[]{:S(2)}) collective-permute-start(bf16[8,36992]{1,0:T(8,128)(2,1)S(1)} %get-tuple-element.43), channel_id=1, source_target_pairs={{0,32},{32,64},{64,96},{96,0},{1,33},{33,65},{65,97},{97,1},{2,34}... | collective-permute-start | bytes 1775624 | tf_op jit(solution)/shard_map/ppermute | solution.py:577
  5.5 29.3 %collective-permute-start.1 = (bf16[8,36992]{1,0:T(8,128)(2,1)S(1)}, bf16[8,36992]{1,0:T(8,128)(2,1)S(1)}, u32[]{:S(2)}, u32[]{:S(2)}) collective-permute-start(bf16[8,36992]{1,0:T(8,128)(2,1)S(1)} %get-tuple-element.44), channel_id=1, source_target_pairs={{0,64},{32,96},{64,0},{96,32},{1,65},{33,97},{65,1},{97,33},{2,66}... | collective-permute-start | bytes 1775624 | tf_op jit(solution)/shard_map/ppermute | solution.py:577
  9.1 25.8 %collective-permute-start.2 = (bf16[8,36992]{1,0:T(8,128)(2,1)S(1)}, bf16[8,36992]{1,0:T(8,128)(2,1)S(1)}, u32[]{:S(2)}, u32[]{:S(2)}) collective-permute-start(bf16[8,36992]{1,0:T(8,128)(2,1)S(1)} %get-tuple-element.45), channel_id=1, source_target_pairs={{0,96},{32,0},{64,32},{96,64},{1,97},{33,1},{65,33},{97,65},{2,98}... | collective-permute-start | bytes 1775624 | tf_op jit(solution)/shard_map/ppermute | solution.py:577
  41.8 21.2 %all-to-all-start = ((bf16[32,32,512]{2,1,0:T(8,128)(2,1)}), bf16[32,32,512]{2,1,0:T(8,128)(2,1)S(1)}, u32[]{:S(2)}, u32[]{:S(2)}) async-start(bf16[32,32,512]{2,1,0:T(8,128)(2,1)} %attend_received.1._after), calls=%async_computation | async-start | bytes 2097152 | tf_op jit(solution)/shard_map/all_to_all | solution.py:586
  68.3 5.2 %collective-permute-start.4 = (bf16[32,7168]{1,0:T(8,128)(2,1)S(1)}, bf16[32,7168]{1,0:T(8,128)(2,1)S(1)}, u32[]{:S(2)}, u32[]{:S(2)}) collective-permute-start(bf16[32,7168]{1,0:T(8,128)(2,1)S(1)} %get-tuple-element.57), channel_id=1, source_target_pairs={{0,1},{1,0},{2,3},{3,2},{4,5},{5,4},{6,7},{7,6},{8,9},{9,8},{10,11... | collective-permute-start | bytes 1376264 | tf_op jit(solution)/shard_map/ppermute | solution.py:46
  68.7 5.7 %collective-permute-start.3 = (bf16[32,7168]{1,0:T(8,128)(2,1)S(1)}, bf16[32,7168]{1,0:T(8,128)(2,1)S(1)}, u32[]{:S(2)}, u32[]{:S(2)}) collective-permute-start(bf16[32,7168]{1,0:T(8,128)(2,1)S(1)} %get-tuple-element.55), channel_id=1, source_target_pairs={{0,1},{1,0},{2,3},{3,2},{4,5},{5,4},{6,7},{7,6},{8,9},{9,8},{10,11... | collective-permute-start | bytes 1376264 | tf_op jit(solution)/shard_map/ppermute | solution.py:46
  70.1 9.8 %collective-permute-start.9 = (bf16[32,7168]{1,0:T(8,128)(2,1)S(1)}, bf16[32,7168]{1,0:T(8,128)(2,1)S(1)}, u32[]{:S(2)}, u32[]{:S(2)}) collective-permute-start(bf16[32,7168]{1,0:T(8,128)(2,1)S(1)} %add_convert_fusion.3), channel_id=1, source_target_pairs={{0,6},{1,25},{2,0},{3,27},{4,2},{5,29},{6,4},{7,31},{8,14},{9,1},{... | collective-permute-start | bytes 1376264 | tf_op jit(solution)/shard_map/ppermute | solution.py:50
  70.8 13.7 %collective-permute-start.7 = (bf16[32,7168]{1,0:T(8,128)(2,1)S(1)}, bf16[32,7168]{1,0:T(8,128)(2,1)S(1)}, u32[]{:S(2)}, u32[]{:S(2)}) collective-permute-start(bf16[32,7168]{1,0:T(8,128)(2,1)S(1)} %add_convert_fusion.4), channel_id=1, source_target_pairs={{0,2},{1,9},{2,4},{3,11},{4,6},{5,13},{6,0},{7,15},{8,10},{9,17},{... | collective-permute-start | bytes 1376264 | tf_op jit(solution)/shard_map/ppermute | solution.py:50
  73.6 11.3 %collective-permute-start.5 = (bf16[32,7168]{1,0:T(8,128)(2,1)S(1)}, bf16[32,7168]{1,0:T(8,128)(2,1)S(1)}, u32[]{:S(2)}, u32[]{:S(2)}) collective-permute-start(bf16[32,7168]{1,0:T(8,128)(2,1)S(1)} %add_convert_fusion.5), channel_id=1, source_target_pairs={{0,4},{1,17},{2,6},{3,19},{4,0},{5,21},{6,2},{7,23},{8,12},{9,25},... | collective-permute-start | bytes 1376264 | tf_op jit(solution)/shard_map/ppermute | solution.py:50
  85.2 14.7 %collective-permute-start.10 = (bf16[32,7168]{1,0:T(8,128)(2,1)S(1)}, bf16[32,7168]{1,0:T(8,128)(2,1)S(1)}, u32[]{:S(2)}, u32[]{:S(2)}) collective-permute-start(bf16[32,7168]{1,0:T(8,128)(2,1)S(1)} %get-tuple-element.63), channel_id=1, source_target_pairs={{0,8},{1,3},{2,10},{3,5},{4,12},{5,7},{6,14},{7,1},{8,16},{9,11},{... | collective-permute-start | bytes 1376264 | tf_op jit(solution)/shard_map/ppermute | solution.py:54
  85.7 14.2 %collective-permute-start.11 = (bf16[32,7168]{1,0:T(8,128)(2,1)S(1)}, bf16[32,7168]{1,0:T(8,128)(2,1)S(1)}, u32[]{:S(2)}, u32[]{:S(2)}) collective-permute-start(bf16[32,7168]{1,0:T(8,128)(2,1)S(1)} %get-tuple-element.63), channel_id=1, source_target_pairs={{0,16},{1,5},{2,18},{3,7},{4,20},{5,1},{6,22},{7,3},{8,24},{9,13},... | collective-permute-start | bytes 1376264 | tf_op jit(solution)/shard_map/ppermute | solution.py:54
  87.7 13.1 %collective-permute-start.12 = (bf16[32,7168]{1,0:T(8,128)(2,1)S(1)}, bf16[32,7168]{1,0:T(8,128)(2,1)S(1)}, u32[]{:S(2)}, u32[]{:S(2)}) collective-permute-start(bf16[32,7168]{1,0:T(8,128)(2,1)S(1)} %get-tuple-element.63), channel_id=1, source_target_pairs={{0,24},{1,7},{2,26},{3,1},{4,28},{5,3},{6,30},{7,5},{8,0},{9,15},{... | collective-permute-start | bytes 1376264 | tf_op jit(solution)/shard_map/ppermute | solution.py:54
  101.2 9.8 %collective-permute-start.13 = (bf16[32,7168]{1,0:T(8,128)(2,1)S(1)}, bf16[32,7168]{1,0:T(8,128)(2,1)S(1)}, u32[]{:S(2)}, u32[]{:S(2)}) collective-permute-start(bf16[32,7168]{1,0:T(8,128)(2,1)S(1)} %get-tuple-element.65.refs_0_), channel_id=1, source_target_pairs={{0,6},{1,25},{2,0},{3,27},{4,2},{5,29},{6,4},{7,31},{8,14},{9,1},{... | collective-permute-start | bytes 1376264 | tf_op jit(solution)/shard_map/ppermute | solution.py:50
  102.8 14.5 %collective-permute-start.14 = (bf16[32,7168]{1,0:T(8,128)(2,1)S(1)}, bf16[32,7168]{1,0:T(8,128)(2,1)S(1)}, u32[]{:S(2)}, u32[]{:S(2)}) collective-permute-start(bf16[32,7168]{1,0:T(8,128)(2,1)S(1)} %get-tuple-element.65.refs_0_), channel_id=1, source_target_pairs={{0,4},{1,17},{2,6},{3,19},{4,0},{5,21},{6,2},{7,23},{8,12},{9,25},... | collective-permute-start | bytes 1376264 | tf_op jit(solution)/shard_map/ppermute | solution.py:50
  105.9 11.4 %collective-permute-start.15 = (bf16[32,7168]{1,0:T(8,128)(2,1)S(1)}, bf16[32,7168]{1,0:T(8,128)(2,1)S(1)}, u32[]{:S(2)}, u32[]{:S(2)}) collective-permute-start(bf16[32,7168]{1,0:T(8,128)(2,1)S(1)} %get-tuple-element.65.refs_0_), channel_id=1, source_target_pairs={{0,2},{1,9},{2,4},{3,11},{4,6},{5,13},{6,0},{7,15},{8,10},{9,17},{... | collective-permute-start | bytes 1376264 | tf_op jit(solution)/shard_map/ppermute | solution.py:50
  105.9 11.9 %collective-permute-start.16 = (bf16[32,7168]{1,0:T(8,128)(2,1)S(1)}, bf16[32,7168]{1,0:T(8,128)(2,1)S(1)}, u32[]{:S(2)}, u32[]{:S(2)}) collective-permute-start(bf16[32,7168]{1,0:T(8,128)(2,1)S(1)} %get-tuple-element.65.refs_0_), channel_id=1, source_target_pairs={{0,1},{1,0},{2,3},{3,2},{4,5},{5,4},{6,7},{7,6},{8,9},{9,8},{10,11... | collective-permute-start | bytes 1376264 | tf_op jit(solution)/shard_map/ppermute | solution.py:46
  110.9 6.9 %collective-permute-start.17 = (bf16[32,7168]{1,0:T(8,128)(2,1)S(1)}, bf16[32,7168]{1,0:T(8,128)(2,1)S(1)}, u32[]{:S(2)}, u32[]{:S(2)}) collective-permute-start(bf16[32,7168]{1,0:T(8,128)(2,1)S(1)} %collective-permute-done.13.refs_1_), channel_id=1, source_target_pairs={{0,1},{1,0},{2,3},{3,2},{4,5},{5,4},{6,7},{7,6},{8,9},{9,8},{10,11... | collective-permute-start | bytes 1376264 | tf_op jit(solution)/shard_map/ppermute | solution.py:46
  124.0 4.6 %collective-permute-start.20 = (bf16[32,7168]{1,0:T(8,128)(2,1)S(1)}, bf16[32,7168]{1,0:T(8,128)(2,1)S(1)}, u32[]{:S(2)}, u32[]{:S(2)}) collective-permute-start(bf16[32,7168]{1,0:T(8,128)(2,1)S(1)} %get-tuple-element.68), channel_id=1, source_target_pairs={{0,1},{1,0},{2,3},{3,2},{4,5},{5,4},{6,7},{7,6},{8,9},{9,8},{10,11... | collective-permute-start | bytes 1376264 | tf_op jit(solution)/shard_map/ppermute | solution.py:46
  125.6 10.2 %collective-permute-start.22 = (bf16[32,7168]{1,0:T(8,128)(2,1)S(1)}, bf16[32,7168]{1,0:T(8,128)(2,1)S(1)}, u32[]{:S(2)}, u32[]{:S(2)}) collective-permute-start(bf16[32,7168]{1,0:T(8,128)(2,1)S(1)} %add_convert_fusion.2), channel_id=1, source_target_pairs={{0,4},{1,17},{2,6},{3,19},{4,0},{5,21},{6,2},{7,23},{8,12},{9,25},... | collective-permute-start | bytes 1376264 | tf_op jit(solution)/shard_map/ppermute | solution.py:50
  126.3 13.2 %collective-permute-start.24 = (bf16[32,7168]{1,0:T(8,128)(2,1)S(1)}, bf16[32,7168]{1,0:T(8,128)(2,1)S(1)}, u32[]{:S(2)}, u32[]{:S(2)}) collective-permute-start(bf16[32,7168]{1,0:T(8,128)(2,1)S(1)} %add_convert_fusion.1), channel_id=1, source_target_pairs={{0,2},{1,9},{2,4},{3,11},{4,6},{5,13},{6,0},{7,15},{8,10},{9,17},{... | collective-permute-start | bytes 1376264 | tf_op jit(solution)/shard_map/ppermute | solution.py:50
  128.5 12.1 %collective-permute-start.26 = (bf16[32,7168]{1,0:T(8,128)(2,1)S(1)}, bf16[32,7168]{1,0:T(8,128)(2,1)S(1)}, u32[]{:S(2)}, u32[]{:S(2)}) collective-permute-start(bf16[32,7168]{1,0:T(8,128)(2,1)S(1)} %add_convert_fusion), channel_id=1, source_target_pairs={{0,6},{1,25},{2,0},{3,27},{4,2},{5,29},{6,4},{7,31},{8,14},{9,1},{... | collective-permute-start | bytes 1376264 | tf_op jit(solution)/shard_map/ppermute | solution.py:50
  140.9 6.4 %collective-permute-start.27 = (bf16[8,7168]{1,0:T(8,128)(2,1)S(1)}, bf16[8,7168]{1,0:T(8,128)(2,1)S(1)}, u32[]{:S(2)}, u32[]{:S(2)}) collective-permute-start(bf16[8,7168]{1,0:T(8,128)(2,1)S(1)} %get-tuple-element.77), channel_id=1, source_target_pairs={{0,16},{1,5},{2,18},{3,7},{4,20},{5,1},{6,22},{7,3},{8,24},{9,13},... | collective-permute-start | bytes 344072 | tf_op jit(solution)/shard_map/ppermute | solution.py:54
  141.9 6.6 %collective-permute-start.28 = (bf16[8,7168]{1,0:T(8,128)(2,1)S(1)}, bf16[8,7168]{1,0:T(8,128)(2,1)S(1)}, u32[]{:S(2)}, u32[]{:S(2)}) collective-permute-start(bf16[8,7168]{1,0:T(8,128)(2,1)S(1)} %get-tuple-element.79), channel_id=1, source_target_pairs={{0,8},{1,3},{2,10},{3,5},{4,12},{5,7},{6,14},{7,1},{8,16},{9,11},{... | collective-permute-start | bytes 344072 | tf_op jit(solution)/shard_map/ppermute | solution.py:54
  144.6 4.8 %collective-permute-start.29 = (bf16[8,7168]{1,0:T(8,128)(2,1)S(1)}, bf16[8,7168]{1,0:T(8,128)(2,1)S(1)}, u32[]{:S(2)}, u32[]{:S(2)}) collective-permute-start(bf16[8,7168]{1,0:T(8,128)(2,1)S(1)} %get-tuple-element.78), channel_id=1, source_target_pairs={{0,24},{1,7},{2,26},{3,1},{4,28},{5,3},{6,30},{7,5},{8,0},{9,15},{... | collective-permute-start | bytes 344072 | tf_op jit(solution)/shard_map/ppermute | solution.py:54
  (23 other events, 254.6 us)
